TPU v7x, 32 devices: a whole 2x2x4 slice. The times are simulated.
32 devices in a mesh: row: 4 (over x, core), mp: 8 (over z, y).
Axes of the slice: x: 2, y: 2, z: 4, core: 2. Of those that a mesh axis runs over, the one named last changes fastest.
Arguments:
- queries: bfloat16 [1280, 16384], P('row', 'mp'), may hold values from -16 to 16
- new_kv: bfloat16 [1280, 2048], P('row', 'mp'), may hold values from -9 to 9
- cache_keys: bfloat16 [256, 16, 512, 128], P('row', 'mp'), may hold values from -26 to 26
- cache_values: bfloat16 [256, 16, 512, 128], P('row', 'mp'), may hold values from -12 to 12
- cache_lens: int32 [256], P('row'), may hold values from 8 to 1019, as said below
- accepted: int32 [256], P('row'), may hold values from 0 to 5
- dest: int32 [256], P('row'), may hold values from 0 to 255, as said below
- out_weight: bfloat16 [16384, 16384], P('mp', 'row'), may hold values from -0.046875 to 0.046875
Outputs:
- mixed: bfloat16 [1280, 16384], P('mp', 'row')
- next_kv: bfloat16 [256, 5, 2048], P('row', None, 'mp')
Inputs may be any that keep to these rules, and one draw needn't show every extreme that they name: `cache_lens`: every beam's cache leaves room for its 5 new tokens. dest is a permutation of 0 to 255; of the beams in each aligned block of 64 beams, exactly 16 go to slots of each aligned block of 64 slots.
All inputs are finite; a program needn't handle non-finite values.
Results may differ from a plain program's by a relative error of at most 0.02.
Values may be sent and summed in bfloat16 or wider, within the bound.
No kernel may reach another device: no remote copies, remote signals or barrier semaphores. Data moves between devices by JAX's collectives and lax.ppermute only.
A program may use at most 128 MiB of HBM per device.

v0:
```python
import jax
import jax.numpy as jnp
from jax import lax
from jax.sharding import PartitionSpec as P

masked_score = -1e30


def partner(block, axis, bit):
    count = lax.axis_size(axis)
    route = []
    for low in range(count):
        high = low | 1 << bit
        if high != low and high < count:
            route += [(low, high), (high, low)]
    return lax.ppermute(block, axis, route)


def head_slice(values, start, count):
    return lax.dynamic_slice_in_dim(values, start, count, 3)


def shards(queries, new_kv, cache_keys, cache_values, cache_lens, accepted, dest, out_weight):
    beams_here = cache_keys.shape[0]
    halves_held = cache_keys.shape[1]
    half_length = cache_keys.shape[2]
    head_size = cache_keys.shape[3]
    drafts = queries.shape[0] // beams_here
    heads_owned = queries.shape[1] // head_size
    kv_columns = new_kv.shape[1]
    mp_place = lax.axis_index("mp")
    lower_side = mp_place % 2 == 0
    if halves_held == 1:
        partner_queries, partner_fresh = partner((queries, new_kv), "mp", 0)
        group_queries = jnp.where(
            lower_side,
            jnp.concatenate([queries, partner_queries], 1),
            jnp.concatenate([partner_queries, queries], 1),
        )
        fresh_pair = jnp.where(
            lower_side,
            jnp.concatenate([new_kv, partner_fresh], 1),
            jnp.concatenate([partner_fresh, new_kv], 1),
        )
    else:
        group_queries = queries
        fresh_pair = new_kv
    group_heads = group_queries.shape[1] // head_size
    sides = (mp_place * halves_held + jnp.arange(halves_held, dtype=jnp.int32)) % 2
    query_block = group_queries.reshape(beams_here, drafts, group_heads, head_size)
    fresh_block = fresh_pair.reshape(beams_here, drafts, 2, head_size)
    fresh_keys = fresh_block[:, :, 0]
    fresh_values = fresh_block[:, :, 1]
    scale = head_size ** (-0.5)
    cache_scores = (
        jnp.einsum("btjd,bsid->bstji", query_block, cache_keys, preferred_element_type=jnp.float32)
        * scale
    )
    fresh_scores = (
        jnp.einsum("btjd,bud->btju", query_block, fresh_keys, preferred_element_type=jnp.float32)
        * scale
    )
    spots = sides[:, None] * half_length + jnp.arange(half_length, dtype=jnp.int32)[None, :]
    cache_valid = (spots[None] < cache_lens[:, None, None])[:, :, None, None, :]
    order = jnp.arange(drafts, dtype=jnp.int32)
    fresh_side = (cache_lens[:, None] + order[None, :]) // half_length
    causal = order[:, None] >= order[None, :]
    fresh_valid = (
        causal[None, None] & (fresh_side[:, None, None, :] == sides[None, :, None, None])
    )[:, :, :, None, :]
    cache_masked = jnp.where(cache_valid, cache_scores, masked_score)
    fresh_masked = jnp.where(fresh_valid, fresh_scores[:, None], masked_score)
    highest = jnp.maximum(jnp.max(cache_masked, -1), jnp.max(fresh_masked, -1))
    cache_weights = jnp.where(cache_valid, jnp.exp(cache_masked - highest[..., None]), 0.0).astype(
        jnp.bfloat16
    )
    fresh_weights = jnp.where(fresh_valid, jnp.exp(fresh_masked - highest[..., None]), 0.0).astype(
        jnp.bfloat16
    )
    partial_value = jnp.einsum(
        "bstji,bsid->bstjd", cache_weights, cache_values, preferred_element_type=jnp.float32
    )
    partial_value = partial_value + jnp.einsum(
        "bstju,bud->bstjd", fresh_weights, fresh_values, preferred_element_type=jnp.float32
    )
    weight_mass = jnp.sum(cache_weights.astype(jnp.float32), -1) + jnp.sum(
        fresh_weights.astype(jnp.float32), -1
    )
    if halves_held == 1:
        own_start = jnp.where(lower_side, 0, heads_owned).astype(jnp.int32)
        other_start = (heads_owned - own_start).astype(jnp.int32)
        got_partial, got_highest, got_mass = partner(
            (
                head_slice(partial_value, other_start, heads_owned),
                head_slice(highest, other_start, heads_owned),
                head_slice(weight_mass, other_start, heads_owned),
            ),
            "mp",
            0,
        )
        own_partial = head_slice(partial_value, own_start, heads_owned)
        own_highest = head_slice(highest, own_start, heads_owned)
        own_mass = head_slice(weight_mass, own_start, heads_owned)
        partial_value = jnp.where(
            lower_side,
            jnp.concatenate([own_partial, got_partial], 1),
            jnp.concatenate([got_partial, own_partial], 1),
        )
        highest = jnp.where(
            lower_side,
            jnp.concatenate([own_highest, got_highest], 1),
            jnp.concatenate([got_highest, own_highest], 1),
        )
        weight_mass = jnp.where(
            lower_side,
            jnp.concatenate([own_mass, got_mass], 1),
            jnp.concatenate([got_mass, own_mass], 1),
        )
    summit = jnp.max(highest, 1)
    factor = jnp.exp(highest - summit[:, None])
    numer = jnp.sum(factor[..., None] * partial_value, 1)
    denom = jnp.sum(factor * weight_mass, 1)
    attention = (
        (numer / denom[..., None])
        .astype(jnp.bfloat16)
        .reshape(beams_here * drafts, heads_owned * head_size)
    )
    projected = jnp.dot(
        lax.all_gather(attention, "row", axis=0, tiled=True),
        out_weight,
        preferred_element_type=jnp.float32,
    )
    rows_owned = projected.shape[0] // lax.axis_size("mp")
    totals = lax.psum(projected.astype(jnp.bfloat16), "mp").astype(jnp.float32)
    owned_rows = lax.dynamic_slice_in_dim(totals, mp_place * rows_owned, rows_owned, 0)
    mixed = owned_rows.astype(jnp.bfloat16)
    fresh_rows = new_kv.reshape(beams_here, drafts, kv_columns)
    kept_mask = order[None, :] < accepted[:, None]
    kept_rows = jnp.where(kept_mask[..., None], fresh_rows, jnp.zeros_like(fresh_rows)).reshape(
        beams_here, drafts * kv_columns
    )
    blocks = lax.axis_size("row")
    share_count = beams_here // blocks
    target = dest // beams_here
    landing = dest % beams_here
    beam_index = jnp.arange(beams_here, dtype=jnp.int32)
    earlier = (target[None, :] == target[:, None]) & (beam_index[None, :] < beam_index[:, None])
    position = jnp.sum(earlier.astype(jnp.int32), 1)
    send_slot = target * share_count + position
    picker = send_slot[None, :] == beam_index[:, None]
    outgoing = jnp.dot(
        picker.astype(jnp.bfloat16), kept_rows, preferred_element_type=jnp.float32
    ).astype(jnp.bfloat16)
    outgoing = outgoing.reshape(blocks, share_count, drafts * kv_columns)
    labels = jnp.sum(jnp.where(picker, landing[None, :], 0), 1).reshape(blocks, share_count)
    arrived, arrived_labels = (
        lax.all_to_all(outgoing, "row", split_axis=0, concat_axis=0, tiled=True),
        lax.all_to_all(labels, "row", split_axis=0, concat_axis=0, tiled=True),
    )
    arrived = arrived.reshape(beams_here, drafts * kv_columns)
    arrived_labels = arrived_labels.reshape(beams_here)
    placer = (arrived_labels[None, :] == beam_index[:, None]).astype(jnp.bfloat16)
    next_kv = jnp.dot(placer, arrived, preferred_element_type=jnp.float32).astype(jnp.bfloat16)
    next_kv = next_kv.reshape(beams_here, drafts, kv_columns)
    return (mixed, next_kv)


def solution(mesh):
    placed = (
        P("row", "mp"),
        P("row", "mp"),
        P("row", "mp", None, None),
        P("row", "mp", None, None),
        P("row"),
        P("row"),
        P("row"),
        P("mp", "row"),
    )
    return jax.shard_map(
        shards,
        mesh=mesh,
        in_specs=placed,
        out_specs=(P("mp", "row"), P("row", None, "mp")),
        check_vma=False,
    )
```

profile of v0, /device:TPU:0, one launch (start us, length us, event | category | flops | bytes accessed | tf_op | source)
XLA Modules:
  0.0 480.2 jit_solution(1508344439228069386)
XLA Ops:
  7.2 0.0 all-gather.2.cloned.1.call-start
  7.2 1.6 copy.30
  8.8 1.0 reshape.180
  9.8 0.9 fusion.31
  10.7 0.7 add_select_fusion
  11.5 0.1 iota_add_fusion.1
  11.5 0.9 broadcast_compare_fusion
  12.4 2.7 convolution_multiply_fusion
  15.1 0.1 broadcast_compare_fusion.1
  15.2 0.1 broadcast_and_fusion
  15.3 2.4 select_reduce_fusion
  17.7 13.4 %bitcast_reduce_fusion = (f32[64,2,5,16]{3,2,1,0:T(8,128)S(1)}, f32[64,2,512,5,16]{2,4,3,1,0:T(8,128)}) fusion(pred[64,2,512]{2,1,0:T(4,128)(4,1)S(1)} %broadcast_compare_fusion, bf16[64,5,16,128,1]{3,2,1,0,4:T(8,128)(2,1)S(1)} %bitcast.68, bf16[64,2,512,128]{3,2,1,0:T(8,128)(2,1)} %param.10), kind=kOutput, calls=%fused_computation.1 | convolution fusion | flops 1357895680 | bytes 39165952 | tf_op jit(solution)/shard_map/btjd,bsid->bstji/dot_general | solution.py:56
  31.1 1.2 fusion.30
  32.3 1.7 convert_reduce_fusion.1
  34.0 12.0 %convert_reduce_fusion = f32[64,2,5,16]{3,2,1,0:T(8,128)S(1)} fusion(f32[64,2,5,16]{3,2,1,0:T(8,128)S(1)} %get-tuple-element.13, f32[64,2,512,5,16]{2,4,3,1,0:T(8,128)} %get-tuple-element.19, pred[64,2,512]{2,1,0:T(4,128)(4,1)S(1)} %broadcast_compare_fusion), kind=kLoop, calls=%fused_computation.5 | loop fusion | flops 36689920 | bytes 21118976 | tf_op jit(solution)/shard_map/reduce_sum | solution.py:86
  46.0 16.7 %fusion.3 = f32[64,2,5,16,128]{4,3,2,1,0:T(8,128)} fusion(bf16[64,2,512,128]{3,2,1,0:T(8,128)(2,1)} %param.11, f32[64,2,512,5,16]{2,4,3,1,0:T(8,128)} %get-tuple-element.19, f32[64,2,5,16]{3,2,1,0:T(8,128)S(1)} %get-tuple-element.13, pred[64,2,512]{2,1,0:T(4,128)(4,1)S(1)} %broadcast_compare_fusion), kind=kOutput, calls=%fused_computation.7 | convolution fusion | flops 1368391680 | bytes 43098112 | tf_op jit(solution)/shard_map/bstji,bsid->bstjd/dot_general | solution.py:80
  62.7 0.2 multiply_reduce_fusion.1
  62.9 7.0 %multiply_reduce_fusion = f32[64,5,16,128]{3,2,1,0:T(8,128)S(1)} fusion(f32[64,2,5,16,128]{4,3,2,1,0:T(8,128)} %fusion.3, f32[64,2,5,16]{3,2,1,0:T(8,128)S(1)} %get-tuple-element.11, f32[64,2,5,16]{3,2,1,0:T(8,128)S(1)} %get-tuple-element.13, f32[64,5,16,5]{2,3,1,0:T(8,128)S(1)} %convolution_multiply_fusion, ...), kind=kOutput, calls=%fused_computation.12 | convolution fusion | flops 16588800 | bytes 8133760 | tf_op jit(solution)/shard_map/bstju,bud->bstjd/dot_general | solution.py:83
  69.9 0.9 divide_convert_fusion
  70.8 1.4 copy.40
  72.2 0.0 all-gather.2.cloned.1.call-update
  72.2 0.0 all-reduce.2.cloned.1.call-start
  72.3 43.2 %all-gather.2.cloned.1.call-done = bf16[1280,2048]{1,0:T(8,128)(2,1)} async-done(((bf16[320,2048]{1,0:T(8,128)(2,1)}), bf16[1280,2048]{1,0:T(8,128)(2,1)}) %all-gather.2.cloned.1.call-update) | async-done | bytes 5242896 | tf_op jit(solution)/shard_map/all_gather | solution.py:129
  115.5 27.9 %convolution_convert_fusion = bf16[1280,4096]{1,0:T(8,128)(2,1)} fusion(bf16[1280,2048]{1,0:T(8,128)(2,1)} %all-gather.2.cloned.1.call-done, bf16[2048,4096]{1,0:T(8,128)(2,1)} %param.15), kind=kOutput, calls=%fused_computation.11 | convolution fusion | flops 21480079360 | bytes 32505856 | tf_op jit(solution)/shard_map/dot_general | solution.py:128
  143.4 0.0 copy-start.2
  143.4 0.0 copy-start
  143.4 0.0 copy-start.1
  143.4 0.0 all-reduce.2.cloned.1.call-update
  143.4 0.6 copy-done.2
  144.0 0.2 convert_reduce_fusion.2
  144.2 0.1 select_reduce_fusion.1
  144.3 0.7 all_to_all.9
  145.0 3.2 all-to-all-start
  148.2 0.0 copy-done
  148.3 0.1 reshape.181
  148.4 0.0 copy-done.1
  148.4 0.1 iota_compare_fusion
  148.5 0.1 broadcast_in_dim.115
  148.7 0.9 convolution_convert_fusion.2
  149.5 2.4 all-to-all-done
  151.9 3.3 all-to-all-start.1
  155.2 0.5 broadcast.215
  155.8 0.7 reduce.3
  156.4 0.1 eq.67
  156.5 3.7 all-to-all-done.1
  160.2 0.2 convolution_convert_fusion.1
  160.4 0.7 copy.41
  161.1 309.8 %all-reduce.2.cloned.1.call-done = bf16[1280,4096]{1,0:T(8,128)(2,1)} async-done(((bf16[1280,4096]{1,0:T(8,128)(2,1)}), bf16[1280,4096]{1,0:T(8,128)(2,1)}) %all-reduce.2.cloned.1.call-update) | async-done | bytes 10485776 | tf_op jit(solution)/shard_map/psum | solution.py:134
  470.9 2.5 convert_convert_fusion
  (5 shorter events, 0.1 us)
Async XLA Ops:
  7.2 108.4 %all-gather.2.cloned.1.call-start = ((), (), s32[]{:S(2)}) async-start(), calls=%async_computation.2 | async-start | bytes 6553600 | tf_op jit(solution)/shard_map/all_gather | solution.py:129
  72.2 398.7 %all-reduce.2.cloned.1.call-start = ((), (), s32[]{:S(2)}) async-start(), calls=%async_computation.3 | async-start | bytes 20971520 | tf_op jit(solution)/shard_map/psum | solution.py:134
  143.4 0.7 copy-start.2
  143.4 4.9 %copy-start = (bf16[320,256]{1,0:T(8,128)(2,1)S(1)}, bf16[320,256]{1,0:T(8,128)(2,1)}, u32[]{:S(2)}) copy-start(bf16[320,256]{1,0:T(8,128)(2,1)} %param.9) | copy-start | bytes 491524
  143.4 5.0 %copy-start.1 = (s32[64]{0:T(128)S(1)}, s32[64]{0:T(128)}, u32[]{:S(2)}) copy-start(s32[64]{0:T(128)} %param.13) | copy-start | bytes 772
  145.0 6.9 %all-to-all-start = ((s32[4,1,16]{2,1,0:T(1,128)}), s32[4,1,16]{2,1,0:T(1,128)S(1)}, u32[]{:S(2)}, u32[]{:S(2)}) async-start(s32[4,1,16]{2,1,0:T(1,128)} %bitcast.12), calls=%async_computation | async-start | bytes 4096 | tf_op jit(solution)/shard_map/all_to_all | solution.py:158
  151.9 8.3 %all-to-all-start.1 = ((bf16[4,16,1280]{2,1,0:T(8,128)(2,1)}), bf16[4,16,1280]{2,1,0:T(8,128)(2,1)S(1)}, u32[]{:S(2)}, u32[]{:S(2)}) async-start(bf16[4,16,1280]{2,1,0:T(8,128)(2,1)} %bitcast.13), calls=%async_computation.1 | async-start | bytes 327680 | tf_op jit(solution)/shard_map/all_to_all | solution.py:157
Sparse Core Ops, SparseCore 0:
  72.4 43.1 all-gather.1
  143.5 327.3 all-reduce.1
where the time goes:
time: 481 us; the launch traced here: 480 us
  waiting for transfers between devices  359 us (75%)
  matrix products  68.7 us (14%)
  other arithmetic  23.8 us (5%)
  between operations  14.2 us (3%)
  local copies, waits for them, and re-layouts  7.75 us (2%)
  starting transfers between devices  6.65 us (1%)
    psum x1, waiting for transfers between devices, shards(): totals = lax.psum(projected.astype(jnp.bfloat16), 'mp').astype(jnp.float32)  310 us
    all_gather x1, waiting for transfers between devices, shards(): lax.all_gather(attention, 'row', axis=0, tiled=True)  43.2 us
    dot_general x1, matrix products, shards(): jnp.dot(lax.all_gather(attention, 'row', axis=0, tiled=True), out_weight,...  27.9 us
    dot_general x1, matrix products, shards(): jnp.einsum('bstji,bsid->bstjd', cache_weights, cache_values, preferred_el...  16.7 us
    dot_general x1, matrix products, shards(): jnp.einsum('btjd,bsid->bstji', query_block, cache_keys, preferred_element...  13.4 us
    reduce_sum x1, other arithmetic, shards(): jnp.sum(cache_weights.astype(jnp.float32), -1)  12 us
  transfers between devices with their start and end apart: 4, of which 4 were waited for; matrix products, arithmetic and copies ran while one was open for 1% of the time, Pallas kernels for 0%

commit v1 on v0

v1 whole, which is shorter than its diff:
```python
import functools

import jax
import jax.numpy as jnp
from jax import lax
from jax.experimental import pallas as pl
from jax.experimental.pallas import tpu as pltpu
from jax.sharding import PartitionSpec as P

masked_score = -1e30
vmem_bytes = 60 * 2**20
early_beams = 8


def partner(block, axis, bit):
    count = lax.axis_size(axis)
    route = []
    for low in range(count):
        high = low | 1 << bit
        if high != low and high < count:
            route += [(low, high), (high, low)]
    return lax.ppermute(block, axis, route)


def head_slice(values, start, count):
    return lax.dynamic_slice_in_dim(values, start, count, 3)


def attention_kernel(scale, first, count, drafts, batch, group, lens, q, k, v, fresh, out,
                     q_raw, q_wide, f_wide, o_wide, k_held, v_held, order, q_sems, k_sems, v_sems):
    halves = out.shape[0]
    size = k.shape[2]
    span = k.shape[1]
    heads = q.shape[1] // size
    stride = k.shape[0] // halves
    block = 2 * size
    most = span // block
    batches = halves * count // batch
    per_half = count // batch
    low = first * drafts // 16 * 16
    shift = first * drafts - low
    taken = q_raw.shape[1]
    rows = heads * 8

    def start_of(n):
        return n // per_half * stride + first + n % per_half * batch

    def copies(n):
        beams = pl.ds(start_of(n), batch)
        slot = n
        return (
            pltpu.make_async_copy(k.at[beams], k_held.at[slot], k_sems.at[slot]),
            pltpu.make_async_copy(v.at[beams], v_held.at[slot], v_sems.at[slot]),
        )

    def query_copy(h):
        start = h * stride * drafts + low
        return pltpu.make_async_copy(q.at[pl.ds(start, taken)], q_raw.at[h], q_sems.at[h])

    for h in range(halves):
        query_copy(h).start()
    ahead = min(2, batches)
    for n in range(ahead):
        for copy in copies(n):
            copy.start()
    for side in range(2):
        f_wide[side, : fresh.shape[0]] = fresh[:, side * size : (side + 1) * size].astype(jnp.float32)
        f_wide[side, fresh.shape[0] :] = jnp.zeros((8, size), jnp.float32)
    for h in range(halves):
        query_copy(h).wait()
        for j in range(heads):
            q_wide[j, h, :taken] = q_raw[h, :, j * size : (j + 1) * size].astype(jnp.float32)
            q_wide[j, h, taken:] = jnp.zeros((8, size), jnp.float32)

    draft = lax.broadcasted_iota(jnp.int32, (2 * rows, 1), 0) % 8
    window = 32
    spot = lax.broadcasted_iota(jnp.int32, (window, 1), 0)
    contract = (((1,), (1,)), ((), ()))
    blank = jnp.zeros((rows, size), jnp.bfloat16)

    def blocks_of(beam):
        return (lens[beam] + (drafts + block - 1)) // block

    def attend_group(n, g, c):
        width = c * block
        for pair in range(group // 2):
            parts = []
            for m in range(2):
                i = order[g * group + 2 * pair + m]
                beam = start_of(n) + i
                length = lens[beam]
                at = pl.multiple_of(jnp.minimum(length // 16 * 16, width - window), 16)
                there = length - at
                inside = (spot >= there) & (spot < there + drafts)
                for side, held in enumerate((k_held, v_held)):
                    new = f_wide[side, pl.ds(beam * drafts, 8), :]
                    new = jnp.concatenate([new, jnp.zeros((window - 8, size), jnp.float32)], 0)
                    new = pltpu.roll(new, there, 0).astype(jnp.bfloat16)
                    old = held[n, i, pl.ds(at, window), :]
                    held[n, i, pl.ds(at, window), :] = jnp.where(inside, new, old)
                row = shift + (beam - start_of(n) + n % per_half * batch) * drafts
                qi = q_wide[:, n // per_half, pl.ds(row, 8), :].reshape(rows, size).astype(jnp.bfloat16)
                parts.append((i, length, row, qi))
            (i, length, row, qi), (i2, length2, row2, qi2) = parts
            left = jnp.concatenate(
                [jnp.concatenate([qi, blank], 1), jnp.concatenate([blank, qi2], 1)], 0
            )
            keys = jnp.concatenate([k_held[n, i, :width], k_held[n, i2, :width]], 1)
            s = lax.dot_general(left, keys, contract, preferred_element_type=jnp.float32)
            which = lax.broadcasted_iota(jnp.int32, (2 * rows, 1), 0) < rows
            limit = jnp.where(which, length, length2) + draft
            s = jnp.where(lax.broadcasted_iota(jnp.int32, (1, width), 1) <= limit, s, masked_score)
            top = jnp.max(s, 1, keepdims=True)
            w = jnp.exp((s - top) * scale).astype(jnp.bfloat16)
            mass = jnp.sum(w.astype(jnp.float32), 1, keepdims=True)
            values = jnp.concatenate([v_held[n, i, :width], v_held[n, i2, :width]], 1)
            total = jnp.dot(w, values, preferred_element_type=jnp.float32)
            share = 1.0 / mass
            for m, start in ((0, row), (1, row2)):
                part = total[m * rows : (m + 1) * rows, m * size : (m + 1) * size]
                part = part * share[m * rows : (m + 1) * rows]
                o_wide[:, n // per_half, pl.ds(start - shift, drafts), :] = part.reshape(heads, 8, size)[:, :drafts]

    def step(n, carry):
        @pl.when(n + ahead < batches)
        def _():
            for copy in copies(jnp.minimum(n + ahead, batches - 1)):
                copy.start()

        held = [blocks_of(start_of(n) + m) for m in range(batch)]
        for m in range(batch):
            rank = jnp.int32(0)
            for other in range(batch):
                if other < m:
                    rank += (held[other] <= held[m]).astype(jnp.int32)
                elif other > m:
                    rank += (held[other] < held[m]).astype(jnp.int32)
            order[rank] = m
        for copy in copies(n):
            copy.wait()
        for g in range(batch // group):
            most_held = blocks_of(start_of(n) + order[g * group + group - 1])
            for c in range(1, most + 1):
                pl.when(most_held == c)(functools.partial(attend_group, n, g, c))
        return carry

    lax.fori_loop(0, batches, step, 0)
    for h in range(halves):
        for j in range(heads):
            out[h, :, j * size : (j + 1) * size] = o_wide[j, h].astype(out.dtype)


def attend(q, k, v, fresh, lens, first, count, halves, drafts, batch=8, group=4):
    beams, size = k.shape[0], k.shape[3]
    span = k.shape[1] * k.shape[2]
    columns = q.shape[1]
    heads = columns // size
    stride = beams // halves
    taken = (first + count) * drafts - first * drafts // 16 * 16
    taken = (taken + 15) // 16 * 16
    batches = halves * count // batch
    full = pl.BlockSpec(memory_space=pltpu.VMEM)
    outside = pl.BlockSpec(memory_space=pl.ANY)
    return pl.pallas_call(
        functools.partial(attention_kernel, size**-0.5, first, count, drafts, batch, group),
        out_shape=jax.ShapeDtypeStruct((halves, count * drafts, columns), jnp.bfloat16),
        in_specs=[pl.BlockSpec(memory_space=pltpu.SMEM), outside, outside, outside, full],
        out_specs=full,
        scratch_shapes=[
            pltpu.VMEM((halves, taken, columns), jnp.bfloat16),
            pltpu.VMEM((heads, halves, taken + 8, size), jnp.float32),
            pltpu.VMEM((2, fresh.shape[0] + 8, size), jnp.float32),
            pltpu.VMEM((heads, halves, count * drafts, size), jnp.float32),
            pltpu.VMEM((batches, batch, span, size), jnp.bfloat16),
            pltpu.VMEM((batches, batch, span, size), jnp.bfloat16),
            pltpu.SMEM((batch,), jnp.int32),
            pltpu.SemaphoreType.DMA((halves,)),
            pltpu.SemaphoreType.DMA((batches,)),
            pltpu.SemaphoreType.DMA((batches,)),
        ],
        compiler_params=pltpu.CompilerParams(vmem_limit_bytes=vmem_bytes),
        cost_estimate=pl.CostEstimate(
            flops=4 * halves * count * drafts * columns * span,
            bytes_accessed=4 * halves * count * size * span,
            transcendentals=halves * count * drafts * heads * span,
        ),
    )(lens, q, k.reshape(beams, span, size), v.reshape(beams, span, size), fresh)


def half_attention(queries, new_kv, cache_keys, cache_values, cache_lens):
    beams_here, halves_held, half_length, head_size = cache_keys.shape
    drafts = queries.shape[0] // beams_here
    heads_owned = queries.shape[1] // head_size
    mp_place = lax.axis_index("mp")
    lower_side = mp_place % 2 == 0
    partner_queries, partner_fresh = partner((queries, new_kv), "mp", 0)
    group_queries = jnp.where(
        lower_side,
        jnp.concatenate([queries, partner_queries], 1),
        jnp.concatenate([partner_queries, queries], 1),
    )
    fresh_pair = jnp.where(
        lower_side,
        jnp.concatenate([new_kv, partner_fresh], 1),
        jnp.concatenate([partner_fresh, new_kv], 1),
    )
    group_heads = group_queries.shape[1] // head_size
    sides = (mp_place * halves_held + jnp.arange(halves_held, dtype=jnp.int32)) % 2
    query_block = group_queries.reshape(beams_here, drafts, group_heads, head_size)
    fresh_block = fresh_pair.reshape(beams_here, drafts, 2, head_size)
    fresh_keys = fresh_block[:, :, 0]
    fresh_values = fresh_block[:, :, 1]
    scale = head_size ** (-0.5)
    cache_scores = (
        jnp.einsum("btjd,bsid->bstji", query_block, cache_keys, preferred_element_type=jnp.float32)
        * scale
    )
    fresh_scores = (
        jnp.einsum("btjd,bud->btju", query_block, fresh_keys, preferred_element_type=jnp.float32)
        * scale
    )
    spots = sides[:, None] * half_length + jnp.arange(half_length, dtype=jnp.int32)[None, :]
    cache_valid = (spots[None] < cache_lens[:, None, None])[:, :, None, None, :]
    order = jnp.arange(drafts, dtype=jnp.int32)
    fresh_side = (cache_lens[:, None] + order[None, :]) // half_length
    causal = order[:, None] >= order[None, :]
    fresh_valid = (
        causal[None, None] & (fresh_side[:, None, None, :] == sides[None, :, None, None])
    )[:, :, :, None, :]
    cache_masked = jnp.where(cache_valid, cache_scores, masked_score)
    fresh_masked = jnp.where(fresh_valid, fresh_scores[:, None], masked_score)
    highest = jnp.maximum(jnp.max(cache_masked, -1), jnp.max(fresh_masked, -1))
    cache_weights = jnp.where(cache_valid, jnp.exp(cache_masked - highest[..., None]), 0.0).astype(
        jnp.bfloat16
    )
    fresh_weights = jnp.where(fresh_valid, jnp.exp(fresh_masked - highest[..., None]), 0.0).astype(
        jnp.bfloat16
    )
    partial_value = jnp.einsum(
        "bstji,bsid->bstjd", cache_weights, cache_values, preferred_element_type=jnp.float32
    )
    partial_value = partial_value + jnp.einsum(
        "bstju,bud->bstjd", fresh_weights, fresh_values, preferred_element_type=jnp.float32
    )
    weight_mass = jnp.sum(cache_weights.astype(jnp.float32), -1) + jnp.sum(
        fresh_weights.astype(jnp.float32), -1
    )
    own_start = jnp.where(lower_side, 0, heads_owned).astype(jnp.int32)
    other_start = (heads_owned - own_start).astype(jnp.int32)
    got_partial, got_highest, got_mass = partner(
        (
            head_slice(partial_value, other_start, heads_owned),
            head_slice(highest, other_start, heads_owned),
            head_slice(weight_mass, other_start, heads_owned),
        ),
        "mp",
        0,
    )
    both_partial = jnp.concatenate(
        [head_slice(partial_value, own_start, heads_owned), got_partial], 1
    )
    both_highest = jnp.concatenate([head_slice(highest, own_start, heads_owned), got_highest], 1)
    both_mass = jnp.concatenate([head_slice(weight_mass, own_start, heads_owned), got_mass], 1)
    summit = jnp.max(both_highest, 1)
    factor = jnp.exp(both_highest - summit[:, None])
    numer = jnp.sum(factor[..., None] * both_partial, 1)
    denom = jnp.sum(factor * both_mass, 1)
    return (
        (numer / denom[..., None])
        .astype(jnp.bfloat16)
        .reshape(beams_here * drafts, heads_owned * head_size)
    )


def gather_rows(block):
    count = lax.axis_size("row")
    if count != 4:
        return [lax.all_gather(block, "row", axis=0, tiled=False)[j] for j in range(count)]
    near = partner(block, "row", 0)
    far = partner(block, "row", 1)
    return [block, near, far, partner(far, "row", 0)]


def project_kernel(gathered, pieces, table, *refs):
    blocks, weight = refs[:gathered], refs[gathered]
    out, held = refs[gathered + 1 : -1], refs[-1]
    rows = blocks[0].shape[1]
    places = held.shape[0] // rows

    @pl.when(pl.program_id(0) == 0)
    def _():
        for at, block in enumerate(blocks):
            for piece in range(pieces):
                place = table[at * pieces + piece]
                for spot in range(places):

                    @pl.when(place == spot)
                    def _():
                        held[pl.ds(spot * rows, rows)] = block[piece]

    total = jnp.dot(held[...], weight[...], preferred_element_type=jnp.float32)
    if len(out) == 1:
        out[0][...] = total.astype(out[0].dtype)
    else:
        for spot in range(places):
            out[spot][...] = total[spot * rows : (spot + 1) * rows].astype(out[spot].dtype)


def project(table, blocks, weight, side, sides, apart):
    pieces, rows, depth = blocks[0].shape
    columns = weight.shape[1] // sides
    tile = min(512, columns)
    tiles = columns // tile
    places = pieces * len(blocks)
    if apart:
        out_shape = [jax.ShapeDtypeStruct((rows, columns), jnp.bfloat16)] * places
        out_specs = [pl.BlockSpec((rows, tile), lambda n, t: (0, n))] * places
    else:
        out_shape = jax.ShapeDtypeStruct((places * rows, columns), jnp.bfloat16)
        out_specs = pl.BlockSpec((places * rows, tile), lambda n, t: (0, n))
    return pl.pallas_call(
        functools.partial(project_kernel, len(blocks), pieces),
        out_shape=out_shape,
        grid_spec=pltpu.PrefetchScalarGridSpec(
            num_scalar_prefetch=1,
            grid=(tiles,),
            in_specs=[pl.BlockSpec((pieces, rows, depth), lambda n, t: (0, 0, 0))] * len(blocks)
            + [pl.BlockSpec((depth, tile), lambda n, t: (0, n + side * tiles))],
            out_specs=out_specs,
            scratch_shapes=[pltpu.VMEM((places * rows, depth), jnp.bfloat16)],
        ),
        compiler_params=pltpu.CompilerParams(vmem_limit_bytes=vmem_bytes),
        cost_estimate=pl.CostEstimate(
            flops=2 * places * rows * depth * columns,
            bytes_accessed=2 * (places * rows * (depth + columns) + depth * columns),
            transcendentals=0,
        ),
    )(table, *blocks, weight)


def plus(*blocks):
    return sum(block.astype(jnp.float32) for block in blocks).astype(jnp.bfloat16)


def ring_order(count):
    return list(range(0, count, 2)) + list(range(count - 1, 0, -2))


class Ring:
    def __init__(self):
        count = lax.axis_size("mp")
        self.order = ring_order(count)
        where = jnp.asarray([self.order.index(device) for device in range(count)], jnp.int32)
        self.ahead = [(self.order[i], self.order[(i + 1) % count]) for i in range(count)]
        self.back = [(b, a) for a, b in self.ahead]
        self.count = count
        rows = lax.axis_size("row")
        pieces = count // rows
        slot_rows = jnp.arange(rows, dtype=jnp.int32)
        if rows == 4:
            slot_rows = slot_rows ^ lax.axis_index("row")
        owner = slot_rows[:, None] * pieces + jnp.arange(pieces, dtype=jnp.int32)
        self.relative = (where[owner.reshape(count)] - where[lax.axis_index("mp")]) % count

    def chain(self, partials, longer):
        n, h = self.count, self.count // 2
        hops = (h, h - 1) if longer else (h - 1, h)
        ahead = back = None
        for k in range(h):
            if k < hops[0]:
                own = partials[hops[0] - k]
                ahead = own if ahead is None else plus(own, ahead)
                ahead = lax.ppermute(ahead, "mp", self.ahead)
            if k < hops[1]:
                own = partials[n - hops[1] + k]
                back = own if back is None else plus(own, back)
                back = lax.ppermute(back, "mp", self.back)
        return plus(partials[0], ahead, back)


def place_rows(new_kv, accepted, dest, beams_here, drafts):
    columns = new_kv.shape[1]
    width = drafts * columns
    fresh_rows = new_kv.reshape(beams_here, drafts, columns)
    order = jnp.arange(drafts, dtype=jnp.int32)
    kept_mask = order[None, :] < accepted[:, None]
    kept_rows = jnp.where(kept_mask[..., None], fresh_rows, jnp.zeros_like(fresh_rows))
    labels = jnp.stack([dest // beams_here, dest % beams_here], 1).astype(jnp.bfloat16)
    labels = jnp.pad(labels, ((0, 0), (0, 126)))
    sent = jnp.concatenate([kept_rows.reshape(beams_here, width), labels], 1)
    all_rows = jnp.concatenate(gather_rows(sent), 0)
    places = all_rows[:, width : width + 2].astype(jnp.int32)
    all_dest = places[:, 0] * beams_here + places[:, 1]
    slot = lax.axis_index("row") * beams_here + jnp.arange(beams_here, dtype=jnp.int32)
    placer = (all_dest[None, :] == slot[:, None]).astype(jnp.bfloat16)
    next_kv = jnp.dot(placer, all_rows[:, :width], preferred_element_type=jnp.float32)
    return next_kv.astype(jnp.bfloat16).reshape(beams_here, drafts, columns)


def after(value, *others):
    return lax.optimization_barrier((value, *others))[0]


def shards(queries, new_kv, cache_keys, cache_values, cache_lens, accepted, dest, out_weight):
    beams_here, halves_held, half_length, head_size = cache_keys.shape
    drafts = queries.shape[0] // beams_here
    depth = queries.shape[1]
    pieces = lax.axis_size("mp") // lax.axis_size("row")
    per_piece = beams_here // pieces
    ring = Ring()
    if halves_held == 1:
        whole = half_attention(queries, new_kv, cache_keys, cache_values, cache_lens)
        whole = whole.reshape(pieces, per_piece * drafts, depth)
    def attention(first, count, before):
        if halves_held == 1:
            return whole[:, first * drafts : (first + count) * drafts]
        q = after(queries, before)
        return attend(q, cache_keys, cache_values, new_kv, cache_lens, first, count, pieces, drafts)

    def halves_of(blocks, before=None):
        parts = []
        for side in range(2):
            if before is not None:
                blocks = [after(blocks[0], before)] + list(blocks[1:])
            part = project(ring.relative, blocks, out_weight, side, 2, True)
            before = part[0]
            parts.append(part)
        return parts

    first = attention(0, early_beams, queries)
    if lax.axis_size("row") == 4:
        far = partner(first, "row", 1)
        near = partner(first, "row", 0)
        second = attention(early_beams, per_piece - early_beams, near)
        second_far = partner(second, "row", 1)
        second_near = partner(second, "row", 0)
        far = after(far, second_near)
        early = halves_of([first, near, far, partner(far, "row", 0)])
        second_far = after(second_far, early[1][0])
        gathered = [second, second_near, second_far, partner(second_far, "row", 0)]
    else:
        early = halves_of(gather_rows(first))
        gathered = gather_rows(attention(early_beams, per_piece - early_beams, first))
    early = [ring.chain(part, side == 0) for side, part in enumerate(early)]
    late = [ring.chain(part, side == 0) for side, part in enumerate(halves_of(gathered))]
    mixed = jnp.concatenate([jnp.concatenate(early, 1), jnp.concatenate(late, 1)], 0)
    moved = after(new_kv, gathered[-1])
    next_kv = place_rows(moved, accepted, dest, beams_here, drafts)
    return (mixed, next_kv)


def solution(mesh):
    placed = (
        P("row", "mp"),
        P("row", "mp"),
        P("row", "mp", None, None),
        P("row", "mp", None, None),
        P("row"),
        P("row"),
        P("row"),
        P("mp", "row"),
    )
    return jax.shard_map(
        shards,
        mesh=mesh,
        in_specs=placed,
        out_specs=(P("mp", "row"), P("row", None, "mp")),
        check_vma=False,
    )
```

time: 481 us -> 190 us (0.40)
  waiting for transfers between devices: 359 us -> 68.1 us
  Pallas kernels: 0 us -> 71.5 us
  matrix products: 68.7 us -> 0.28 us
  starting transfers between devices: 6.65 us -> 39.4 us
  other arithmetic: 23.8 us -> 5.91 us
  between operations: 14.2 us -> 1.14 us
    psum x1 -> x0, waiting for transfers between devices: 310 us -> none  [shards(): totals = lax.psum(projected.astype(jnp.bfloat16), 'mp').astype(jnp.float32)]
    pallas_call x0 -> x6, Pallas kernels: none -> 71.5 us  [the longest x4 43.5 us: project(): pl.pallas_call(functools.partial(project_kernel, len(blocks), pieces), ou...]
    dot_general x7 -> x1, matrix products: 68.7 us -> 0.28 us  [place_rows(): jnp.dot(placer, all_rows[:, :width], preferred_element_type=jnp.float32)]
    ppermute x0 -> x37, waiting for transfers between devices: none -> 68.1 us  [the longest x14 42 us: chain(): ahead = lax.ppermute(ahead, 'mp', self.ahead)]
    all_gather x1 -> x0, waiting for transfers between devices: 43.2 us -> none  [shards(): lax.all_gather(attention, 'row', axis=0, tiled=True)]
    ppermute x0 -> x37, starting transfers between devices: none -> 39.4 us  [the longest x14 16.7 us: chain(): ahead = lax.ppermute(ahead, 'mp', self.ahead)]
    reduce_sum x5 -> x0, other arithmetic: 14.2 us -> none  [the longest x1 12 us: shards(): jnp.sum(cache_weights.astype(jnp.float32), -1)]
    all_to_all x2 -> x0, starting transfers between devices: 6.57 us -> none  [the longest x1 3.35 us: shards(): lax.all_to_all(outgoing, 'row', split_axis=0, concat_axis=0, tiled=True)]
  transfers between devices with their start and end apart: 4 -> 37, of which waited for: 4 -> 17; matrix products, arithmetic and copies ran while one was open for 1% -> 4% of each run, Pallas kernels for 0% -> 33%
where the time goes in v1:
time: 190 us
  Pallas kernels  71.5 us (38%)
  waiting for transfers between devices  68.1 us (36%)
  starting transfers between devices  39.4 us (21%)
  other arithmetic  5.91 us (3%)
  local copies, waits for them, and re-layouts  3.35 us (2%)
    pallas_call x4, Pallas kernels, project(): pl.pallas_call(functools.partial(project_kernel, len(blocks), pieces), ou...  43.5 us
    ppermute x14, waiting for transfers between devices, chain(): ahead = lax.ppermute(ahead, 'mp', self.ahead)  42 us
    pallas_call x2, Pallas kernels, attend(): pl.pallas_call(functools.partial(attention_kernel, size ** (-0.5), first,...  28 us
    ppermute x14, waiting for transfers between devices, chain(): back = lax.ppermute(back, 'mp', self.back)  25.4 us
    ppermute x14, starting transfers between devices, chain(): ahead = lax.ppermute(ahead, 'mp', self.ahead)  16.7 us
    ppermute x14, starting transfers between devices, chain(): back = lax.ppermute(back, 'mp', self.back)  15.1 us
    ppermute x9, starting transfers between devices, partner(): return lax.ppermute(block, axis, route)  7.62 us
  transfers between devices with their start and end apart: 37, of which 17 were waited for; matrix products, arithmetic and copies ran while one was open for 4% of the time, Pallas kernels for 33%

profile of v1, /device:TPU:0, one launch (start us, length us, event | category | flops | bytes accessed | tf_op | source)
XLA Modules:
  0.0 189.8 jit_solution(12178266527473462264)
XLA Ops:
  0.6 8.7 %shard_map.104.refs_0_ = bf16[2,40,2048]{2,1,0:T(8,128)(2,1)} custom-call(s32[64]{0:T(128)} %lens.3, bf16[320,2048]{1,0:T(8,128)(2,1)} %q.1, bf16[64,1024,128]{2,1,0:T(8,128)(2,1)} %bitcast.15, bf16[64,1024,128]{2,1,0:T(8,128)(2,1)} %bitcast.17, bf16[320,256]{1,0:T(8,128)(2,1)} %fresh.3), custom_call_target="tpu_custom_call" | custom-call | flops 671088640 | bytes 8388608 | tf_op jit(solution)/shard_map/pallas_call | solution.py:164
  9.3 0.5 collective-permute-start
  9.8 2.7 %collective-permute-start.1 = (bf16[2,40,2048]{2,1,0:T(8,128)(2,1)}, bf16[2,40,2048]{2,1,0:T(8,128)(2,1)S(1)}, u32[]{:S(2)}, u32[]{:S(2)}) collective-permute-start(bf16[2,40,2048]{2,1,0:T(8,128)(2,1)} %shard_map.104.refs_0_), channel_id=1, source_target_pairs={{0,16},{16,0},{8,24},{24,8},{1,17},{17,1},{9,25},{25,9},{2,18},{18... | collective-permute-start | bytes 983048 | tf_op jit(solution)/shard_map/ppermute | solution.py:22
  12.5 19.4 %shard_map.105.refs_0_ = bf16[2,120,2048]{2,1,0:T(8,128)(2,1)} custom-call(s32[64]{0:T(128)} %lens.3, bf16[320,2048]{1,0:T(8,128)(2,1)} %q.1, bf16[64,1024,128]{2,1,0:T(8,128)(2,1)} %bitcast.16, bf16[64,1024,128]{2,1,0:T(8,128)(2,1)} %bitcast.18, bf16[320,256]{1,0:T(8,128)(2,1)} %fresh.3), custom_call_target="tpu_custom_call" | custom-call | flops 2013265920 | bytes 25165824 | tf_op jit(solution)/shard_map/pallas_call | solution.py:164
  31.9 0.3 collective-permute-start.2
  32.5 2.2 %collective-permute-start.18 = (bf16[2,120,2048]{2,1,0:T(8,128)(2,1)}, bf16[2,120,2048]{2,1,0:T(8,128)(2,1)S(1)}, u32[]{:S(2)}, u32[]{:S(2)}) collective-permute-start(bf16[2,120,2048]{2,1,0:T(8,128)(2,1)} %shard_map.105.refs_0_), channel_id=1, source_target_pairs={{0,16},{16,0},{8,24},{24,8},{1,17},{17,1},{9,25},{25,9},{2,18},{18... | collective-permute-start | bytes 2949128 | tf_op jit(solution)/shard_map/ppermute | solution.py:22
  34.7 0.6 dynamic_slice.3
  35.3 0.6 gather_fusion
  36.4 1.3 and_select_fusion.2.table
  37.7 0.3 collective-permute-done.3.refs_3_
  38.1 0.7 copy-done.4
  38.8 8.0 %shard_map.106 = (bf16[40,2048]{1,0:T(8,128)(2,1)}, bf16[40,2048]{1,0:T(8,128)(2,1)}, bf16[40,2048]{1,0:T(8,128)(2,1)}, bf16[40,2048]{1,0:T(8,128)(2,1)}, bf16[4...) custom-call(s32[8]{0:T(128)} %and_select_fusion.2.table, ...), custom_call_target="tpu_custom_call" | custom-call | flops 2684354560 | bytes 11010048 | tf_op jit(solution)/shard_map/pallas_call | solution.py:321
  46.9 1.6 collective-permute-start.4
  48.5 8.0 %shard_map.107 = (bf16[40,2048]{1,0:T(8,128)(2,1)}, bf16[40,2048]{1,0:T(8,128)(2,1)}, bf16[40,2048]{1,0:T(8,128)(2,1)}, bf16[40,2048]{1,0:T(8,128)(2,1)}, bf16[4...) custom-call(s32[8]{0:T(128)} %and_select_fusion.2.table, ...), custom_call_target="tpu_custom_call" | custom-call | flops 2684354560 | bytes 11010048 | tf_op jit(solution)/shard_map/pallas_call | solution.py:321
  56.5 0.4 collective-permute-done.18.refs_2_
  56.9 1.6 collective-permute-start.8
  58.5 1.6 collective-permute-start.14
  60.1 0.5 collective-permute-start.11
  60.6 0.5 collective-permute-start.5
  61.1 2.8 %collective-permute-done.8 = bf16[40,2048]{1,0:T(8,128)(2,1)S(1)} collective-permute-done((bf16[40,2048]{1,0:T(8,128)(2,1)S(1)}, bf16[40,2048]{1,0:T(8,128)(2,1)S(1)}, u32[]{:S(2)}, u32[]{:S(2)}) %collective-permute-start.8) | collective-permute-done | bytes 163872 | tf_op jit(solution)/shard_map/ppermute | solution.py:377
  64.0 1.6 collective-permute-start.9
  65.6 1.8 collective-permute-done.14
  67.5 1.0 add_convert_fusion.15
  68.4 1.6 collective-permute-start.15
  70.1 0.5 collective-permute-start.12
  70.7 1.7 collective-permute-start.6
  72.4 0.7 collective-permute-start.10
  73.1 1.2 collective-permute-done.15
  74.3 2.5 %collective-permute-start.16 = (bf16[40,2048]{1,0:T(8,128)(2,1)S(1)}, bf16[40,2048]{1,0:T(8,128)(2,1)S(1)}, u32[]{:S(2)}, u32[]{:S(2)}) collective-permute-start(bf16[40,2048]{1,0:T(8,128)(2,1)S(1)} %add_convert_fusion.14), channel_id=1, source_target_pairs={{2,0},{4,2},{6,4},{7,6},{5,7},{3,5},{1,3},{0,1},{10,8},{12,10},{14... | collective-permute-start | bytes 491528 | tf_op jit(solution)/shard_map/ppermute | solution.py:377
  76.9 0.3 collective-permute-done.12
  77.3 0.5 collective-permute-start.13
  77.8 3.0 %collective-permute-done.6 = bf16[40,2048]{1,0:T(8,128)(2,1)S(1)} collective-permute-done((bf16[40,2048]{1,0:T(8,128)(2,1)S(1)}, bf16[40,2048]{1,0:T(8,128)(2,1)S(1)}, u32[]{:S(2)}, u32[]{:S(2)}) %collective-permute-start.6) | collective-permute-done | bytes 163872 | tf_op jit(solution)/shard_map/ppermute | solution.py:373
  80.8 0.5 collective-permute-start.7
  81.3 1.6 collective-permute-start.17
  83.0 3.2 %collective-permute-done.7 = bf16[40,2048]{1,0:T(8,128)(2,1)S(1)} collective-permute-done((bf16[40,2048]{1,0:T(8,128)(2,1)S(1)}, bf16[40,2048]{1,0:T(8,128)(2,1)S(1)}, u32[]{:S(2)}, u32[]{:S(2)}) %collective-permute-start.7) | collective-permute-done | bytes 163872 | tf_op jit(solution)/shard_map/ppermute | solution.py:373
  86.2 0.5 collective-permute-done.17
  87.0 1.8 collective-permute-start.35
  88.8 13.7 %shard_map.108 = (bf16[120,2048]{1,0:T(8,128)(2,1)}, bf16[120,2048]{1,0:T(8,128)(2,1)}, bf16[120,2048]{1,0:T(8,128)(2,1)}, bf16[120,2048]{1,0:T(8,128)(2,1)}, bf...) custom-call(s32[8]{0:T(128)} %and_select_fusion.2.table, ...), custom_call_target="tpu_custom_call" | custom-call | flops 8053063680 | bytes 16252928 | tf_op jit(solution)/shard_map/pallas_call | solution.py:321
  102.5 1.6 collective-permute-start.20
  104.1 0.5 collective-permute-start.24
  104.6 13.7 %shard_map.109 = (bf16[120,2048]{1,0:T(8,128)(2,1)}, bf16[120,2048]{1,0:T(8,128)(2,1)}, bf16[120,2048]{1,0:T(8,128)(2,1)}, bf16[120,2048]{1,0:T(8,128)(2,1)}, bf...) custom-call(s32[8]{0:T(128)} %and_select_fusion.2.table, ...), custom_call_target="tpu_custom_call" | custom-call | flops 8053063680 | bytes 16252928 | tf_op jit(solution)/shard_map/pallas_call | solution.py:321
  118.3 1.5 collective-permute-start.27
  119.9 0.5 collective-permute-start.30
  120.6 0.3 convolution_convert_fusion
  120.9 0.7 copy.21
  121.8 1.6 collective-permute-start.21
  123.5 0.6 collective-permute-start.25
  124.0 8.6 %collective-permute-done.27 = bf16[120,2048]{1,0:T(8,128)(2,1)S(1)} collective-permute-done((bf16[120,2048]{1,0:T(8,128)(2,1)}, bf16[120,2048]{1,0:T(8,128)(2,1)S(1)}, u32[]{:S(2)}, u32[]{:S(2)}) %collective-permute-start.27) | collective-permute-done | bytes 491552 | tf_op jit(solution)/shard_map/ppermute | solution.py:373
  132.7 1.6 collective-permute-start.28
  134.4 0.6 collective-permute-start.31
  135.0 8.1 %collective-permute-done.21 = bf16[120,2048]{1,0:T(8,128)(2,1)S(1)} collective-permute-done((bf16[120,2048]{1,0:T(8,128)(2,1)S(1)}, bf16[120,2048]{1,0:T(8,128)(2,1)S(1)}, u32[]{:S(2)}, u32[]{:S(2)}) %collective-permute-start.21) | collective-permute-done | bytes 491552 | tf_op jit(solution)/shard_map/ppermute | solution.py:373
  143.3 1.6 collective-permute-start.22
  144.9 0.6 collective-permute-start.26
  145.5 9.7 %collective-permute-done.31 = bf16[120,2048]{1,0:T(8,128)(2,1)S(1)} collective-permute-done((bf16[120,2048]{1,0:T(8,128)(2,1)S(1)}, bf16[120,2048]{1,0:T(8,128)(2,1)S(1)}, u32[]{:S(2)}, u32[]{:S(2)}) %collective-permute-start.31) | collective-permute-done | bytes 491552 | tf_op jit(solution)/shard_map/ppermute | solution.py:377
  155.3 0.6 collective-permute-start.32
  155.9 7.9 %collective-permute-done.22 = bf16[120,2048]{1,0:T(8,128)(2,1)S(1)} collective-permute-done((bf16[120,2048]{1,0:T(8,128)(2,1)S(1)}, bf16[120,2048]{1,0:T(8,128)(2,1)S(1)}, u32[]{:S(2)}, u32[]{:S(2)}) %collective-permute-start.22) | collective-permute-done | bytes 491552 | tf_op jit(solution)/shard_map/ppermute | solution.py:373
  163.9 1.6 collective-permute-start.23
  165.7 1.6 collective-permute-start.29
  167.3 8.3 %collective-permute-done.32 = bf16[120,2048]{1,0:T(8,128)(2,1)S(1)} collective-permute-done((bf16[120,2048]{1,0:T(8,128)(2,1)S(1)}, bf16[120,2048]{1,0:T(8,128)(2,1)S(1)}, u32[]{:S(2)}, u32[]{:S(2)}) %collective-permute-start.32) | collective-permute-done | bytes 491552 | tf_op jit(solution)/shard_map/ppermute | solution.py:377
  175.8 0.5 collective-permute-start.33
  176.3 1.8 collective-permute-done.23
  178.3 9.0 %collective-permute-done.29 = bf16[120,2048]{1,0:T(8,128)(2,1)S(1)} collective-permute-done((bf16[120,2048]{1,0:T(8,128)(2,1)S(1)}, bf16[120,2048]{1,0:T(8,128)(2,1)S(1)}, u32[]{:S(2)}, u32[]{:S(2)}) %collective-permute-start.29) | collective-permute-done | bytes 491552 | tf_op jit(solution)/shard_map/ppermute | solution.py:373
  187.4 1.0 collective-permute-done.33
  188.6 1.1 maximum_maximum_fusion
  (132 shorter events, 3.4 us)
Async XLA Ops:
  9.3 3.2 %collective-permute-start = (bf16[2,40,2048]{2,1,0:T(8,128)(2,1)}, bf16[2,40,2048]{2,1,0:T(8,128)(2,1)S(1)}, u32[]{:S(2)}, u32[]{:S(2)}) collective-permute-start(bf16[2,40,2048]{2,1,0:T(8,128)(2,1)} %shard_map.104.refs_0_), channel_id=1, source_target_pairs={{0,8},{8,0},{16,24},{24,16},{1,9},{9,1},{17,25},{25,17},{2,10},{10... | collective-permute-start | bytes 983048 | tf_op jit(solution)/shard_map/ppermute | solution.py:22
  9.8 26.5 %collective-permute-start.1 = (bf16[2,40,2048]{2,1,0:T(8,128)(2,1)}, bf16[2,40,2048]{2,1,0:T(8,128)(2,1)S(1)}, u32[]{:S(2)}, u32[]{:S(2)}) collective-permute-start(bf16[2,40,2048]{2,1,0:T(8,128)(2,1)} %shard_map.104.refs_0_), channel_id=1, source_target_pairs={{0,16},{16,0},{8,24},{24,8},{1,17},{17,1},{9,25},{25,9},{2,18},{18... | collective-permute-start | bytes 983048 | tf_op jit(solution)/shard_map/ppermute | solution.py:22
  12.5 19.9 %copy-start.33 = (s32[64]{0:T(128)S(1)}, s32[64]{0:T(128)}, u32[]{:S(2)}) copy-start(s32[64]{0:T(128)} %param.15) | copy-start | bytes 772
  12.5 19.9 %copy-start.28 = (s32[64]{0:T(128)S(1)}, s32[64]{0:T(128)}, u32[]{:S(2)}) copy-start(s32[64]{0:T(128)} %param.14) | copy-start | bytes 772
  12.5 22.3 %copy-start = (s32[8]{0:T(128)S(1)}, s32[8]{0:T(128)}, u32[]{:S(2)}) copy-start(s32[8]{0:T(128)} %constant.61.clone) | copy-start | bytes 100
  12.5 19.4 %copy-start.2 = (bf16[2,40,2048]{2,1,0:T(8,128)(2,1)}, bf16[2,40,2048]{2,1,0:T(8,128)(2,1)S(1)}, u32[]{:S(2)}) copy-start(bf16[2,40,2048]{2,1,0:T(8,128)(2,1)S(1)} %collective-permute-done.refs_1_) | copy-start | bytes 983044
  31.9 4.4 %collective-permute-start.2 = (bf16[2,120,2048]{2,1,0:T(8,128)(2,1)}, bf16[2,120,2048]{2,1,0:T(8,128)(2,1)S(1)}, u32[]{:S(2)}, u32[]{:S(2)}) collective-permute-start(bf16[2,120,2048]{2,1,0:T(8,128)(2,1)} %shard_map.105.refs_0_), channel_id=1, source_target_pairs={{0,8},{8,0},{16,24},{24,16},{1,9},{9,1},{17,25},{25,17},{2,10},{10... | collective-permute-start | bytes 2949128 | tf_op jit(solution)/shard_map/ppermute | solution.py:22
  32.5 24.4 %collective-permute-start.18 = (bf16[2,120,2048]{2,1,0:T(8,128)(2,1)}, bf16[2,120,2048]{2,1,0:T(8,128)(2,1)S(1)}, u32[]{:S(2)}, u32[]{:S(2)}) collective-permute-start(bf16[2,120,2048]{2,1,0:T(8,128)(2,1)} %shard_map.105.refs_0_), channel_id=1, source_target_pairs={{0,16},{16,0},{8,24},{24,8},{1,17},{17,1},{9,25},{25,9},{2,18},{18... | collective-permute-start | bytes 2949128 | tf_op jit(solution)/shard_map/ppermute | solution.py:22
  36.3 10.5 %copy-start.29 = (bf16[2,120,2048]{2,1,0:T(8,128)(2,1)}, bf16[2,120,2048]{2,1,0:T(8,128)(2,1)S(1)}, u32[]{:S(2)}) copy-start(bf16[2,120,2048]{2,1,0:T(8,128)(2,1)S(1)} %collective-permute-done.2.refs_1_) | copy-start | bytes 2949124
  36.4 1.7 collective-permute-start.3
  46.8 13.7 %copy-start.27 = (bf16[40,2048]{1,0:T(8,128)(2,1)S(1)}, bf16[40,2048]{1,0:T(8,128)(2,1)}, u32[]{:S(2)}) copy-start(bf16[40,2048]{1,0:T(8,128)(2,1)} %get-tuple-element.47) | copy-start | bytes 491524
  46.9 17.1 %copy-start.26 = (bf16[40,2048]{1,0:T(8,128)(2,1)S(1)}, bf16[40,2048]{1,0:T(8,128)(2,1)}, u32[]{:S(2)}) copy-start(bf16[40,2048]{1,0:T(8,128)(2,1)} %get-tuple-element.50) | copy-start | bytes 491524
  46.9 13.7 %collective-permute-start.4 = (bf16[40,2048]{1,0:T(8,128)(2,1)}, bf16[40,2048]{1,0:T(8,128)(2,1)S(1)}, u32[]{:S(2)}, u32[]{:S(2)}) collective-permute-start(bf16[40,2048]{1,0:T(8,128)(2,1)} %get-tuple-element.48), channel_id=1, source_target_pairs={{0,2},{2,4},{4,6},{6,7},{7,5},{5,3},{3,1},{1,0},{8,10},{10,12},{12... | collective-permute-start | bytes 491528 | tf_op jit(solution)/shard_map/ppermute | solution.py:373
  56.5 13.6 %copy-start.25 = (bf16[40,2048]{1,0:T(8,128)(2,1)S(1)}, bf16[40,2048]{1,0:T(8,128)(2,1)}, u32[]{:S(2)}) copy-start(bf16[40,2048]{1,0:T(8,128)(2,1)} %get-tuple-element.55) | copy-start | bytes 491524
  56.5 14.2 %copy-start.24 = (bf16[40,2048]{1,0:T(8,128)(2,1)S(1)}, bf16[40,2048]{1,0:T(8,128)(2,1)}, u32[]{:S(2)}) copy-start(bf16[40,2048]{1,0:T(8,128)(2,1)} %get-tuple-element.46) | copy-start | bytes 491524
  56.5 15.9 %copy-start.22 = (bf16[40,2048]{1,0:T(8,128)(2,1)S(1)}, bf16[40,2048]{1,0:T(8,128)(2,1)}, u32[]{:S(2)}) copy-start(bf16[40,2048]{1,0:T(8,128)(2,1)} %get-tuple-element.49) | copy-start | bytes 491524
  56.9 15.5 %copy-start.30 = (bf16[2,120,2048]{2,1,0:T(8,128)(2,1)}, bf16[2,120,2048]{2,1,0:T(8,128)(2,1)S(1)}, u32[]{:S(2)}) copy-start(bf16[2,120,2048]{2,1,0:T(8,128)(2,1)S(1)} %collective-permute-done.18.refs_2_) | copy-start | bytes 2949124
  56.9 29.9 %collective-permute-start.19 = (bf16[2,120,2048]{2,1,0:T(8,128)(2,1)S(1)}, bf16[2,120,2048]{2,1,0:T(8,128)(2,1)S(1)}, u32[]{:S(2)}, u32[]{:S(2)}) collective-permute-start(bf16[2,120,2048]{2,1,0:T(8,128)(2,1)S(1)} %collective-permute-done.18.refs_2_), channel_id=1, source_target_pairs={{0,8},{8,0},{16,24},{24,16},{1,9},{9,1},{17,25},{25,17},{2,10},{10... | collective-permute-start | bytes 2949128 | tf_op jit(solution)/shard_map/ppermute | solution.py:22
  56.9 7.1 %collective-permute-start.8 = (bf16[40,2048]{1,0:T(8,128)(2,1)S(1)}, bf16[40,2048]{1,0:T(8,128)(2,1)S(1)}, u32[]{:S(2)}, u32[]{:S(2)}) collective-permute-start(bf16[40,2048]{1,0:T(8,128)(2,1)S(1)} %copy-done.32), channel_id=1, source_target_pairs={{2,0},{4,2},{6,4},{7,6},{5,7},{3,5},{1,3},{0,1},{10,8},{12,10},{14... | collective-permute-start | bytes 491528 | tf_op jit(solution)/shard_map/ppermute | solution.py:377
  58.5 8.9 %collective-permute-start.14 = (bf16[40,2048]{1,0:T(8,128)(2,1)}, bf16[40,2048]{1,0:T(8,128)(2,1)S(1)}, u32[]{:S(2)}, u32[]{:S(2)}) collective-permute-start(bf16[40,2048]{1,0:T(8,128)(2,1)} %get-tuple-element.60), channel_id=1, source_target_pairs={{2,0},{4,2},{6,4},{7,6},{5,7},{3,5},{1,3},{0,1},{10,8},{12,10},{14... | collective-permute-start | bytes 491528 | tf_op jit(solution)/shard_map/ppermute | solution.py:377
  60.1 10.0 %collective-permute-start.11 = (bf16[40,2048]{1,0:T(8,128)(2,1)}, bf16[40,2048]{1,0:T(8,128)(2,1)S(1)}, u32[]{:S(2)}, u32[]{:S(2)}) collective-permute-start(bf16[40,2048]{1,0:T(8,128)(2,1)} %get-tuple-element.56), channel_id=1, source_target_pairs={{0,2},{2,4},{4,6},{6,7},{7,5},{5,3},{3,1},{1,0},{8,10},{10,12},{12... | collective-permute-start | bytes 491528 | tf_op jit(solution)/shard_map/ppermute | solution.py:373
  60.6 13.7 %copy-start.23 = (bf16[40,2048]{1,0:T(8,128)(2,1)S(1)}, bf16[40,2048]{1,0:T(8,128)(2,1)}, u32[]{:S(2)}) copy-start(bf16[40,2048]{1,0:T(8,128)(2,1)} %get-tuple-element.58) | copy-start | bytes 491524
  60.6 10.0 %collective-permute-start.5 = (bf16[40,2048]{1,0:T(8,128)(2,1)S(1)}, bf16[40,2048]{1,0:T(8,128)(2,1)S(1)}, u32[]{:S(2)}, u32[]{:S(2)}) collective-permute-start(bf16[40,2048]{1,0:T(8,128)(2,1)S(1)} %add_convert_fusion.23), channel_id=1, source_target_pairs={{0,2},{2,4},{4,6},{6,7},{7,5},{5,3},{3,1},{1,0},{8,10},{10,12},{12... | collective-permute-start | bytes 491528 | tf_op jit(solution)/shard_map/ppermute | solution.py:373
  64.0 13.2 %copy-start.21 = (bf16[40,2048]{1,0:T(8,128)(2,1)S(1)}, bf16[40,2048]{1,0:T(8,128)(2,1)}, u32[]{:S(2)}) copy-start(bf16[40,2048]{1,0:T(8,128)(2,1)} %get-tuple-element.54) | copy-start | bytes 491524
  64.0 8.4 %collective-permute-start.9 = (bf16[40,2048]{1,0:T(8,128)(2,1)S(1)}, bf16[40,2048]{1,0:T(8,128)(2,1)S(1)}, u32[]{:S(2)}, u32[]{:S(2)}) collective-permute-start(bf16[40,2048]{1,0:T(8,128)(2,1)S(1)} %add_convert_fusion.20), channel_id=1, source_target_pairs={{2,0},{4,2},{6,4},{7,6},{5,7},{3,5},{1,3},{0,1},{10,8},{12,10},{14... | collective-permute-start | bytes 491528 | tf_op jit(solution)/shard_map/ppermute | solution.py:377
  68.4 12.3 %copy-start.19 = (bf16[40,2048]{1,0:T(8,128)(2,1)S(1)}, bf16[40,2048]{1,0:T(8,128)(2,1)}, u32[]{:S(2)}) copy-start(bf16[40,2048]{1,0:T(8,128)(2,1)} %get-tuple-element.45) | copy-start | bytes 491524
  68.4 5.9 %collective-permute-start.15 = (bf16[40,2048]{1,0:T(8,128)(2,1)S(1)}, bf16[40,2048]{1,0:T(8,128)(2,1)S(1)}, u32[]{:S(2)}, u32[]{:S(2)}) collective-permute-start(bf16[40,2048]{1,0:T(8,128)(2,1)S(1)} %add_convert_fusion.15), channel_id=1, source_target_pairs={{2,0},{4,2},{6,4},{7,6},{5,7},{3,5},{1,3},{0,1},{10,8},{12,10},{14... | collective-permute-start | bytes 491528 | tf_op jit(solution)/shard_map/ppermute | solution.py:377
  70.1 11.2 %copy-start.20 = (bf16[40,2048]{1,0:T(8,128)(2,1)S(1)}, bf16[40,2048]{1,0:T(8,128)(2,1)}, u32[]{:S(2)}) copy-start(bf16[40,2048]{1,0:T(8,128)(2,1)} %get-tuple-element.57) | copy-start | bytes 491524
  70.1 7.1 %collective-permute-start.12 = (bf16[40,2048]{1,0:T(8,128)(2,1)S(1)}, bf16[40,2048]{1,0:T(8,128)(2,1)S(1)}, u32[]{:S(2)}, u32[]{:S(2)}) collective-permute-start(bf16[40,2048]{1,0:T(8,128)(2,1)S(1)} %add_convert_fusion.17), channel_id=1, source_target_pairs={{0,2},{2,4},{4,6},{6,7},{7,5},{5,3},{3,1},{1,0},{8,10},{10,12},{12... | collective-permute-start | bytes 491528 | tf_op jit(solution)/shard_map/ppermute | solution.py:373
  70.7 15.5 %copy-start.17 = (bf16[40,2048]{1,0:T(8,128)(2,1)S(1)}, bf16[40,2048]{1,0:T(8,128)(2,1)}, u32[]{:S(2)}) copy-start(bf16[40,2048]{1,0:T(8,128)(2,1)} %get-tuple-element.44) | copy-start | bytes 491524
  70.7 10.0 %collective-permute-start.6 = (bf16[40,2048]{1,0:T(8,128)(2,1)S(1)}, bf16[40,2048]{1,0:T(8,128)(2,1)S(1)}, u32[]{:S(2)}, u32[]{:S(2)}) collective-permute-start(bf16[40,2048]{1,0:T(8,128)(2,1)S(1)} %add_convert_fusion.22), channel_id=1, source_target_pairs={{0,2},{2,4},{4,6},{6,7},{7,5},{5,3},{3,1},{1,0},{8,10},{10,12},{12... | collective-permute-start | bytes 491528 | tf_op jit(solution)/shard_map/ppermute | solution.py:373
  72.4 10.5 %collective-permute-start.10 = (bf16[40,2048]{1,0:T(8,128)(2,1)S(1)}, bf16[40,2048]{1,0:T(8,128)(2,1)S(1)}, u32[]{:S(2)}, u32[]{:S(2)}) collective-permute-start(bf16[40,2048]{1,0:T(8,128)(2,1)S(1)} %add_convert_fusion.19), channel_id=1, source_target_pairs={{2,0},{4,2},{6,4},{7,6},{5,7},{3,5},{1,3},{0,1},{10,8},{12,10},{14... | collective-permute-start | bytes 491528 | tf_op jit(solution)/shard_map/ppermute | solution.py:377
  74.3 12.4 %copy-start.18 = (bf16[40,2048]{1,0:T(8,128)(2,1)S(1)}, bf16[40,2048]{1,0:T(8,128)(2,1)}, u32[]{:S(2)}) copy-start(bf16[40,2048]{1,0:T(8,128)(2,1)} %get-tuple-element.53) | copy-start | bytes 491524
  74.3 6.9 %collective-permute-start.16 = (bf16[40,2048]{1,0:T(8,128)(2,1)S(1)}, bf16[40,2048]{1,0:T(8,128)(2,1)S(1)}, u32[]{:S(2)}, u32[]{:S(2)}) collective-permute-start(bf16[40,2048]{1,0:T(8,128)(2,1)S(1)} %add_convert_fusion.14), channel_id=1, source_target_pairs={{2,0},{4,2},{6,4},{7,6},{5,7},{3,5},{1,3},{0,1},{10,8},{12,10},{14... | collective-permute-start | bytes 491528 | tf_op jit(solution)/shard_map/ppermute | solution.py:377
  77.3 9.0 %collective-permute-start.13 = (bf16[40,2048]{1,0:T(8,128)(2,1)S(1)}, bf16[40,2048]{1,0:T(8,128)(2,1)S(1)}, u32[]{:S(2)}, u32[]{:S(2)}) collective-permute-start(bf16[40,2048]{1,0:T(8,128)(2,1)S(1)} %add_convert_fusion.16), channel_id=1, source_target_pairs={{0,2},{2,4},{4,6},{6,7},{7,5},{5,3},{3,1},{1,0},{8,10},{10,12},{12... | collective-permute-start | bytes 491528 | tf_op jit(solution)/shard_map/ppermute | solution.py:373
  80.8 5.4 %collective-permute-start.7 = (bf16[40,2048]{1,0:T(8,128)(2,1)S(1)}, bf16[40,2048]{1,0:T(8,128)(2,1)S(1)}, u32[]{:S(2)}, u32[]{:S(2)}) collective-permute-start(bf16[40,2048]{1,0:T(8,128)(2,1)S(1)} %add_convert_fusion.21), channel_id=1, source_target_pairs={{0,2},{2,4},{4,6},{6,7},{7,5},{5,3},{3,1},{1,0},{8,10},{10,12},{12... | collective-permute-start | bytes 491528 | tf_op jit(solution)/shard_map/ppermute | solution.py:373
  81.3 5.4 %collective-permute-start.17 = (bf16[40,2048]{1,0:T(8,128)(2,1)S(1)}, bf16[40,2048]{1,0:T(8,128)(2,1)S(1)}, u32[]{:S(2)}, u32[]{:S(2)}) collective-permute-start(bf16[40,2048]{1,0:T(8,128)(2,1)S(1)} %add_convert_fusion.13), channel_id=1, source_target_pairs={{2,0},{4,2},{6,4},{7,6},{5,7},{3,5},{1,3},{0,1},{10,8},{12,10},{14... | collective-permute-start | bytes 491528 | tf_op jit(solution)/shard_map/ppermute | solution.py:377
  87.0 17.6 %collective-permute-start.35 = (bf16[64,1408]{1,0:T(8,128)(2,1)S(1)}, bf16[64,1408]{1,0:T(8,128)(2,1)S(1)}, u32[]{:S(2)}, u32[]{:S(2)}) collective-permute-start(bf16[64,1408]{1,0:T(8,128)(2,1)S(1)} %pad_maximum_fusion.8), channel_id=1, source_target_pairs={{0,16},{16,0},{8,24},{24,8},{1,17},{17,1},{9,25},{25,9},{2,18},{18... | collective-permute-start | bytes 540680 | tf_op jit(solution)/shard_map/ppermute | solution.py:22
  88.8 31.1 %collective-permute-start.34 = (bf16[64,1408]{1,0:T(8,128)(2,1)S(1)}, bf16[64,1408]{1,0:T(8,128)(2,1)S(1)}, u32[]{:S(2)}, u32[]{:S(2)}) collective-permute-start(bf16[64,1408]{1,0:T(8,128)(2,1)S(1)} %pad_maximum_fusion.8), channel_id=1, source_target_pairs={{0,8},{8,0},{16,24},{24,16},{1,9},{9,1},{17,25},{25,17},{2,10},{10... | collective-permute-start | bytes 540680 | tf_op jit(solution)/shard_map/ppermute | solution.py:22
  102.5 19.0 %collective-permute-start.20 = (bf16[120,2048]{1,0:T(8,128)(2,1)}, bf16[120,2048]{1,0:T(8,128)(2,1)S(1)}, u32[]{:S(2)}, u32[]{:S(2)}) collective-permute-start(bf16[120,2048]{1,0:T(8,128)(2,1)} %get-tuple-element.66), channel_id=1, source_target_pairs={{0,2},{2,4},{4,6},{6,7},{7,5},{5,3},{3,1},{1,0},{8,10},{10,12},{12... | collective-permute-start | bytes 1474568 | tf_op jit(solution)/shard_map/ppermute | solution.py:373
  104.1 19.2 %collective-permute-start.24 = (bf16[120,2048]{1,0:T(8,128)(2,1)}, bf16[120,2048]{1,0:T(8,128)(2,1)S(1)}, u32[]{:S(2)}, u32[]{:S(2)}) collective-permute-start(bf16[120,2048]{1,0:T(8,128)(2,1)} %get-tuple-element.69), channel_id=1, source_target_pairs={{2,0},{4,2},{6,4},{7,6},{5,7},{3,5},{1,3},{0,1},{10,8},{12,10},{14... | collective-permute-start | bytes 1474568 | tf_op jit(solution)/shard_map/ppermute | solution.py:377
  104.6 15.8 %collective-permute-start.36 = (bf16[64,1408]{1,0:T(8,128)(2,1)S(1)}, bf16[64,1408]{1,0:T(8,128)(2,1)S(1)}, u32[]{:S(2)}, u32[]{:S(2)}) collective-permute-start(bf16[64,1408]{1,0:T(8,128)(2,1)S(1)} %collective-permute-done.35), channel_id=1, source_target_pairs={{0,8},{8,0},{16,24},{24,16},{1,9},{9,1},{17,25},{25,17},{2,10},{10... | collective-permute-start | bytes 540680 | tf_op jit(solution)/shard_map/ppermute | solution.py:22
  118.3 14.3 %collective-permute-start.27 = (bf16[120,2048]{1,0:T(8,128)(2,1)}, bf16[120,2048]{1,0:T(8,128)(2,1)S(1)}, u32[]{:S(2)}, u32[]{:S(2)}) collective-permute-start(bf16[120,2048]{1,0:T(8,128)(2,1)} %get-tuple-element.74), channel_id=1, source_target_pairs={{0,2},{2,4},{4,6},{6,7},{7,5},{5,3},{3,1},{1,0},{8,10},{10,12},{12... | collective-permute-start | bytes 1474568 | tf_op jit(solution)/shard_map/ppermute | solution.py:373
  119.9 14.4 %collective-permute-start.30 = (bf16[120,2048]{1,0:T(8,128)(2,1)}, bf16[120,2048]{1,0:T(8,128)(2,1)S(1)}, u32[]{:S(2)}, u32[]{:S(2)}) collective-permute-start(bf16[120,2048]{1,0:T(8,128)(2,1)} %get-tuple-element.78), channel_id=1, source_target_pairs={{2,0},{4,2},{6,4},{7,6},{5,7},{3,5},{1,3},{0,1},{10,8},{12,10},{14... | collective-permute-start | bytes 1474568 | tf_op jit(solution)/shard_map/ppermute | solution.py:377
  121.6 11.0 %copy-start.14 = (bf16[120,2048]{1,0:T(8,128)(2,1)S(1)}, bf16[120,2048]{1,0:T(8,128)(2,1)}, u32[]{:S(2)}) copy-start(bf16[120,2048]{1,0:T(8,128)(2,1)} %get-tuple-element.73) | copy-start | bytes 1474564
  121.8 21.4 %collective-permute-start.21 = (bf16[120,2048]{1,0:T(8,128)(2,1)S(1)}, bf16[120,2048]{1,0:T(8,128)(2,1)S(1)}, u32[]{:S(2)}, u32[]{:S(2)}) collective-permute-start(bf16[120,2048]{1,0:T(8,128)(2,1)S(1)} %add_convert_fusion.11), channel_id=1, source_target_pairs={{0,2},{2,4},{4,6},{6,7},{7,5},{5,3},{3,1},{1,0},{8,10},{10,12},{12... | collective-permute-start | bytes 1474568 | tf_op jit(solution)/shard_map/ppermute | solution.py:373
  123.3 11.0 %copy-start.12 = (bf16[120,2048]{1,0:T(8,128)(2,1)S(1)}, bf16[120,2048]{1,0:T(8,128)(2,1)}, u32[]{:S(2)}) copy-start(bf16[120,2048]{1,0:T(8,128)(2,1)} %get-tuple-element.77) | copy-start | bytes 1474564
  123.5 21.4 %collective-permute-start.25 = (bf16[120,2048]{1,0:T(8,128)(2,1)S(1)}, bf16[120,2048]{1,0:T(8,128)(2,1)S(1)}, u32[]{:S(2)}, u32[]{:S(2)}) collective-permute-start(bf16[120,2048]{1,0:T(8,128)(2,1)S(1)} %add_convert_fusion.8), channel_id=1, source_target_pairs={{2,0},{4,2},{6,4},{7,6},{5,7},{3,5},{1,3},{0,1},{10,8},{12,10},{14... | collective-permute-start | bytes 1474568 | tf_op jit(solution)/shard_map/ppermute | solution.py:377
  132.6 10.5 %copy-start.9 = (bf16[120,2048]{1,0:T(8,128)(2,1)S(1)}, bf16[120,2048]{1,0:T(8,128)(2,1)}, u32[]{:S(2)}) copy-start(bf16[120,2048]{1,0:T(8,128)(2,1)} %get-tuple-element.64) | copy-start | bytes 1474564
  132.7 32.8 %collective-permute-start.28 = (bf16[120,2048]{1,0:T(8,128)(2,1)S(1)}, bf16[120,2048]{1,0:T(8,128)(2,1)S(1)}, u32[]{:S(2)}, u32[]{:S(2)}) collective-permute-start(bf16[120,2048]{1,0:T(8,128)(2,1)S(1)} %add_convert_fusion.5), channel_id=1, source_target_pairs={{0,2},{2,4},{4,6},{6,7},{7,5},{5,3},{3,1},{1,0},{8,10},{10,12},{12... | collective-permute-start | bytes 1474568 | tf_op jit(solution)/shard_map/ppermute | solution.py:373
  134.3 10.5 %copy-start.8 = (bf16[120,2048]{1,0:T(8,128)(2,1)S(1)}, bf16[120,2048]{1,0:T(8,128)(2,1)}, u32[]{:S(2)}) copy-start(bf16[120,2048]{1,0:T(8,128)(2,1)} %get-tuple-element.67) | copy-start | bytes 1474564
  134.4 20.8 %collective-permute-start.31 = (bf16[120,2048]{1,0:T(8,128)(2,1)S(1)}, bf16[120,2048]{1,0:T(8,128)(2,1)S(1)}, u32[]{:S(2)}, u32[]{:S(2)}) collective-permute-start(bf16[120,2048]{1,0:T(8,128)(2,1)S(1)} %add_convert_fusion.3), channel_id=1, source_target_pairs={{2,0},{4,2},{6,4},{7,6},{5,7},{3,5},{1,3},{0,1},{10,8},{12,10},{14... | collective-permute-start | bytes 1474568 | tf_op jit(solution)/shard_map/ppermute | solution.py:377
  143.1 12.1 %copy-start.10 = (bf16[120,2048]{1,0:T(8,128)(2,1)S(1)}, bf16[120,2048]{1,0:T(8,128)(2,1)}, u32[]{:S(2)}) copy-start(bf16[120,2048]{1,0:T(8,128)(2,1)} %get-tuple-element.76) | copy-start | bytes 1474564
  143.3 20.5 %collective-permute-start.22 = (bf16[120,2048]{1,0:T(8,128)(2,1)S(1)}, bf16[120,2048]{1,0:T(8,128)(2,1)S(1)}, u32[]{:S(2)}, u32[]{:S(2)}) collective-permute-start(bf16[120,2048]{1,0:T(8,128)(2,1)S(1)} %add_convert_fusion.10), channel_id=1, source_target_pairs={{0,2},{2,4},{4,6},{6,7},{7,5},{5,3},{3,1},{1,0},{8,10},{10,12},{12... | collective-permute-start | bytes 1474568 | tf_op jit(solution)/shard_map/ppermute | solution.py:373
  144.8 19.0 %copy-start.5 = (bf16[120,2048]{1,0:T(8,128)(2,1)S(1)}, bf16[120,2048]{1,0:T(8,128)(2,1)}, u32[]{:S(2)}) copy-start(bf16[120,2048]{1,0:T(8,128)(2,1)} %get-tuple-element.63) | copy-start | bytes 1474564
  144.9 31.3 %collective-permute-start.26 = (bf16[120,2048]{1,0:T(8,128)(2,1)S(1)}, bf16[120,2048]{1,0:T(8,128)(2,1)S(1)}, u32[]{:S(2)}, u32[]{:S(2)}) collective-permute-start(bf16[120,2048]{1,0:T(8,128)(2,1)S(1)} %add_convert_fusion.7), channel_id=1, source_target_pairs={{2,0},{4,2},{6,4},{7,6},{5,7},{3,5},{1,3},{0,1},{10,8},{12,10},{14... | collective-permute-start | bytes 1474568 | tf_op jit(solution)/shard_map/ppermute | solution.py:377
  155.2 10.3 %copy-start.7 = (bf16[120,2048]{1,0:T(8,128)(2,1)S(1)}, bf16[120,2048]{1,0:T(8,128)(2,1)}, u32[]{:S(2)}) copy-start(bf16[120,2048]{1,0:T(8,128)(2,1)} %get-tuple-element.72) | copy-start | bytes 1474564
  155.3 20.3 %collective-permute-start.32 = (bf16[120,2048]{1,0:T(8,128)(2,1)S(1)}, bf16[120,2048]{1,0:T(8,128)(2,1)S(1)}, u32[]{:S(2)}, u32[]{:S(2)}) collective-permute-start(bf16[120,2048]{1,0:T(8,128)(2,1)S(1)} %add_convert_fusion.2), channel_id=1, source_target_pairs={{2,0},{4,2},{6,4},{7,6},{5,7},{3,5},{1,3},{0,1},{10,8},{12,10},{14... | collective-permute-start | bytes 1474568 | tf_op jit(solution)/shard_map/ppermute | solution.py:377
  163.8 11.8 %copy-start.6 = (bf16[120,2048]{1,0:T(8,128)(2,1)S(1)}, bf16[120,2048]{1,0:T(8,128)(2,1)}, u32[]{:S(2)}) copy-start(bf16[120,2048]{1,0:T(8,128)(2,1)} %get-tuple-element.75) | copy-start | bytes 1474564
  163.9 14.2 %collective-permute-start.23 = (bf16[120,2048]{1,0:T(8,128)(2,1)S(1)}, bf16[120,2048]{1,0:T(8,128)(2,1)S(1)}, u32[]{:S(2)}, u32[]{:S(2)}) collective-permute-start(bf16[120,2048]{1,0:T(8,128)(2,1)S(1)} %add_convert_fusion.9), channel_id=1, source_target_pairs={{0,2},{2,4},{4,6},{6,7},{7,5},{5,3},{3,1},{1,0},{8,10},{10,12},{12... | collective-permute-start | bytes 1474568 | tf_op jit(solution)/shard_map/ppermute | solution.py:373
  165.5 12.6 %copy-start.15 = (bf16[120,2048]{1,0:T(8,128)(2,1)S(1)}, bf16[120,2048]{1,0:T(8,128)(2,1)}, u32[]{:S(2)}) copy-start(bf16[120,2048]{1,0:T(8,128)(2,1)} %get-tuple-element.62) | copy-start | bytes 1474564
  165.7 21.7 %collective-permute-start.29 = (bf16[120,2048]{1,0:T(8,128)(2,1)S(1)}, bf16[120,2048]{1,0:T(8,128)(2,1)S(1)}, u32[]{:S(2)}, u32[]{:S(2)}) collective-permute-start(bf16[120,2048]{1,0:T(8,128)(2,1)S(1)} %add_convert_fusion.4), channel_id=1, source_target_pairs={{0,2},{2,4},{4,6},{6,7},{7,5},{5,3},{3,1},{1,0},{8,10},{10,12},{12... | collective-permute-start | bytes 1474568 | tf_op jit(solution)/shard_map/ppermute | solution.py:373
  175.7 12.6 %copy-start.16 = (bf16[120,2048]{1,0:T(8,128)(2,1)S(1)}, bf16[120,2048]{1,0:T(8,128)(2,1)}, u32[]{:S(2)}) copy-start(bf16[120,2048]{1,0:T(8,128)(2,1)} %get-tuple-element.71) | copy-start | bytes 1474564
  175.8 12.6 %collective-permute-start.33 = (bf16[120,2048]{1,0:T(8,128)(2,1)S(1)}, bf16[120,2048]{1,0:T(8,128)(2,1)S(1)}, u32[]{:S(2)}, u32[]{:S(2)}) collective-permute-start(bf16[120,2048]{1,0:T(8,128)(2,1)S(1)} %add_convert_fusion.1), channel_id=1, source_target_pairs={{2,0},{4,2},{6,4},{7,6},{5,7},{3,5},{1,3},{0,1},{10,8},{12,10},{14... | collective-permute-start | bytes 1474568 | tf_op jit(solution)/shard_map/ppermute | solution.py:377
  (7 other events, 27.6 us)

commit v2 on v1

v2 whole, which is shorter than its diff:
```python
import functools

import jax
import jax.numpy as jnp
from jax import lax
from jax.experimental import pallas as pl
from jax.experimental.pallas import tpu as pltpu
from jax.sharding import PartitionSpec as P

masked_score = -1e30
vmem_bytes = 60 * 2**20
early_beams = 8
order_of_work = ("one", "product", "kept", "one", "product", "0", "one")


def partner(block, axis, bit):
    count = lax.axis_size(axis)
    route = []
    for low in range(count):
        high = low | 1 << bit
        if high != low and high < count:
            route += [(low, high), (high, low)]
    return lax.ppermute(block, axis, route)


def head_slice(values, start, count):
    return lax.dynamic_slice_in_dim(values, start, count, 3)


def attention_kernel(scale, first, count, drafts, group, ahead, lens, q, k, v, fresh, out,
                     q_raw, q_wide, f_wide, o_wide, k_held, v_held, order, q_sems, k_sems, v_sems):
    halves = out.shape[0]
    size = k.shape[2]
    span = k.shape[1]
    heads = q.shape[1] // size
    stride = k.shape[0] // halves
    block = 2 * size
    most = span // block
    beams = halves * count
    groups = beams // group
    low = first * drafts // 16 * 16
    shift = first * drafts - low
    taken = q_raw.shape[1]
    rows = heads * drafts

    def half_of(i):
        return sum((i >= h * count).astype(jnp.int32) for h in range(1, halves))

    def beam_of(i):
        return i + half_of(i) * (stride - count) + first

    def blocks_of(i):
        return sum((lens[beam_of(i)] + drafts > c * block).astype(jnp.int32) for c in range(1, most)) + 1

    def tally(i, totals):
        held = blocks_of(i)
        return tuple(total + (held <= c + 1).astype(jnp.int32) for c, total in enumerate(totals))

    def rank(i, starts):
        held = blocks_of(i)
        spot = starts[0]
        for c in range(1, most):
            spot = jnp.where(held == c + 1, starts[c], spot)
        order[spot] = i
        return tuple(start + (held == c + 1).astype(jnp.int32) for c, start in enumerate(starts))

    def copies(g, c):
        part = pl.ds(0, c * block)
        for m in range(group):
            at = g * group + m
            beam = beam_of(order[at])
            yield pltpu.make_async_copy(k.at[beam, part], k_held.at[at, part], k_sems.at[at])
            yield pltpu.make_async_copy(v.at[beam, part], v_held.at[at, part], v_sems.at[at])

    def by_length(g, do):
        held = blocks_of(order[g * group + group - 1])
        for c in range(1, most + 1):
            pl.when(held == c)(functools.partial(do, g, c))

    def begin(g, c):
        for copy in copies(g, c):
            copy.start()

    def query_copy(h):
        start = h * stride * drafts + low
        return pltpu.make_async_copy(q.at[pl.ds(start, taken)], q_raw.at[h], q_sems.at[h])

    for h in range(halves):
        query_copy(h).start()
    totals = lax.fori_loop(0, beams, tally, (jnp.int32(0),) * most)
    lax.fori_loop(0, beams, rank, (jnp.int32(0),) + totals[:-1])
    ahead = min(ahead, groups)
    for g in range(ahead):
        by_length(g, begin)
    for side in range(2):
        f_wide[side, : fresh.shape[0]] = fresh[:, side * size : (side + 1) * size].astype(jnp.float32)
        f_wide[side, fresh.shape[0] :] = jnp.zeros((8, size), jnp.float32)
    for h in range(halves):
        query_copy(h).wait()
        q_wide[h] = q_raw[h].astype(jnp.float32).reshape(taken, heads, size)

    draft = lax.broadcasted_iota(jnp.int32, (2 * rows, 1), 0) % rows // heads
    upper = lax.broadcasted_iota(jnp.int32, (2 * rows, 1), 0) < rows
    window = 32
    spot = lax.broadcasted_iota(jnp.int32, (window, 1), 0)
    contract = (((1,), (1,)), ((), ()))
    blank = jnp.zeros((rows, size), jnp.bfloat16)

    def attend_group(g, c):
        width = c * block
        for copy in copies(g, c):
            copy.wait()
        chosen = []
        for m in range(group):
            i = g * group + m
            picked = order[i]
            half, beam = half_of(picked), beam_of(picked)
            length = lens[beam]
            at = jnp.minimum(lax.shift_left(lax.shift_right_logical(length, 4), 4), width - window)
            at = pl.multiple_of(at, 16)
            there = length - at
            inside = (spot >= there) & (spot < there + drafts)
            for side, held in enumerate((k_held, v_held)):
                new = f_wide[side, pl.ds(beam * drafts, 8), :]
                new = jnp.concatenate([new, jnp.zeros((window - 8, size), jnp.float32)], 0)
                new = pltpu.roll(new, there, 0).astype(jnp.bfloat16)
                old = held[i, pl.ds(at, window), :]
                held[i, pl.ds(at, window), :] = jnp.where(inside, new, old)
            chosen.append((i, length, half, (picked - half * count) * drafts))
        spots = lax.broadcasted_iota(jnp.int32, (1, width), 1)
        scores, limits = [], []
        for one, two in zip(chosen[::2], chosen[1::2]):
            qs = [
                q_wide[half, pl.ds(shift + row, drafts)].reshape(rows, size).astype(jnp.bfloat16)
                for _, _, half, row in (one, two)
            ]
            left = jnp.concatenate(
                [jnp.concatenate([qs[0], blank], 1), jnp.concatenate([blank, qs[1]], 1)], 0
            )
            keys = jnp.concatenate([k_held[one[0], :width], k_held[two[0], :width]], 1)
            scores.append(lax.dot_general(left, keys, contract, preferred_element_type=jnp.float32))
            limits.append(jnp.where(upper, one[1], two[1]) + draft)
        weights = []
        for s, limit in zip(scores, limits):
            s = jnp.where(spots <= limit, s, masked_score)
            top = jnp.max(s, 1, keepdims=True)
            w = jnp.exp((s - top) * scale).astype(jnp.bfloat16)
            weights.append((w, 1.0 / jnp.sum(w.astype(jnp.float32), 1, keepdims=True)))
        totals = []
        for (w, share), one, two in zip(weights, chosen[::2], chosen[1::2]):
            values = jnp.concatenate([v_held[one[0], :width], v_held[two[0], :width]], 1)
            totals.append(jnp.dot(w, values, preferred_element_type=jnp.float32) * share)
        for total, one, two in zip(totals, chosen[::2], chosen[1::2]):
            for m, (_, _, half, row) in enumerate((one, two)):
                part = total[m * rows : (m + 1) * rows, m * size : (m + 1) * size]
                o_wide[half, pl.ds(row, drafts)] = part.reshape(drafts, heads, size)

    def step(g, carry):
        @pl.when(g + ahead < groups)
        def _():
            by_length(jnp.minimum(g + ahead, groups - 1), begin)

        by_length(g, attend_group)
        return carry

    lax.fori_loop(0, groups, step, 0)
    for h in range(halves):
        out[h] = o_wide[h].reshape(out.shape[1], out.shape[2]).astype(out.dtype)


def attend(q, k, v, fresh, lens, first, count, halves, drafts, group=8, ahead=6):
    beams, size = k.shape[0], k.shape[3]
    span = k.shape[1] * k.shape[2]
    columns = q.shape[1]
    heads = columns // size
    stride = beams // halves
    taken = (first + count) * drafts - first * drafts // 16 * 16
    taken = (taken + 15) // 16 * 16
    chosen = halves * count
    full = pl.BlockSpec(memory_space=pltpu.VMEM)
    outside = pl.BlockSpec(memory_space=pl.ANY)
    return pl.pallas_call(
        functools.partial(attention_kernel, size**-0.5, first, count, drafts, group, ahead),
        out_shape=jax.ShapeDtypeStruct((halves, count * drafts, columns), jnp.bfloat16),
        in_specs=[pl.BlockSpec(memory_space=pltpu.SMEM), outside, outside, outside, full],
        out_specs=full,
        scratch_shapes=[
            pltpu.VMEM((halves, taken, columns), jnp.bfloat16),
            pltpu.VMEM((halves, taken, heads, size), jnp.float32),
            pltpu.VMEM((2, fresh.shape[0] + 8, size), jnp.float32),
            pltpu.VMEM((halves, count * drafts, heads, size), jnp.float32),
            pltpu.VMEM((chosen, span, size), jnp.bfloat16),
            pltpu.VMEM((chosen, span, size), jnp.bfloat16),
            pltpu.SMEM((chosen,), jnp.int32),
            pltpu.SemaphoreType.DMA((halves,)),
            pltpu.SemaphoreType.DMA((chosen,)),
            pltpu.SemaphoreType.DMA((chosen,)),
        ],
        compiler_params=pltpu.CompilerParams(vmem_limit_bytes=vmem_bytes),
        cost_estimate=pl.CostEstimate(
            flops=4 * halves * count * drafts * columns * span,
            bytes_accessed=4 * halves * count * size * span,
            transcendentals=halves * count * drafts * heads * span,
        ),
    )(lens, q, k.reshape(beams, span, size), v.reshape(beams, span, size), fresh)


def half_attention(queries, new_kv, cache_keys, cache_values, cache_lens):
    beams_here, halves_held, half_length, head_size = cache_keys.shape
    drafts = queries.shape[0] // beams_here
    heads_owned = queries.shape[1] // head_size
    mp_place = lax.axis_index("mp")
    lower_side = mp_place % 2 == 0
    partner_queries, partner_fresh = partner((queries, new_kv), "mp", 0)
    group_queries = jnp.where(
        lower_side,
        jnp.concatenate([queries, partner_queries], 1),
        jnp.concatenate([partner_queries, queries], 1),
    )
    fresh_pair = jnp.where(
        lower_side,
        jnp.concatenate([new_kv, partner_fresh], 1),
        jnp.concatenate([partner_fresh, new_kv], 1),
    )
    group_heads = group_queries.shape[1] // head_size
    sides = (mp_place * halves_held + jnp.arange(halves_held, dtype=jnp.int32)) % 2
    query_block = group_queries.reshape(beams_here, drafts, group_heads, head_size)
    fresh_block = fresh_pair.reshape(beams_here, drafts, 2, head_size)
    fresh_keys = fresh_block[:, :, 0]
    fresh_values = fresh_block[:, :, 1]
    scale = head_size ** (-0.5)
    cache_scores = (
        jnp.einsum("btjd,bsid->bstji", query_block, cache_keys, preferred_element_type=jnp.float32)
        * scale
    )
    fresh_scores = (
        jnp.einsum("btjd,bud->btju", query_block, fresh_keys, preferred_element_type=jnp.float32)
        * scale
    )
    spots = sides[:, None] * half_length + jnp.arange(half_length, dtype=jnp.int32)[None, :]
    cache_valid = (spots[None] < cache_lens[:, None, None])[:, :, None, None, :]
    order = jnp.arange(drafts, dtype=jnp.int32)
    fresh_side = (cache_lens[:, None] + order[None, :]) // half_length
    causal = order[:, None] >= order[None, :]
    fresh_valid = (
        causal[None, None] & (fresh_side[:, None, None, :] == sides[None, :, None, None])
    )[:, :, :, None, :]
    cache_masked = jnp.where(cache_valid, cache_scores, masked_score)
    fresh_masked = jnp.where(fresh_valid, fresh_scores[:, None], masked_score)
    highest = jnp.maximum(jnp.max(cache_masked, -1), jnp.max(fresh_masked, -1))
    cache_weights = jnp.where(cache_valid, jnp.exp(cache_masked - highest[..., None]), 0.0).astype(
        jnp.bfloat16
    )
    fresh_weights = jnp.where(fresh_valid, jnp.exp(fresh_masked - highest[..., None]), 0.0).astype(
        jnp.bfloat16
    )
    partial_value = jnp.einsum(
        "bstji,bsid->bstjd", cache_weights, cache_values, preferred_element_type=jnp.float32
    )
    partial_value = partial_value + jnp.einsum(
        "bstju,bud->bstjd", fresh_weights, fresh_values, preferred_element_type=jnp.float32
    )
    weight_mass = jnp.sum(cache_weights.astype(jnp.float32), -1) + jnp.sum(
        fresh_weights.astype(jnp.float32), -1
    )
    own_start = jnp.where(lower_side, 0, heads_owned).astype(jnp.int32)
    other_start = (heads_owned - own_start).astype(jnp.int32)
    got_partial, got_highest, got_mass = partner(
        (
            head_slice(partial_value, other_start, heads_owned),
            head_slice(highest, other_start, heads_owned),
            head_slice(weight_mass, other_start, heads_owned),
        ),
        "mp",
        0,
    )
    both_partial = jnp.concatenate(
        [head_slice(partial_value, own_start, heads_owned), got_partial], 1
    )
    both_highest = jnp.concatenate([head_slice(highest, own_start, heads_owned), got_highest], 1)
    both_mass = jnp.concatenate([head_slice(weight_mass, own_start, heads_owned), got_mass], 1)
    summit = jnp.max(both_highest, 1)
    factor = jnp.exp(both_highest - summit[:, None])
    numer = jnp.sum(factor[..., None] * both_partial, 1)
    denom = jnp.sum(factor * both_mass, 1)
    return (
        (numer / denom[..., None])
        .astype(jnp.bfloat16)
        .reshape(beams_here * drafts, heads_owned * head_size)
    )


def gather_rows(block):
    count = lax.axis_size("row")
    if count != 4:
        return [lax.all_gather(block, "row", axis=0, tiled=False)[j] for j in range(count)]
    near = partner(block, "row", 0)
    far = partner(block, "row", 1)
    return [block, near, far, partner(far, "row", 0)]


def project_kernel(gathered, pieces, half, table, *refs):
    blocks, weight = refs[:gathered], refs[gathered]
    out, held = refs[gathered + 1 : -1], refs[-1]
    rows = blocks[0].shape[1]
    places = held.shape[0] // rows
    pairs = half - 1
    ahead, back = out[:pairs], out[pairs : 2 * pairs]
    ahead_last, back_last, own_left, own_right = out[2 * pairs :]
    phase = pl.program_id(0) // (pl.num_programs(0) // 2)

    @pl.when(pl.program_id(0) == 0)
    def _():
        for at, block in enumerate(blocks):
            for piece in range(pieces):
                place = table[at * pieces + piece]
                for spot in range(places):

                    @pl.when(place == spot)
                    def _():
                        held[pl.ds(spot * rows, rows)] = block[piece]

    total = jnp.dot(held[...], weight[...], preferred_element_type=jnp.float32)
    total = total.astype(jnp.bfloat16)

    def of(place):
        place = place % places
        return total[place * rows : (place + 1) * rows]

    @pl.when(phase == 0)
    def _():
        for k in range(pairs):
            ahead[k][0] = of(half - k)
            back[k][0] = of(k + 1 - half)
        ahead_last[...] = of(1)
        own_left[...] = of(0)

    @pl.when(phase == 1)
    def _():
        for k in range(pairs):
            ahead[k][0] = of(half - 1 - k)
            back[k][0] = of(k - half)
        back_last[...] = of(-1)
        own_right[...] = of(0)


def project(table, blocks, weight):
    pieces, rows, depth = blocks[0].shape
    places = pieces * len(blocks)
    half = places // 2
    columns = weight.shape[1] // 2
    tile = min(1024, columns)
    tiles = columns // tile
    pair = jax.ShapeDtypeStruct((2, rows, columns), jnp.bfloat16)
    single = jax.ShapeDtypeStruct((rows, columns), jnp.bfloat16)
    ahead = pl.BlockSpec((1, rows, tile), lambda n, t: (n // tiles, 0, n % tiles))
    back = pl.BlockSpec((1, rows, tile), lambda n, t: (1 - n // tiles, 0, n % tiles))
    first = pl.BlockSpec((rows, tile), lambda n, t: (0, jnp.minimum(n, tiles - 1)))
    second = pl.BlockSpec((rows, tile), lambda n, t: (0, jnp.maximum(n - tiles, 0)))
    out = pl.pallas_call(
        functools.partial(project_kernel, len(blocks), pieces, half),
        out_shape=[pair] * (2 * half - 2) + [single] * 4,
        grid_spec=pltpu.PrefetchScalarGridSpec(
            num_scalar_prefetch=1,
            grid=(2 * tiles,),
            in_specs=[pl.BlockSpec((pieces, rows, depth), lambda n, t: (0, 0, 0))] * len(blocks)
            + [pl.BlockSpec((depth, tile), lambda n, t: (0, n))],
            out_specs=[ahead] * (half - 1) + [back] * (half - 1) + [first, second, first, second],
            scratch_shapes=[pltpu.VMEM((places * rows, depth), jnp.bfloat16)],
        ),
        compiler_params=pltpu.CompilerParams(vmem_limit_bytes=vmem_bytes),
        cost_estimate=pl.CostEstimate(
            flops=4 * places * rows * depth * columns,
            bytes_accessed=4 * (places * rows * (depth + columns) + depth * columns),
            transcendentals=0,
        ),
    )(table, *blocks, weight)
    steps = [list(step) for step in zip(out[: half - 1], out[half - 1 : 2 * half - 2])]
    return steps + [list(out[-4:-2])], list(out[-2:])


def project_side_kernel(gathered, pieces, table, *refs):
    blocks, weight = refs[:gathered], refs[gathered]
    out, held = refs[gathered + 1 : -1], refs[-1]
    rows = blocks[0].shape[1]
    places = held.shape[0] // rows

    @pl.when(pl.program_id(0) == 0)
    def _():
        for at, block in enumerate(blocks):
            for piece in range(pieces):
                place = table[at * pieces + piece]
                for spot in range(places):

                    @pl.when(place == spot)
                    def _():
                        held[pl.ds(spot * rows, rows)] = block[piece]

    total = jnp.dot(held[...], weight[...], preferred_element_type=jnp.float32)
    total = total.astype(jnp.bfloat16)
    for spot in range(places):
        out[spot][...] = total[spot * rows : (spot + 1) * rows]


def project_side(table, blocks, weight, side):
    pieces, rows, depth = blocks[0].shape
    columns = weight.shape[1] // 2
    tile = min(512, columns)
    tiles = columns // tile
    places = pieces * len(blocks)
    return pl.pallas_call(
        functools.partial(project_side_kernel, len(blocks), pieces),
        out_shape=[jax.ShapeDtypeStruct((rows, columns), jnp.bfloat16)] * places,
        grid_spec=pltpu.PrefetchScalarGridSpec(
            num_scalar_prefetch=1,
            grid=(tiles,),
            in_specs=[pl.BlockSpec((pieces, rows, depth), lambda n, t: (0, 0, 0))] * len(blocks)
            + [pl.BlockSpec((depth, tile), lambda n, t: (0, n + side * tiles))],
            out_specs=[pl.BlockSpec((rows, tile), lambda n, t: (0, n))] * places,
            scratch_shapes=[pltpu.VMEM((places * rows, depth), jnp.bfloat16)],
        ),
        compiler_params=pltpu.CompilerParams(vmem_limit_bytes=vmem_bytes),
        cost_estimate=pl.CostEstimate(
            flops=2 * places * rows * depth * columns,
            bytes_accessed=2 * (places * rows * (depth + columns) + depth * columns),
            transcendentals=0,
        ),
    )(table, *blocks, weight)


def plus(*blocks):
    return sum(block.astype(jnp.float32) for block in blocks).astype(jnp.bfloat16)


def ring_order(count):
    return list(range(0, count, 2)) + list(range(count - 1, 0, -2))


class Ring:
    def __init__(self):
        count = lax.axis_size("mp")
        order = ring_order(count)
        self.ahead = [(order[i], order[(i + 1) % count]) for i in range(count)]
        self.back = [(b, a) for a, b in self.ahead]
        self.count = count
        rows = lax.axis_size("row")
        slot = jnp.arange(count, dtype=jnp.int32)
        pieces = count // rows
        slot_row = slot // pieces
        if rows == 4:
            slot_row = slot_row ^ lax.axis_index("row")
        owner = slot_row * pieces + slot % pieces
        self.relative = (self.place(owner) - self.place(lax.axis_index("mp"))) % count

    def place(self, device):
        return jnp.where(device % 2 == 0, device // 2, self.count - 1 - device // 2)


class Chain:
    def __init__(self, ring, partials):
        self.ring = ring
        self.partials, self.own = partials
        self.arrived = None
        self.step = 0

    def advance(self, before=()):
        sent = self.partials[self.step]
        if self.arrived is not None:
            arrived = lax.optimization_barrier((*self.arrived, *before))[:2]
            if self.step == len(self.partials) - 1:
                self.own = [plus(self.own[0], arrived[1][1]), plus(self.own[1], arrived[0][1])]
                arrived = [got[0] for got in arrived]
            sent = [plus(own, got) for own, got in zip(sent, arrived)]
        routes = (self.ring.ahead, self.ring.back)
        self.arrived = [lax.ppermute(block, "mp", route) for block, route in zip(sent, routes)]
        self.step += 1
        return sent

    def finish(self, before):
        arrived = lax.optimization_barrier((*self.arrived, *before))[:2]
        return jnp.concatenate([plus(own, got) for own, got in zip(self.own, arrived)], 1)


class SideChain:
    def __init__(self, ring, partials, longer):
        half = ring.count // 2
        self.ring = ring
        self.partials = partials
        self.hops = (half, half - 1) if longer else (half - 1, half)
        self.arrived = []
        self.step = 0

    def advance(self, before=()):
        k, n = self.step, self.ring.count
        places = (self.hops[0] - k, n - self.hops[1] + k)
        arrived = list(self.arrived)
        if arrived:
            arrived = lax.optimization_barrier((*arrived, *before))[:2]
        sent, self.arrived = [], []
        for way, route in enumerate((self.ring.ahead, self.ring.back)):
            if k < self.hops[way]:
                own = self.partials[places[way]]
                own = plus(own, arrived[way]) if arrived else own
                sent.append(own)
                self.arrived.append(lax.ppermute(own, "mp", route))
            else:
                self.arrived.append(arrived[way])
        self.step += 1
        return sent

    def finish(self, before):
        arrived = lax.optimization_barrier((*self.arrived, *before))[:2]
        return plus(self.partials[0], *arrived)


def kept_rows(new_kv, accepted, dest, beams_here, drafts):
    columns = new_kv.shape[1]
    fresh_rows = new_kv.reshape(beams_here, drafts, columns)
    order = jnp.arange(drafts, dtype=jnp.int32)
    kept_mask = order[None, :] < accepted[:, None]
    kept = jnp.where(kept_mask[..., None], fresh_rows, jnp.zeros_like(fresh_rows))
    labels = jnp.stack([dest // beams_here, dest % beams_here], 1).astype(jnp.bfloat16)
    labels = jnp.pad(labels, ((0, 0), (0, 126)))
    return jnp.concatenate([kept.reshape(beams_here, drafts * columns), labels], 1)


def place_rows(gathered, beams_here, drafts, columns):
    width = drafts * columns
    all_rows = jnp.concatenate(gathered, 0)
    places = all_rows[:, width : width + 2].astype(jnp.int32)
    all_dest = places[:, 0] * beams_here + places[:, 1]
    slot = lax.axis_index("row") * beams_here + jnp.arange(beams_here, dtype=jnp.int32)
    placer = (all_dest[None, :] == slot[:, None]).astype(jnp.bfloat16)
    next_kv = jnp.dot(placer, all_rows[:, :width], preferred_element_type=jnp.float32)
    return next_kv.astype(jnp.bfloat16).reshape(beams_here, drafts, columns)


def after(value, *others):
    return lax.optimization_barrier((value, *others))[0]


def shards(queries, new_kv, cache_keys, cache_values, cache_lens, accepted, dest, out_weight):
    beams_here, halves_held, half_length, head_size = cache_keys.shape
    drafts = queries.shape[0] // beams_here
    depth = queries.shape[1]
    pieces = lax.axis_size("mp") // lax.axis_size("row")
    per_piece = beams_here // pieces
    ring = Ring()
    if halves_held == 1:
        whole = half_attention(queries, new_kv, cache_keys, cache_values, cache_lens)
        whole = whole.reshape(pieces, per_piece * drafts, depth)
    def attention(first, count, before):
        if halves_held == 1:
            return whole[:, first * drafts : (first + count) * drafts]
        q = after(queries, before)
        return attend(q, cache_keys, cache_values, new_kv, cache_lens, first, count, pieces, drafts)

    def chain_of(blocks, before=()):
        blocks = [after(blocks[0], *before)] + list(blocks[1:]) if before else blocks
        return Chain(ring, project(ring.relative, blocks, out_weight))

    by_chip = lax.axis_size("row") == 4
    first = attention(0, early_beams, queries)
    if by_chip:
        far = partner(first, "row", 1)
        near = partner(first, "row", 0)
        second = attention(early_beams, per_piece - early_beams, first)
        second_far = partner(second, "row", 1)
        second_near = partner(second, "row", 0)
        far = after(far, second)
        early = [first, near, far, partner(far, "row", 0)]
    else:
        early = gather_rows(first)
    chain_one = chain_of(early)
    sent = chain_one.advance()
    kept = kept_rows(after(new_kv, *sent), accepted, dest, beams_here, drafts)
    if by_chip:
        second_far = after(second_far, *sent)
        late = [second, second_near, second_far, partner(second_far, "row", 0)]
        kept_far = partner(kept, "row", 1)
        kept_near = partner(kept, "row", 0)
    else:
        late = gather_rows(attention(early_beams, per_piece - early_beams, first))
        kept = gather_rows(kept)
    half = ring.count // 2
    sides = []
    for word in order_of_work:
        if word == "one":
            sent = chain_one.advance(sent)
        elif word == "product":
            blocks = [after(late[0], *sent)] + late[1:]
            partials = project_side(ring.relative, blocks, out_weight, len(sides))
            sides.append(SideChain(ring, partials, not sides))
            sides[-1].advance()
            sent = partials[:1]
        elif word == "kept" and by_chip:
            kept_far, kept_near = lax.optimization_barrier((kept_far, kept_near, *sent))[:2]
            sent = (*sent, kept_far, kept_near)
            kept = [kept, kept_near, kept_far, partner(kept_far, "row", 0)]
        elif word in ("0", "1"):
            sent = sides[int(word)].advance(sent)
    for step in range(chain_one.step, half):
        sent = chain_one.advance(sent)
    for step in range(1, half):
        for side in range(2):
            if sides[side].step == step:
                sent = sides[side].advance(sent)
    kept[-1] = after(kept[-1], *sent)
    next_kv = place_rows(kept, beams_here, drafts, new_kv.shape[1])
    done = [chain_one.finish(sent)]
    done.append(sides[0].finish(done[:1]))
    done.append(sides[1].finish(done[1:]))
    mixed = jnp.concatenate([done[0], jnp.concatenate(done[1:], 1)], 0)
    return (mixed, next_kv)


def solution(mesh):
    placed = (
        P("row", "mp"),
        P("row", "mp"),
        P("row", "mp", None, None),
        P("row", "mp", None, None),
        P("row"),
        P("row"),
        P("row"),
        P("mp", "row"),
    )
    return jax.shard_map(
        shards,
        mesh=mesh,
        in_specs=placed,
        out_specs=(P("mp", "row"), P("row", None, "mp")),
        check_vma=False,
    )
```

time: 190 us -> 157 us (0.83)
  Pallas kernels: 71.5 us -> 60 us
  waiting for transfers between devices: 68.1 us -> 59 us
  starting transfers between devices: 39.4 us -> 30.4 us
    ppermute x28 -> x22, waiting for transfers between devices: 67.4 us -> 51.6 us  [the longest x14 49.4 us: advance(): self.arrived.append(lax.ppermute(own, 'mp', route))]
    ppermute x28 -> x22, starting transfers between devices: 31.8 us -> 24.4 us  [the longest x14 15.8 us: advance(): self.arrived.append(lax.ppermute(own, 'mp', route))]
    pallas_call x2, Pallas kernels: 28 us -> 20.7 us  [attend(): pl.pallas_call(functools.partial(attention_kernel, size ** (-0.5), first,...]
    ppermute x9, waiting for transfers between devices: 0.73 us -> 7.45 us  [partner(): return lax.ppermute(block, axis, route)]
    pallas_call x4 -> x3, Pallas kernels: 43.5 us -> 39.4 us  [the longest x2 27.4 us: project_side(): pl.pallas_call(functools.partial(project_side_kernel, len(blocks), pieces...]
  transfers between devices with their start and end apart: 37 -> 31, of which waited for: 17 -> 13; matrix products, arithmetic and copies ran while one was open for 4% -> 3% of each run, Pallas kernels for 33% -> 34%
where the time goes in v2:
time: 157 us
  Pallas kernels  60 us (38%)
  waiting for transfers between devices  59 us (38%)
  starting transfers between devices  30.4 us (19%)
  other arithmetic  4.16 us (3%)
  local copies, waits for them, and re-layouts  1.94 us (1%)
    ppermute x14, waiting for transfers between devices, advance(): self.arrived.append(lax.ppermute(own, 'mp', route))  49.4 us
    pallas_call x2, Pallas kernels, project_side(): pl.pallas_call(functools.partial(project_side_kernel, len(blocks), pieces...  27.4 us
    pallas_call x2, Pallas kernels, attend(): pl.pallas_call(functools.partial(attention_kernel, size ** (-0.5), first,...  20.7 us
    ppermute x14, starting transfers between devices, advance(): self.arrived.append(lax.ppermute(own, 'mp', route))  15.8 us
    pallas_call x1, Pallas kernels, project(): pl.pallas_call(functools.partial(project_kernel, len(blocks), pieces, hal...  11.9 us
    ppermute x8, starting transfers between devices, advance(): lax.ppermute(block, 'mp', route)  8.58 us
    ppermute x9, waiting for transfers between devices, partner(): return lax.ppermute(block, axis, route)  7.45 us
    ppermute x9, starting transfers between devices, partner(): return lax.ppermute(block, axis, route)  6.03 us
  transfers between devices with their start and end apart: 31, of which 13 were waited for; matrix products, arithmetic and copies ran while one was open for 3% of the time, Pallas kernels for 34%

profile of v2, /device:TPU:0, one launch (start us, length us, event | category | flops | bytes accessed | tf_op | source)
XLA Modules:
  0.0 157.0 jit_solution(12132764661891191986)
XLA Ops:
  0.6 7.1 %shard_map.95.refs_0_ = bf16[2,40,2048]{2,1,0:T(8,128)(2,1)} custom-call(s32[64]{0:T(128)} %lens.3, bf16[320,2048]{1,0:T(8,128)(2,1)} %q.1, bf16[64,1024,128]{2,1,0:T(8,128)(2,1)} %bitcast.24, bf16[64,1024,128]{2,1,0:T(8,128)(2,1)} %bitcast.26, bf16[320,256]{1,0:T(8,128)(2,1)} %fresh.3), custom_call_target="tpu_custom_call" | custom-call | flops 671088640 | bytes 8388608 | tf_op jit(solution)/shard_map/pallas_call | solution.py:182
  7.8 3.0 %collective-permute-start.1 = (bf16[2,40,2048]{2,1,0:T(8,128)(2,1)}, bf16[2,40,2048]{2,1,0:T(8,128)(2,1)S(1)}, u32[]{:S(2)}, u32[]{:S(2)}) collective-permute-start(bf16[2,40,2048]{2,1,0:T(8,128)(2,1)} %shard_map.95.refs_0_), channel_id=1, source_target_pairs={{0,16},{16,0},{8,24},{24,8},{1,17},{17,1},{9,25},{25,9},{2,18},{18... | collective-permute-start | bytes 983048 | tf_op jit(solution)/shard_map/ppermute | solution.py:23
  10.8 13.5 %shard_map.96.refs_0_ = bf16[2,120,2048]{2,1,0:T(8,128)(2,1)} custom-call(s32[64]{0:T(128)} %lens.3, bf16[320,2048]{1,0:T(8,128)(2,1)} %q.1, bf16[64,1024,128]{2,1,0:T(8,128)(2,1)} %bitcast.25, bf16[64,1024,128]{2,1,0:T(8,128)(2,1)} %bitcast.27, bf16[320,256]{1,0:T(8,128)(2,1)} %fresh.3), custom_call_target="tpu_custom_call" | custom-call | flops 2013265920 | bytes 25165824 | tf_op jit(solution)/shard_map/pallas_call | solution.py:182
  24.3 0.2 collective-permute-start.8
  24.6 0.6 and_select_fusion.2.table
  25.2 0.5 collective-permute-start.2
  25.8 0.1 copy.15
  25.9 0.1 broadcast_in_dim.18
  26.1 1.4 collective-permute-done.2.refs_3_
  27.5 0.7 copy-done.25
  28.3 11.9 %shard_map.97 = (bf16[2,40,2048]{2,1,0:T(8,128)(2,1)}, bf16[2,40,2048]{2,1,0:T(8,128)(2,1)}, bf16[2,40,2048]{2,1,0:T(8,128)(2,1)}, bf16[2,40,2048]{2,1,0:T(8,128...) custom-call(s32[8]{0:T(128)} %and_select_fusion.2.table, ...), custom_call_target="tpu_custom_call" | custom-call | flops 5368709120 | bytes 22020096 | tf_op jit(solution)/shard_map/pallas_call | solution.py:360
  40.2 2.0 %collective-permute-start.3 = (bf16[2,40,2048]{2,1,0:T(8,128)(2,1)}, bf16[2,40,2048]{2,1,0:T(8,128)(2,1)S(1)}, u32[]{:S(2)}, u32[]{:S(2)}) collective-permute-start(bf16[2,40,2048]{2,1,0:T(8,128)(2,1)} %get-tuple-element.68), channel_id=1, source_target_pairs={{0,2},{2,4},{4,6},{6,7},{7,5},{5,3},{3,1},{1,0},{8,10},{10,12},{12... | collective-permute-start | bytes 983048 | tf_op jit(solution)/shard_map/ppermute | solution.py:475
  42.3 0.1 reshape.69
  42.5 6.0 %collective-permute-done.8.refs_2_ = bf16[2,120,2048]{2,1,0:T(8,128)(2,1)} collective-permute-done((bf16[2,120,2048]{2,1,0:T(8,128)(2,1)}, bf16[2,120,2048]{2,1,0:T(8,128)(2,1)}, u32[]{:S(2)}, u32[]{:S(2)}) %collective-permute-start.8) | collective-permute-done | bytes 983072 | tf_op jit(solution)/shard_map/ppermute | solution.py:23
  48.5 0.6 collective-permute-start.11
  49.1 1.4 collective-permute-done.3
  50.5 1.7 %collective-permute-start.10 = (bf16[64,1408]{1,0:T(8,128)(2,1)S(1)}, bf16[64,1408]{1,0:T(8,128)(2,1)S(1)}, u32[]{:S(2)}, u32[]{:S(2)}) collective-permute-start(bf16[64,1408]{1,0:T(8,128)(2,1)S(1)} %pad_maximum_fusion.8), channel_id=1, source_target_pairs={{0,16},{16,0},{8,24},{24,8},{1,17},{17,1},{9,25},{25,9},{2,18},{18... | collective-permute-start | bytes 540680 | tf_op jit(solution)/shard_map/ppermute | solution.py:23
  52.3 1.6 collective-permute-start.6
  53.9 0.8 collective-permute-start.5
  54.7 13.7 %shard_map.98 = (bf16[120,2048]{1,0:T(8,128)(2,1)}, bf16[120,2048]{1,0:T(8,128)(2,1)}, bf16[120,2048]{1,0:T(8,128)(2,1)}, bf16[120,2048]{1,0:T(8,128)(2,1)}, bf1...) custom-call(s32[8]{0:T(128)} %and_select_fusion.2.table, ...), custom_call_target="tpu_custom_call" | custom-call | flops 8053063680 | bytes 16252928 | tf_op jit(solution)/shard_map/pallas_call | solution.py:411
  68.6 1.6 %collective-permute-start.13 = (bf16[2,40,2048]{2,1,0:T(8,128)(2,1)S(1)}, bf16[2,40,2048]{2,1,0:T(8,128)(2,1)S(1)}, u32[]{:S(2)}, u32[]{:S(2)}) collective-permute-start(bf16[2,40,2048]{2,1,0:T(8,128)(2,1)S(1)} %add_convert_fusion.12), channel_id=1, source_target_pairs={{2,0},{4,2},{6,4},{7,6},{5,7},{3,5},{1,3},{0,1},{10,8},{12,10},{14... | collective-permute-start | bytes 983048 | tf_op jit(solution)/shard_map/ppermute | solution.py:475
  70.3 0.6 collective-permute-start.12
  70.8 1.5 collective-permute-start.14
  72.4 0.5 collective-permute-start.15
  72.9 13.7 %shard_map.99 = (bf16[120,2048]{1,0:T(8,128)(2,1)}, bf16[120,2048]{1,0:T(8,128)(2,1)}, bf16[120,2048]{1,0:T(8,128)(2,1)}, bf16[120,2048]{1,0:T(8,128)(2,1)}, bf1...) custom-call(s32[8]{0:T(128)} %and_select_fusion.2.table, ...), custom_call_target="tpu_custom_call" | custom-call | flops 8053063680 | bytes 16252928 | tf_op jit(solution)/shard_map/pallas_call | solution.py:411
  86.6 1.6 collective-permute-start.18
  88.1 2.3 %collective-permute-done.14 = bf16[120,2048]{1,0:T(8,128)(2,1)S(1)} collective-permute-done((bf16[120,2048]{1,0:T(8,128)(2,1)}, bf16[120,2048]{1,0:T(8,128)(2,1)S(1)}, u32[]{:S(2)}, u32[]{:S(2)}) %collective-permute-start.14) | collective-permute-done | bytes 491552 | tf_op jit(solution)/shard_map/ppermute | solution.py:505
  90.5 1.6 %collective-permute-start.19 = (bf16[120,2048]{1,0:T(8,128)(2,1)}, bf16[120,2048]{1,0:T(8,128)(2,1)S(1)}, u32[]{:S(2)}, u32[]{:S(2)}) collective-permute-start(bf16[120,2048]{1,0:T(8,128)(2,1)} %get-tuple-element.98), channel_id=1, source_target_pairs={{2,0},{4,2},{6,4},{7,6},{5,7},{3,5},{1,3},{0,1},{10,8},{12,10},{14... | collective-permute-start | bytes 1474568 | tf_op jit(solution)/shard_map/ppermute | solution.py:505
  92.1 0.1 add_convert_fusion.10
  92.2 1.6 %collective-permute-start.23 = (bf16[120,2048]{1,0:T(8,128)(2,1)S(1)}, bf16[120,2048]{1,0:T(8,128)(2,1)S(1)}, u32[]{:S(2)}, u32[]{:S(2)}) collective-permute-start(bf16[120,2048]{1,0:T(8,128)(2,1)S(1)} %add_convert_fusion.10), channel_id=1, source_target_pairs={{2,0},{4,2},{6,4},{7,6},{5,7},{3,5},{1,3},{0,1},{10,8},{12,10},{14... | collective-permute-start | bytes 1474568 | tf_op jit(solution)/shard_map/ppermute | solution.py:505
  93.8 0.1 add_convert_fusion.11
  94.0 0.5 collective-permute-start.22
  94.6 6.4 %collective-permute-done.18 = bf16[120,2048]{1,0:T(8,128)(2,1)S(1)} collective-permute-done((bf16[120,2048]{1,0:T(8,128)(2,1)}, bf16[120,2048]{1,0:T(8,128)(2,1)S(1)}, u32[]{:S(2)}, u32[]{:S(2)}) %collective-permute-start.18) | collective-permute-done | bytes 491552 | tf_op jit(solution)/shard_map/ppermute | solution.py:505
  101.0 3.8 %collective-permute-done.19 = bf16[120,2048]{1,0:T(8,128)(2,1)S(1)} collective-permute-done((bf16[120,2048]{1,0:T(8,128)(2,1)}, bf16[120,2048]{1,0:T(8,128)(2,1)S(1)}, u32[]{:S(2)}, u32[]{:S(2)}) %collective-permute-start.19) | collective-permute-done | bytes 491552 | tf_op jit(solution)/shard_map/ppermute | solution.py:505
  104.8 0.1 add_convert_fusion.8
  105.0 1.7 %collective-permute-start.21 = (bf16[120,2048]{1,0:T(8,128)(2,1)S(1)}, bf16[120,2048]{1,0:T(8,128)(2,1)S(1)}, u32[]{:S(2)}, u32[]{:S(2)}) collective-permute-start(bf16[120,2048]{1,0:T(8,128)(2,1)S(1)} %add_convert_fusion.8), channel_id=1, source_target_pairs={{2,0},{4,2},{6,4},{7,6},{5,7},{3,5},{1,3},{0,1},{10,8},{12,10},{14... | collective-permute-start | bytes 1474568 | tf_op jit(solution)/shard_map/ppermute | solution.py:505
  106.6 0.1 add_convert_fusion.9
  106.7 0.5 collective-permute-start.20
  107.2 8.1 %collective-permute-done.23 = bf16[120,2048]{1,0:T(8,128)(2,1)S(1)} collective-permute-done((bf16[120,2048]{1,0:T(8,128)(2,1)S(1)}, bf16[120,2048]{1,0:T(8,128)(2,1)S(1)}, u32[]{:S(2)}, u32[]{:S(2)}) %collective-permute-start.23) | collective-permute-done | bytes 491552 | tf_op jit(solution)/shard_map/ppermute | solution.py:505
  115.4 0.1 add_convert_fusion.6
  115.5 1.7 %collective-permute-start.27 = (bf16[120,2048]{1,0:T(8,128)(2,1)S(1)}, bf16[120,2048]{1,0:T(8,128)(2,1)S(1)}, u32[]{:S(2)}, u32[]{:S(2)}) collective-permute-start(bf16[120,2048]{1,0:T(8,128)(2,1)S(1)} %add_convert_fusion.6), channel_id=1, source_target_pairs={{2,0},{4,2},{6,4},{7,6},{5,7},{3,5},{1,3},{0,1},{10,8},{12,10},{14... | collective-permute-start | bytes 1474568 | tf_op jit(solution)/shard_map/ppermute | solution.py:505
  117.2 0.1 add_convert_fusion.7
  117.3 0.5 collective-permute-start.26
  117.8 8.1 %collective-permute-done.21 = bf16[120,2048]{1,0:T(8,128)(2,1)S(1)} collective-permute-done((bf16[120,2048]{1,0:T(8,128)(2,1)S(1)}, bf16[120,2048]{1,0:T(8,128)(2,1)S(1)}, u32[]{:S(2)}, u32[]{:S(2)}) %collective-permute-start.21) | collective-permute-done | bytes 491552 | tf_op jit(solution)/shard_map/ppermute | solution.py:505
  125.9 0.1 add_convert_fusion.4
  126.0 1.7 %collective-permute-start.25 = (bf16[120,2048]{1,0:T(8,128)(2,1)S(1)}, bf16[120,2048]{1,0:T(8,128)(2,1)S(1)}, u32[]{:S(2)}, u32[]{:S(2)}) collective-permute-start(bf16[120,2048]{1,0:T(8,128)(2,1)S(1)} %add_convert_fusion.4), channel_id=1, source_target_pairs={{2,0},{4,2},{6,4},{7,6},{5,7},{3,5},{1,3},{0,1},{10,8},{12,10},{14... | collective-permute-start | bytes 1474568 | tf_op jit(solution)/shard_map/ppermute | solution.py:505
  127.7 0.1 add_convert_fusion.5
  127.8 0.5 collective-permute-start.24
  128.3 8.1 %collective-permute-done.27 = bf16[120,2048]{1,0:T(8,128)(2,1)S(1)} collective-permute-done((bf16[120,2048]{1,0:T(8,128)(2,1)S(1)}, bf16[120,2048]{1,0:T(8,128)(2,1)S(1)}, u32[]{:S(2)}, u32[]{:S(2)}) %collective-permute-start.27) | collective-permute-done | bytes 491552 | tf_op jit(solution)/shard_map/ppermute | solution.py:505
  136.4 2.0 %collective-permute-start.17 = (bf16[40,2048]{1,0:T(8,128)(2,1)S(1)}, bf16[40,2048]{1,0:T(8,128)(2,1)S(1)}, u32[]{:S(2)}, u32[]{:S(2)}) collective-permute-start(bf16[40,2048]{1,0:T(8,128)(2,1)S(1)} %fusion.2), channel_id=1, source_target_pairs={{2,0},{4,2},{6,4},{7,6},{5,7},{3,5},{1,3},{0,1},{10,8},{12,10},{14... | collective-permute-start | bytes 491528 | tf_op jit(solution)/shard_map/ppermute | solution.py:475
  138.5 0.1 add_convert_fusion.3
  138.6 5.2 %collective-permute-done.25 = bf16[120,2048]{1,0:T(8,128)(2,1)S(1)} collective-permute-done((bf16[120,2048]{1,0:T(8,128)(2,1)S(1)}, bf16[120,2048]{1,0:T(8,128)(2,1)S(1)}, u32[]{:S(2)}, u32[]{:S(2)}) %collective-permute-start.25) | collective-permute-done | bytes 491552 | tf_op jit(solution)/shard_map/ppermute | solution.py:505
  143.8 2.0 %collective-permute-start.28 = (bf16[120,2048]{1,0:T(8,128)(2,1)S(1)}, bf16[120,2048]{1,0:T(8,128)(2,1)S(1)}, u32[]{:S(2)}, u32[]{:S(2)}) collective-permute-start(bf16[120,2048]{1,0:T(8,128)(2,1)S(1)} %add_convert_fusion.3), channel_id=1, source_target_pairs={{0,2},{2,4},{4,6},{6,7},{7,5},{5,3},{3,1},{1,0},{8,10},{10,12},{12... | collective-permute-start | bytes 1474568 | tf_op jit(solution)/shard_map/ppermute | solution.py:505
  145.8 0.1 add_convert_fusion.2
  146.0 0.2 fusion.5
  146.2 0.3 convolution_convert_fusion
  146.5 0.1 collective-permute-done.16
  146.6 0.7 collective-permute-done.17
  147.3 0.7 copy.20
  148.0 0.1 add_convert_fusion.16
  148.1 7.2 %collective-permute-done.28 = bf16[120,2048]{1,0:T(8,128)(2,1)S(1)} collective-permute-done((bf16[120,2048]{1,0:T(8,128)(2,1)S(1)}, bf16[120,2048]{1,0:T(8,128)(2,1)S(1)}, u32[]{:S(2)}, u32[]{:S(2)}) %collective-permute-start.28) | collective-permute-done | bytes 491552 | tf_op jit(solution)/shard_map/ppermute | solution.py:505
  155.3 0.2 add_convert_fusion.1
  155.6 0.2 add_convert_fusion
  155.8 1.1 maximum_maximum_fusion
  (93 shorter events, 1.0 us)
Async XLA Ops:
  7.8 17.4 %copy-start.21 = (s32[64]{0:T(128)S(1)}, s32[64]{0:T(128)}, u32[]{:S(2)}) copy-start(s32[64]{0:T(128)} %param.13) | copy-start | bytes 772
  7.8 17.9 %copy-start.26 = (s32[64]{0:T(128)S(1)}, s32[64]{0:T(128)}, u32[]{:S(2)}) copy-start(s32[64]{0:T(128)} %param.14) | copy-start | bytes 772
  7.8 17.4 %collective-permute-start.1 = (bf16[2,40,2048]{2,1,0:T(8,128)(2,1)}, bf16[2,40,2048]{2,1,0:T(8,128)(2,1)S(1)}, u32[]{:S(2)}, u32[]{:S(2)}) collective-permute-start(bf16[2,40,2048]{2,1,0:T(8,128)(2,1)} %shard_map.95.refs_0_), channel_id=1, source_target_pairs={{0,16},{16,0},{8,24},{24,8},{1,17},{17,1},{9,25},{25,9},{2,18},{18... | collective-permute-start | bytes 983048 | tf_op jit(solution)/shard_map/ppermute | solution.py:23
  10.8 15.3 %collective-permute-start = (bf16[2,40,2048]{2,1,0:T(8,128)(2,1)}, bf16[2,40,2048]{2,1,0:T(8,128)(2,1)S(1)}, u32[]{:S(2)}, u32[]{:S(2)}) collective-permute-start(bf16[2,40,2048]{2,1,0:T(8,128)(2,1)} %shard_map.95.refs_0_), channel_id=1, source_target_pairs={{0,8},{8,0},{16,24},{24,16},{1,9},{9,1},{17,25},{25,17},{2,10},{10... | collective-permute-start | bytes 983048 | tf_op jit(solution)/shard_map/ppermute | solution.py:23
  24.3 24.2 %collective-permute-start.8 = (bf16[2,120,2048]{2,1,0:T(8,128)(2,1)}, bf16[2,120,2048]{2,1,0:T(8,128)(2,1)}, u32[]{:S(2)}, u32[]{:S(2)}) collective-permute-start(bf16[2,120,2048]{2,1,0:T(8,128)(2,1)} %shard_map.96.refs_0_), channel_id=1, source_target_pairs={{0,16},{16,0},{8,24},{24,8},{1,17},{17,1},{9,25},{25,9},{2,18},{18... | collective-permute-start | bytes 2949128 | tf_op jit(solution)/shard_map/ppermute | solution.py:23
  24.5 29.4 %collective-permute-start.7 = (bf16[2,120,2048]{2,1,0:T(8,128)(2,1)}, bf16[2,120,2048]{2,1,0:T(8,128)(2,1)}, u32[]{:S(2)}, u32[]{:S(2)}) collective-permute-start(bf16[2,120,2048]{2,1,0:T(8,128)(2,1)} %shard_map.96.refs_0_), channel_id=1, source_target_pairs={{0,8},{8,0},{16,24},{24,16},{1,9},{9,1},{17,25},{25,17},{2,10},{10... | collective-permute-start | bytes 2949128 | tf_op jit(solution)/shard_map/ppermute | solution.py:23
  25.2 2.3 %copy-start.23 = (bf16[2,40,2048]{2,1,0:T(8,128)(2,1)}, bf16[2,40,2048]{2,1,0:T(8,128)(2,1)S(1)}, u32[]{:S(2)}) copy-start(bf16[2,40,2048]{2,1,0:T(8,128)(2,1)S(1)} %collective-permute-done.1.refs_2_) | copy-start | bytes 983044
  25.2 2.3 %collective-permute-start.2 = (bf16[2,40,2048]{2,1,0:T(8,128)(2,1)S(1)}, bf16[2,40,2048]{2,1,0:T(8,128)(2,1)S(1)}, u32[]{:S(2)}, u32[]{:S(2)}) collective-permute-start(bf16[2,40,2048]{2,1,0:T(8,128)(2,1)S(1)} %collective-permute-done.1.refs_2_), channel_id=1, source_target_pairs={{0,8},{8,0},{16,24},{24,16},{1,9},{9,1},{17,25},{25,17},{2,10},{10... | collective-permute-start | bytes 983048 | tf_op jit(solution)/shard_map/ppermute | solution.py:23
  26.1 16.2 %copy-start = (bf16[320,256]{1,0:T(8,128)(2,1)S(1)}, bf16[320,256]{1,0:T(8,128)(2,1)}, u32[]{:S(2)}) copy-start(bf16[320,256]{1,0:T(8,128)(2,1)} %fresh.3) | copy-start | bytes 491524
  26.1 1.4 copy-start.24
  27.5 0.7 copy-start.25
  40.2 12.0 %copy-start.16 = (bf16[2,40,2048]{2,1,0:T(8,128)(2,1)S(1)}, bf16[2,40,2048]{2,1,0:T(8,128)(2,1)}, u32[]{:S(2)}) copy-start(bf16[2,40,2048]{2,1,0:T(8,128)(2,1)} %get-tuple-element.71) | copy-start | bytes 983044
  40.2 13.6 %copy-start.15 = (bf16[2,40,2048]{2,1,0:T(8,128)(2,1)S(1)}, bf16[2,40,2048]{2,1,0:T(8,128)(2,1)}, u32[]{:S(2)}) copy-start(bf16[2,40,2048]{2,1,0:T(8,128)(2,1)} %get-tuple-element.67) | copy-start | bytes 983044
  40.2 10.2 %collective-permute-start.3 = (bf16[2,40,2048]{2,1,0:T(8,128)(2,1)}, bf16[2,40,2048]{2,1,0:T(8,128)(2,1)S(1)}, u32[]{:S(2)}, u32[]{:S(2)}) collective-permute-start(bf16[2,40,2048]{2,1,0:T(8,128)(2,1)} %get-tuple-element.68), channel_id=1, source_target_pairs={{0,2},{2,4},{4,6},{6,7},{7,5},{5,3},{3,1},{1,0},{8,10},{10,12},{12... | collective-permute-start | bytes 983048 | tf_op jit(solution)/shard_map/ppermute | solution.py:475
  42.3 9.9 %collective-permute-start.4 = (bf16[2,40,2048]{2,1,0:T(8,128)(2,1)}, bf16[2,40,2048]{2,1,0:T(8,128)(2,1)S(1)}, u32[]{:S(2)}, u32[]{:S(2)}) collective-permute-start(bf16[2,40,2048]{2,1,0:T(8,128)(2,1)} %get-tuple-element.69), channel_id=1, source_target_pairs={{2,0},{4,2},{6,4},{7,6},{5,7},{3,5},{1,3},{0,1},{10,8},{12,10},{14... | collective-permute-start | bytes 983048 | tf_op jit(solution)/shard_map/ppermute | solution.py:475
  48.5 6.2 %collective-permute-start.9 = (bf16[2,120,2048]{2,1,0:T(8,128)(2,1)}, bf16[2,120,2048]{2,1,0:T(8,128)(2,1)}, u32[]{:S(2)}, u32[]{:S(2)}) collective-permute-start(bf16[2,120,2048]{2,1,0:T(8,128)(2,1)} %collective-permute-done.8.refs_2_), channel_id=1, source_target_pairs={{0,8},{8,0},{16,24},{24,16},{1,9},{9,1},{17,25},{25,17},{2,10},{10... | collective-permute-start | bytes 2949128 | tf_op jit(solution)/shard_map/ppermute | solution.py:23
  48.5 20.0 %collective-permute-start.11 = (bf16[64,1408]{1,0:T(8,128)(2,1)S(1)}, bf16[64,1408]{1,0:T(8,128)(2,1)S(1)}, u32[]{:S(2)}, u32[]{:S(2)}) collective-permute-start(bf16[64,1408]{1,0:T(8,128)(2,1)S(1)} %pad_maximum_fusion.8), channel_id=1, source_target_pairs={{0,8},{8,0},{16,24},{24,16},{1,9},{9,1},{17,25},{25,17},{2,10},{10... | collective-permute-start | bytes 540680 | tf_op jit(solution)/shard_map/ppermute | solution.py:23
  50.5 18.0 %collective-permute-start.10 = (bf16[64,1408]{1,0:T(8,128)(2,1)S(1)}, bf16[64,1408]{1,0:T(8,128)(2,1)S(1)}, u32[]{:S(2)}, u32[]{:S(2)}) collective-permute-start(bf16[64,1408]{1,0:T(8,128)(2,1)S(1)} %pad_maximum_fusion.8), channel_id=1, source_target_pairs={{0,16},{16,0},{8,24},{24,8},{1,17},{17,1},{9,25},{25,9},{2,18},{18... | collective-permute-start | bytes 540680 | tf_op jit(solution)/shard_map/ppermute | solution.py:23
  52.3 16.2 %collective-permute-start.6 = (bf16[2,40,2048]{2,1,0:T(8,128)(2,1)S(1)}, bf16[2,40,2048]{2,1,0:T(8,128)(2,1)S(1)}, u32[]{:S(2)}, u32[]{:S(2)}) collective-permute-start(bf16[2,40,2048]{2,1,0:T(8,128)(2,1)S(1)} %add_convert_fusion.14), channel_id=1, source_target_pairs={{2,0},{4,2},{6,4},{7,6},{5,7},{3,5},{1,3},{0,1},{10,8},{12,10},{14... | collective-permute-start | bytes 983048 | tf_op jit(solution)/shard_map/ppermute | solution.py:475
  53.9 14.6 %copy-start.14 = (bf16[2,40,2048]{2,1,0:T(8,128)(2,1)S(1)}, bf16[2,40,2048]{2,1,0:T(8,128)(2,1)}, u32[]{:S(2)}) copy-start(bf16[2,40,2048]{2,1,0:T(8,128)(2,1)} %get-tuple-element.80) | copy-start | bytes 983044
  53.9 16.3 %copy-start.13 = (bf16[2,40,2048]{2,1,0:T(8,128)(2,1)S(1)}, bf16[2,40,2048]{2,1,0:T(8,128)(2,1)}, u32[]{:S(2)}) copy-start(bf16[2,40,2048]{2,1,0:T(8,128)(2,1)} %get-tuple-element.66) | copy-start | bytes 983044
  53.9 14.6 %collective-permute-start.5 = (bf16[2,40,2048]{2,1,0:T(8,128)(2,1)S(1)}, bf16[2,40,2048]{2,1,0:T(8,128)(2,1)S(1)}, u32[]{:S(2)}, u32[]{:S(2)}) collective-permute-start(bf16[2,40,2048]{2,1,0:T(8,128)(2,1)S(1)} %add_convert_fusion.15), channel_id=1, source_target_pairs={{0,2},{2,4},{4,6},{6,7},{7,5},{5,3},{3,1},{1,0},{8,10},{10,12},{12... | collective-permute-start | bytes 983048 | tf_op jit(solution)/shard_map/ppermute | solution.py:475
  68.5 3.9 %copy-start.22 = (bf16[120,2048]{1,0:T(8,128)(2,1)S(1)}, bf16[120,2048]{1,0:T(8,128)(2,1)}, u32[]{:S(2)}) copy-start(bf16[120,2048]{1,0:T(8,128)(2,1)} %get-tuple-element.84) | copy-start | bytes 1474564
  68.6 25.4 %collective-permute-start.13 = (bf16[2,40,2048]{2,1,0:T(8,128)(2,1)S(1)}, bf16[2,40,2048]{2,1,0:T(8,128)(2,1)S(1)}, u32[]{:S(2)}, u32[]{:S(2)}) collective-permute-start(bf16[2,40,2048]{2,1,0:T(8,128)(2,1)S(1)} %add_convert_fusion.12), channel_id=1, source_target_pairs={{2,0},{4,2},{6,4},{7,6},{5,7},{3,5},{1,3},{0,1},{10,8},{12,10},{14... | collective-permute-start | bytes 983048 | tf_op jit(solution)/shard_map/ppermute | solution.py:475
  70.3 24.2 %collective-permute-start.12 = (bf16[2,40,2048]{2,1,0:T(8,128)(2,1)S(1)}, bf16[2,40,2048]{2,1,0:T(8,128)(2,1)S(1)}, u32[]{:S(2)}, u32[]{:S(2)}) collective-permute-start(bf16[2,40,2048]{2,1,0:T(8,128)(2,1)S(1)} %add_convert_fusion.13), channel_id=1, source_target_pairs={{0,2},{2,4},{4,6},{6,7},{7,5},{5,3},{3,1},{1,0},{8,10},{10,12},{12... | collective-permute-start | bytes 983048 | tf_op jit(solution)/shard_map/ppermute | solution.py:475
  70.8 19.6 %collective-permute-start.14 = (bf16[120,2048]{1,0:T(8,128)(2,1)}, bf16[120,2048]{1,0:T(8,128)(2,1)S(1)}, u32[]{:S(2)}, u32[]{:S(2)}) collective-permute-start(bf16[120,2048]{1,0:T(8,128)(2,1)} %get-tuple-element.83), channel_id=1, source_target_pairs={{0,2},{2,4},{4,6},{6,7},{7,5},{5,3},{3,1},{1,0},{8,10},{10,12},{12... | collective-permute-start | bytes 1474568 | tf_op jit(solution)/shard_map/ppermute | solution.py:505
  72.4 19.7 %copy-start.8 = (bf16[120,2048]{1,0:T(8,128)(2,1)S(1)}, bf16[120,2048]{1,0:T(8,128)(2,1)}, u32[]{:S(2)}) copy-start(bf16[120,2048]{1,0:T(8,128)(2,1)} %get-tuple-element.88) | copy-start | bytes 1474564
  72.4 19.7 %collective-permute-start.15 = (bf16[120,2048]{1,0:T(8,128)(2,1)S(1)}, bf16[120,2048]{1,0:T(8,128)(2,1)S(1)}, u32[]{:S(2)}, u32[]{:S(2)}) collective-permute-start(bf16[120,2048]{1,0:T(8,128)(2,1)S(1)} %copy-done.22), channel_id=1, source_target_pairs={{2,0},{4,2},{6,4},{7,6},{5,7},{3,5},{1,3},{0,1},{10,8},{12,10},{14... | collective-permute-start | bytes 1474568 | tf_op jit(solution)/shard_map/ppermute | solution.py:505
  86.6 7.3 %copy-start.7 = (bf16[120,2048]{1,0:T(8,128)(2,1)S(1)}, bf16[120,2048]{1,0:T(8,128)(2,1)}, u32[]{:S(2)}) copy-start(bf16[120,2048]{1,0:T(8,128)(2,1)} %get-tuple-element.82) | copy-start | bytes 1474564
  86.6 14.4 %collective-permute-start.18 = (bf16[120,2048]{1,0:T(8,128)(2,1)}, bf16[120,2048]{1,0:T(8,128)(2,1)S(1)}, u32[]{:S(2)}, u32[]{:S(2)}) collective-permute-start(bf16[120,2048]{1,0:T(8,128)(2,1)} %get-tuple-element.97), channel_id=1, source_target_pairs={{0,2},{2,4},{4,6},{6,7},{7,5},{5,3},{3,1},{1,0},{8,10},{10,12},{12... | collective-permute-start | bytes 1474568 | tf_op jit(solution)/shard_map/ppermute | solution.py:505
  90.5 14.4 %collective-permute-start.19 = (bf16[120,2048]{1,0:T(8,128)(2,1)}, bf16[120,2048]{1,0:T(8,128)(2,1)S(1)}, u32[]{:S(2)}, u32[]{:S(2)}) collective-permute-start(bf16[120,2048]{1,0:T(8,128)(2,1)} %get-tuple-element.98), channel_id=1, source_target_pairs={{2,0},{4,2},{6,4},{7,6},{5,7},{3,5},{1,3},{0,1},{10,8},{12,10},{14... | collective-permute-start | bytes 1474568 | tf_op jit(solution)/shard_map/ppermute | solution.py:505
  92.1 2.4 %copy-start.20 = (bf16[40,2048]{1,0:T(8,128)(2,1)S(1)}, bf16[40,2048]{1,0:T(8,128)(2,1)}, u32[]{:S(2)}) copy-start(bf16[40,2048]{1,0:T(8,128)(2,1)} %get-tuple-element.93) | copy-start | bytes 491524
  92.2 2.4 %copy-start.19 = (bf16[40,2048]{1,0:T(8,128)(2,1)S(1)}, bf16[40,2048]{1,0:T(8,128)(2,1)}, u32[]{:S(2)}) copy-start(bf16[40,2048]{1,0:T(8,128)(2,1)} %get-tuple-element.91) | copy-start | bytes 491524
  92.2 12.6 %copy-start.10 = (bf16[120,2048]{1,0:T(8,128)(2,1)S(1)}, bf16[120,2048]{1,0:T(8,128)(2,1)}, u32[]{:S(2)}) copy-start(bf16[120,2048]{1,0:T(8,128)(2,1)} %get-tuple-element.100) | copy-start | bytes 1474564
  92.2 23.1 %collective-permute-start.23 = (bf16[120,2048]{1,0:T(8,128)(2,1)S(1)}, bf16[120,2048]{1,0:T(8,128)(2,1)S(1)}, u32[]{:S(2)}, u32[]{:S(2)}) collective-permute-start(bf16[120,2048]{1,0:T(8,128)(2,1)S(1)} %add_convert_fusion.10), channel_id=1, source_target_pairs={{2,0},{4,2},{6,4},{7,6},{5,7},{3,5},{1,3},{0,1},{10,8},{12,10},{14... | collective-permute-start | bytes 1474568 | tf_op jit(solution)/shard_map/ppermute | solution.py:505
  94.0 12.7 %copy-start.9 = (bf16[120,2048]{1,0:T(8,128)(2,1)S(1)}, bf16[120,2048]{1,0:T(8,128)(2,1)}, u32[]{:S(2)}) copy-start(bf16[120,2048]{1,0:T(8,128)(2,1)} %get-tuple-element.96) | copy-start | bytes 1474564
  94.0 21.4 %collective-permute-start.22 = (bf16[120,2048]{1,0:T(8,128)(2,1)S(1)}, bf16[120,2048]{1,0:T(8,128)(2,1)S(1)}, u32[]{:S(2)}, u32[]{:S(2)}) collective-permute-start(bf16[120,2048]{1,0:T(8,128)(2,1)S(1)} %add_convert_fusion.11), channel_id=1, source_target_pairs={{0,2},{2,4},{4,6},{6,7},{7,5},{5,3},{3,1},{1,0},{8,10},{10,12},{12... | collective-permute-start | bytes 1474568 | tf_op jit(solution)/shard_map/ppermute | solution.py:505
  104.8 10.5 %copy-start.4 = (bf16[120,2048]{1,0:T(8,128)(2,1)S(1)}, bf16[120,2048]{1,0:T(8,128)(2,1)}, u32[]{:S(2)}) copy-start(bf16[120,2048]{1,0:T(8,128)(2,1)} %get-tuple-element.104) | copy-start | bytes 1474564
  105.0 20.9 %collective-permute-start.21 = (bf16[120,2048]{1,0:T(8,128)(2,1)S(1)}, bf16[120,2048]{1,0:T(8,128)(2,1)S(1)}, u32[]{:S(2)}, u32[]{:S(2)}) collective-permute-start(bf16[120,2048]{1,0:T(8,128)(2,1)S(1)} %add_convert_fusion.8), channel_id=1, source_target_pairs={{2,0},{4,2},{6,4},{7,6},{5,7},{3,5},{1,3},{0,1},{10,8},{12,10},{14... | collective-permute-start | bytes 1474568 | tf_op jit(solution)/shard_map/ppermute | solution.py:505
  106.6 10.5 %copy-start.3 = (bf16[120,2048]{1,0:T(8,128)(2,1)S(1)}, bf16[120,2048]{1,0:T(8,128)(2,1)}, u32[]{:S(2)}) copy-start(bf16[120,2048]{1,0:T(8,128)(2,1)} %get-tuple-element.102) | copy-start | bytes 1474564
  106.7 19.1 %collective-permute-start.20 = (bf16[120,2048]{1,0:T(8,128)(2,1)S(1)}, bf16[120,2048]{1,0:T(8,128)(2,1)S(1)}, u32[]{:S(2)}, u32[]{:S(2)}) collective-permute-start(bf16[120,2048]{1,0:T(8,128)(2,1)S(1)} %add_convert_fusion.9), channel_id=1, source_target_pairs={{0,2},{2,4},{4,6},{6,7},{7,5},{5,3},{3,1},{1,0},{8,10},{10,12},{12... | collective-permute-start | bytes 1474568 | tf_op jit(solution)/shard_map/ppermute | solution.py:505
  115.4 10.5 %copy-start.6 = (bf16[120,2048]{1,0:T(8,128)(2,1)S(1)}, bf16[120,2048]{1,0:T(8,128)(2,1)}, u32[]{:S(2)}) copy-start(bf16[120,2048]{1,0:T(8,128)(2,1)} %get-tuple-element.107) | copy-start | bytes 1474564
  115.5 20.9 %collective-permute-start.27 = (bf16[120,2048]{1,0:T(8,128)(2,1)S(1)}, bf16[120,2048]{1,0:T(8,128)(2,1)S(1)}, u32[]{:S(2)}, u32[]{:S(2)}) collective-permute-start(bf16[120,2048]{1,0:T(8,128)(2,1)S(1)} %add_convert_fusion.6), channel_id=1, source_target_pairs={{2,0},{4,2},{6,4},{7,6},{5,7},{3,5},{1,3},{0,1},{10,8},{12,10},{14... | collective-permute-start | bytes 1474568 | tf_op jit(solution)/shard_map/ppermute | solution.py:505
  117.2 10.5 %copy-start.5 = (bf16[120,2048]{1,0:T(8,128)(2,1)S(1)}, bf16[120,2048]{1,0:T(8,128)(2,1)}, u32[]{:S(2)}) copy-start(bf16[120,2048]{1,0:T(8,128)(2,1)} %get-tuple-element.95) | copy-start | bytes 1474564
  117.3 19.1 %collective-permute-start.26 = (bf16[120,2048]{1,0:T(8,128)(2,1)S(1)}, bf16[120,2048]{1,0:T(8,128)(2,1)S(1)}, u32[]{:S(2)}, u32[]{:S(2)}) collective-permute-start(bf16[120,2048]{1,0:T(8,128)(2,1)S(1)} %add_convert_fusion.7), channel_id=1, source_target_pairs={{0,2},{2,4},{4,6},{6,7},{7,5},{5,3},{3,1},{1,0},{8,10},{10,12},{12... | collective-permute-start | bytes 1474568 | tf_op jit(solution)/shard_map/ppermute | solution.py:505
  125.9 12.6 %copy-start.1 = (bf16[120,2048]{1,0:T(8,128)(2,1)S(1)}, bf16[120,2048]{1,0:T(8,128)(2,1)}, u32[]{:S(2)}) copy-start(bf16[120,2048]{1,0:T(8,128)(2,1)} %get-tuple-element.109) | copy-start | bytes 1474564
  126.0 17.8 %collective-permute-start.25 = (bf16[120,2048]{1,0:T(8,128)(2,1)S(1)}, bf16[120,2048]{1,0:T(8,128)(2,1)S(1)}, u32[]{:S(2)}, u32[]{:S(2)}) collective-permute-start(bf16[120,2048]{1,0:T(8,128)(2,1)S(1)} %add_convert_fusion.4), channel_id=1, source_target_pairs={{2,0},{4,2},{6,4},{7,6},{5,7},{3,5},{1,3},{0,1},{10,8},{12,10},{14... | collective-permute-start | bytes 1474568 | tf_op jit(solution)/shard_map/ppermute | solution.py:505
  127.7 18.1 %copy-start.2 = (bf16[120,2048]{1,0:T(8,128)(2,1)S(1)}, bf16[120,2048]{1,0:T(8,128)(2,1)}, u32[]{:S(2)}) copy-start(bf16[120,2048]{1,0:T(8,128)(2,1)} %get-tuple-element.94) | copy-start | bytes 1474564
  127.8 18.0 %collective-permute-start.24 = (bf16[120,2048]{1,0:T(8,128)(2,1)S(1)}, bf16[120,2048]{1,0:T(8,128)(2,1)S(1)}, u32[]{:S(2)}, u32[]{:S(2)}) collective-permute-start(bf16[120,2048]{1,0:T(8,128)(2,1)S(1)} %add_convert_fusion.5), channel_id=1, source_target_pairs={{0,2},{2,4},{4,6},{6,7},{7,5},{5,3},{3,1},{1,0},{8,10},{10,12},{12... | collective-permute-start | bytes 1474568 | tf_op jit(solution)/shard_map/ppermute | solution.py:505
  128.3 17.7 %collective-permute-start.30 = (bf16[64,1408]{1,0:T(8,128)(2,1)S(1)}, bf16[64,1408]{1,0:T(8,128)(2,1)S(1)}, u32[]{:S(2)}, u32[]{:S(2)}) collective-permute-start(bf16[64,1408]{1,0:T(8,128)(2,1)S(1)} %collective-permute-done.10), channel_id=1, source_target_pairs={{0,8},{8,0},{16,24},{24,16},{1,9},{9,1},{17,25},{25,17},{2,10},{10... | collective-permute-start | bytes 540680 | tf_op jit(solution)/shard_map/ppermute | solution.py:23
  136.4 10.2 %collective-permute-start.16 = (bf16[40,2048]{1,0:T(8,128)(2,1)S(1)}, bf16[40,2048]{1,0:T(8,128)(2,1)S(1)}, u32[]{:S(2)}, u32[]{:S(2)}) collective-permute-start(bf16[40,2048]{1,0:T(8,128)(2,1)S(1)} %fusion.3), channel_id=1, source_target_pairs={{0,2},{2,4},{4,6},{6,7},{7,5},{5,3},{3,1},{1,0},{8,10},{10,12},{12... | collective-permute-start | bytes 491528 | tf_op jit(solution)/shard_map/ppermute | solution.py:475
  136.4 10.9 %collective-permute-start.17 = (bf16[40,2048]{1,0:T(8,128)(2,1)S(1)}, bf16[40,2048]{1,0:T(8,128)(2,1)S(1)}, u32[]{:S(2)}, u32[]{:S(2)}) collective-permute-start(bf16[40,2048]{1,0:T(8,128)(2,1)S(1)} %fusion.2), channel_id=1, source_target_pairs={{2,0},{4,2},{6,4},{7,6},{5,7},{3,5},{1,3},{0,1},{10,8},{12,10},{14... | collective-permute-start | bytes 491528 | tf_op jit(solution)/shard_map/ppermute | solution.py:475
  143.8 11.6 %collective-permute-start.28 = (bf16[120,2048]{1,0:T(8,128)(2,1)S(1)}, bf16[120,2048]{1,0:T(8,128)(2,1)S(1)}, u32[]{:S(2)}, u32[]{:S(2)}) collective-permute-start(bf16[120,2048]{1,0:T(8,128)(2,1)S(1)} %add_convert_fusion.3), channel_id=1, source_target_pairs={{0,2},{2,4},{4,6},{6,7},{7,5},{5,3},{3,1},{1,0},{8,10},{10,12},{12... | collective-permute-start | bytes 1474568 | tf_op jit(solution)/shard_map/ppermute | solution.py:505
  145.9 9.7 %collective-permute-start.29 = (bf16[120,2048]{1,0:T(8,128)(2,1)S(1)}, bf16[120,2048]{1,0:T(8,128)(2,1)S(1)}, u32[]{:S(2)}, u32[]{:S(2)}) collective-permute-start(bf16[120,2048]{1,0:T(8,128)(2,1)S(1)} %add_convert_fusion.2), channel_id=1, source_target_pairs={{2,0},{4,2},{6,4},{7,6},{5,7},{3,5},{1,3},{0,1},{10,8},{12,10},{14... | collective-permute-start | bytes 1474568 | tf_op jit(solution)/shard_map/ppermute | solution.py:505
  146.2 1.8 %copy-start.17 = (bf16[40,2048]{1,0:T(8,128)(2,1)S(1)}, bf16[40,2048]{1,0:T(8,128)(2,1)}, u32[]{:S(2)}) copy-start(bf16[40,2048]{1,0:T(8,128)(2,1)} %get-tuple-element.65) | copy-start | bytes 491524
  146.2 1.8 %copy-start.18 = (bf16[40,2048]{1,0:T(8,128)(2,1)S(1)}, bf16[40,2048]{1,0:T(8,128)(2,1)}, u32[]{:S(2)}) copy-start(bf16[40,2048]{1,0:T(8,128)(2,1)} %get-tuple-element.113) | copy-start | bytes 491524
  146.5 8.8 %copy-start.11 = (bf16[120,2048]{1,0:T(8,128)(2,1)S(1)}, bf16[120,2048]{1,0:T(8,128)(2,1)}, u32[]{:S(2)}) copy-start(bf16[120,2048]{1,0:T(8,128)(2,1)} %get-tuple-element.75) | copy-start | bytes 1474564
  148.0 7.6 %copy-start.12 = (bf16[120,2048]{1,0:T(8,128)(2,1)S(1)}, bf16[120,2048]{1,0:T(8,128)(2,1)}, u32[]{:S(2)}) copy-start(bf16[120,2048]{1,0:T(8,128)(2,1)} %get-tuple-element.86) | copy-start | bytes 1474564

commit v3 on v2

--- a/solution.py
+++ b/solution.py
@@ -28,7 +28,7 @@
 
 
 def attention_kernel(scale, first, count, drafts, group, ahead, lens, q, k, v, fresh, out,
-                     q_raw, q_wide, f_wide, o_wide, k_held, v_held, order, q_sems, k_sems, v_sems):
+                     q_raw, q_wide, f_raw, f_wide, o_wide, k_held, v_held, order, f_sem, q_sems, k_sems, v_sems):
     halves = out.shape[0]
     size = k.shape[2]
     span = k.shape[1]
@@ -85,15 +85,18 @@
         start = h * stride * drafts + low
         return pltpu.make_async_copy(q.at[pl.ds(start, taken)], q_raw.at[h], q_sems.at[h])
 
+    fresh_copy = pltpu.make_async_copy(fresh, f_raw, f_sem)
+    fresh_copy.start()
     for h in range(halves):
         query_copy(h).start()
-    totals = lax.fori_loop(0, beams, tally, (jnp.int32(0),) * most)
-    lax.fori_loop(0, beams, rank, (jnp.int32(0),) + totals[:-1])
+    totals = lax.fori_loop(0, beams, tally, (jnp.int32(0),) * most, unroll=8)
+    lax.fori_loop(0, beams, rank, (jnp.int32(0),) + totals[:-1], unroll=8)
     ahead = min(ahead, groups)
     for g in range(ahead):
         by_length(g, begin)
+    fresh_copy.wait()
     for side in range(2):
-        f_wide[side, : fresh.shape[0]] = fresh[:, side * size : (side + 1) * size].astype(jnp.float32)
+        f_wide[side, : fresh.shape[0]] = f_raw[:, side * size : (side + 1) * size].astype(jnp.float32)
         f_wide[side, fresh.shape[0] :] = jnp.zeros((8, size), jnp.float32)
     for h in range(halves):
         query_copy(h).wait()
@@ -177,21 +180,24 @@
     taken = (first + count) * drafts - first * drafts // 16 * 16
     taken = (taken + 15) // 16 * 16
     chosen = halves * count
+    group = group if count > 8 else 4
     full = pl.BlockSpec(memory_space=pltpu.VMEM)
     outside = pl.BlockSpec(memory_space=pl.ANY)
     return pl.pallas_call(
         functools.partial(attention_kernel, size**-0.5, first, count, drafts, group, ahead),
         out_shape=jax.ShapeDtypeStruct((halves, count * drafts, columns), jnp.bfloat16),
-        in_specs=[pl.BlockSpec(memory_space=pltpu.SMEM), outside, outside, outside, full],
+        in_specs=[pl.BlockSpec(memory_space=pltpu.SMEM), outside, outside, outside, outside],
         out_specs=full,
         scratch_shapes=[
             pltpu.VMEM((halves, taken, columns), jnp.bfloat16),
             pltpu.VMEM((halves, taken, heads, size), jnp.float32),
+            pltpu.VMEM(fresh.shape, jnp.bfloat16),
             pltpu.VMEM((2, fresh.shape[0] + 8, size), jnp.float32),
             pltpu.VMEM((halves, count * drafts, heads, size), jnp.float32),
             pltpu.VMEM((chosen, span, size), jnp.bfloat16),
             pltpu.VMEM((chosen, span, size), jnp.bfloat16),
             pltpu.SMEM((chosen,), jnp.int32),
+            pltpu.SemaphoreType.DMA,
             pltpu.SemaphoreType.DMA((halves,)),
             pltpu.SemaphoreType.DMA((chosen,)),
             pltpu.SemaphoreType.DMA((chosen,)),

time: 157 us -> 155 us (0.987)
  waiting for transfers between devices: 59 us -> 56.7 us
  starting transfers between devices: 30.4 us -> 32.3 us
  Pallas kernels: 60 us -> 58.3 us
    ppermute x14, waiting for transfers between devices: 49.4 us -> 46 us  [advance(): self.arrived.append(lax.ppermute(own, 'mp', route))]
    ppermute x14, starting transfers between devices: 15.8 us -> 17.9 us  [advance(): self.arrived.append(lax.ppermute(own, 'mp', route))]
    ppermute x8, waiting for transfers between devices: 2.18 us -> 4.13 us  [advance(): lax.ppermute(block, 'mp', route)]
    pallas_call x2, Pallas kernels: 20.7 us -> 18.9 us  [attend(): pl.pallas_call(functools.partial(attention_kernel, size ** (-0.5), first,...]
  transfers between devices with their start and end apart: 31 -> 31, of which waited for: 13 -> 13; matrix products, arithmetic and copies ran while one was open for 3% -> 3% of each run, Pallas kernels for 34% -> 33%
where the time goes in v3:
time: 155 us
  Pallas kernels  58.3 us (38%)
  waiting for transfers between devices  56.7 us (37%)
  starting transfers between devices  32.3 us (21%)
  other arithmetic  4.16 us (3%)
  local copies, waits for them, and re-layouts  1.94 us (1%)
    ppermute x14, waiting for transfers between devices, advance(): self.arrived.append(lax.ppermute(own, 'mp', route))  46 us
    pallas_call x2, Pallas kernels, project_side(): pl.pallas_call(functools.partial(project_side_kernel, len(blocks), pieces...  27.4 us
    pallas_call x2, Pallas kernels, attend(): pl.pallas_call(functools.partial(attention_kernel, size ** (-0.5), first,...  18.9 us
    ppermute x14, starting transfers between devices, advance(): self.arrived.append(lax.ppermute(own, 'mp', route))  17.9 us
    pallas_call x1, Pallas kernels, project(): pl.pallas_call(functools.partial(project_kernel, len(blocks), pieces, hal...  11.9 us
    ppermute x8, starting transfers between devices, advance(): lax.ppermute(block, 'mp', route)  9.48 us
    ppermute x9, waiting for transfers between devices, partner(): return lax.ppermute(block, axis, route)  6.54 us
    ppermute x9, starting transfers between devices, partner(): return lax.ppermute(block, axis, route)  4.89 us
  transfers between devices with their start and end apart: 31, of which 13 were waited for; matrix products, arithmetic and copies ran while one was open for 3% of the time, Pallas kernels for 33%

profile of v3, /device:TPU:0, one launch (start us, length us, event | category | flops | bytes accessed | tf_op | source)
XLA Modules:
  0.0 154.8 jit_solution(12872580264697102382)
XLA Ops:
  0.6 6.6 %shard_map.95.refs_0_ = bf16[2,40,2048]{2,1,0:T(8,128)(2,1)} custom-call(s32[64]{0:T(128)} %lens.3, bf16[320,2048]{1,0:T(8,128)(2,1)} %q.1, bf16[64,1024,128]{2,1,0:T(8,128)(2,1)} %bitcast.24, bf16[64,1024,128]{2,1,0:T(8,128)(2,1)} %bitcast.26, bf16[320,256]{1,0:T(8,128)(2,1)} %fresh.3), custom_call_target="tpu_custom_call" | custom-call | flops 671088640 | bytes 8388608 | tf_op jit(solution)/shard_map/pallas_call | solution.py:186
  7.2 2.6 %collective-permute-start.1 = (bf16[2,40,2048]{2,1,0:T(8,128)(2,1)}, bf16[2,40,2048]{2,1,0:T(8,128)(2,1)S(1)}, u32[]{:S(2)}, u32[]{:S(2)}) collective-permute-start(bf16[2,40,2048]{2,1,0:T(8,128)(2,1)} %shard_map.95.refs_0_), channel_id=1, source_target_pairs={{0,16},{16,0},{8,24},{24,8},{1,17},{17,1},{9,25},{25,9},{2,18},{18... | collective-permute-start | bytes 983048 | tf_op jit(solution)/shard_map/ppermute | solution.py:23
  9.8 12.4 %shard_map.96.refs_0_ = bf16[2,120,2048]{2,1,0:T(8,128)(2,1)} custom-call(s32[64]{0:T(128)} %lens.3, bf16[320,2048]{1,0:T(8,128)(2,1)} %q.1, bf16[64,1024,128]{2,1,0:T(8,128)(2,1)} %bitcast.25, bf16[64,1024,128]{2,1,0:T(8,128)(2,1)} %bitcast.27, bf16[320,256]{1,0:T(8,128)(2,1)} %fresh.3), custom_call_target="tpu_custom_call" | custom-call | flops 2013265920 | bytes 25165824 | tf_op jit(solution)/shard_map/pallas_call | solution.py:186
  22.3 0.7 collective-permute-start.7
  22.9 0.6 and_select_fusion.2.table
  23.7 0.1 copy.15
  23.8 0.1 broadcast_in_dim.18
  24.0 1.5 collective-permute-done.2.refs_3_
  25.6 0.7 copy-done.25
  26.3 11.9 %shard_map.97 = (bf16[2,40,2048]{2,1,0:T(8,128)(2,1)}, bf16[2,40,2048]{2,1,0:T(8,128)(2,1)}, bf16[2,40,2048]{2,1,0:T(8,128)(2,1)}, bf16[2,40,2048]{2,1,0:T(8,128...) custom-call(s32[8]{0:T(128)} %and_select_fusion.2.table, ...), custom_call_target="tpu_custom_call" | custom-call | flops 5368709120 | bytes 22020096 | tf_op jit(solution)/shard_map/pallas_call | solution.py:366
  38.3 2.5 %collective-permute-start.3 = (bf16[2,40,2048]{2,1,0:T(8,128)(2,1)}, bf16[2,40,2048]{2,1,0:T(8,128)(2,1)S(1)}, u32[]{:S(2)}, u32[]{:S(2)}) collective-permute-start(bf16[2,40,2048]{2,1,0:T(8,128)(2,1)} %get-tuple-element.68), channel_id=1, source_target_pairs={{0,2},{2,4},{4,6},{6,7},{7,5},{5,3},{3,1},{1,0},{8,10},{10,12},{12... | collective-permute-start | bytes 983048 | tf_op jit(solution)/shard_map/ppermute | solution.py:481
  40.8 0.1 reshape.69
  41.0 5.0 %collective-permute-done.8.refs_2_ = bf16[2,120,2048]{2,1,0:T(8,128)(2,1)} collective-permute-done((bf16[2,120,2048]{2,1,0:T(8,128)(2,1)}, bf16[2,120,2048]{2,1,0:T(8,128)(2,1)}, u32[]{:S(2)}, u32[]{:S(2)}) %collective-permute-start.8) | collective-permute-done | bytes 983072 | tf_op jit(solution)/shard_map/ppermute | solution.py:23
  46.0 0.6 collective-permute-start.11
  46.5 2.6 %collective-permute-done.3 = bf16[2,40,2048]{2,1,0:T(8,128)(2,1)S(1)} collective-permute-done((bf16[2,40,2048]{2,1,0:T(8,128)(2,1)}, bf16[2,40,2048]{2,1,0:T(8,128)(2,1)S(1)}, u32[]{:S(2)}, u32[]{:S(2)}) %collective-permute-start.3) | collective-permute-done | bytes 327712 | tf_op jit(solution)/shard_map/ppermute | solution.py:481
  49.2 0.8 collective-permute-start.10
  50.0 0.7 collective-permute-done.4
  50.7 0.1 add_convert_fusion.14
  50.8 0.9 collective-permute-start.6
  51.8 1.5 collective-permute-start.5
  53.3 13.7 %shard_map.98 = (bf16[120,2048]{1,0:T(8,128)(2,1)}, bf16[120,2048]{1,0:T(8,128)(2,1)}, bf16[120,2048]{1,0:T(8,128)(2,1)}, bf16[120,2048]{1,0:T(8,128)(2,1)}, bf1...) custom-call(s32[8]{0:T(128)} %and_select_fusion.2.table, ...), custom_call_target="tpu_custom_call" | custom-call | flops 8053063680 | bytes 16252928 | tf_op jit(solution)/shard_map/pallas_call | solution.py:417
  67.1 0.1 add_convert_fusion.12
  67.1 0.9 collective-permute-start.13
  68.1 1.3 collective-permute-start.12
  69.4 1.5 collective-permute-start.14
  70.8 0.5 collective-permute-start.15
  71.4 13.7 %shard_map.99 = (bf16[120,2048]{1,0:T(8,128)(2,1)}, bf16[120,2048]{1,0:T(8,128)(2,1)}, bf16[120,2048]{1,0:T(8,128)(2,1)}, bf16[120,2048]{1,0:T(8,128)(2,1)}, bf1...) custom-call(s32[8]{0:T(128)} %and_select_fusion.2.table, ...), custom_call_target="tpu_custom_call" | custom-call | flops 8053063680 | bytes 16252928 | tf_op jit(solution)/shard_map/pallas_call | solution.py:417
  85.1 1.5 collective-permute-start.18
  86.6 0.7 collective-permute-done.14
  87.3 2.5 %collective-permute-start.19 = (bf16[120,2048]{1,0:T(8,128)(2,1)}, bf16[120,2048]{1,0:T(8,128)(2,1)S(1)}, u32[]{:S(2)}, u32[]{:S(2)}) collective-permute-start(bf16[120,2048]{1,0:T(8,128)(2,1)} %get-tuple-element.98), channel_id=1, source_target_pairs={{2,0},{4,2},{6,4},{7,6},{5,7},{3,5},{1,3},{0,1},{10,8},{12,10},{14... | collective-permute-start | bytes 1474568 | tf_op jit(solution)/shard_map/ppermute | solution.py:511
  89.9 0.1 add_convert_fusion.10
  90.0 1.7 %collective-permute-start.23 = (bf16[120,2048]{1,0:T(8,128)(2,1)S(1)}, bf16[120,2048]{1,0:T(8,128)(2,1)S(1)}, u32[]{:S(2)}, u32[]{:S(2)}) collective-permute-start(bf16[120,2048]{1,0:T(8,128)(2,1)S(1)} %add_convert_fusion.10), channel_id=1, source_target_pairs={{2,0},{4,2},{6,4},{7,6},{5,7},{3,5},{1,3},{0,1},{10,8},{12,10},{14... | collective-permute-start | bytes 1474568 | tf_op jit(solution)/shard_map/ppermute | solution.py:511
  91.7 0.1 add_convert_fusion.11
  91.8 0.5 collective-permute-start.22
  92.4 7.1 %collective-permute-done.18 = bf16[120,2048]{1,0:T(8,128)(2,1)S(1)} collective-permute-done((bf16[120,2048]{1,0:T(8,128)(2,1)}, bf16[120,2048]{1,0:T(8,128)(2,1)S(1)}, u32[]{:S(2)}, u32[]{:S(2)}) %collective-permute-start.18) | collective-permute-done | bytes 491552 | tf_op jit(solution)/shard_map/ppermute | solution.py:511
  99.5 2.4 %collective-permute-done.19 = bf16[120,2048]{1,0:T(8,128)(2,1)S(1)} collective-permute-done((bf16[120,2048]{1,0:T(8,128)(2,1)}, bf16[120,2048]{1,0:T(8,128)(2,1)S(1)}, u32[]{:S(2)}, u32[]{:S(2)}) %collective-permute-start.19) | collective-permute-done | bytes 491552 | tf_op jit(solution)/shard_map/ppermute | solution.py:511
  101.9 0.1 add_convert_fusion.8
  102.0 2.4 %collective-permute-start.21 = (bf16[120,2048]{1,0:T(8,128)(2,1)S(1)}, bf16[120,2048]{1,0:T(8,128)(2,1)S(1)}, u32[]{:S(2)}, u32[]{:S(2)}) collective-permute-start(bf16[120,2048]{1,0:T(8,128)(2,1)S(1)} %add_convert_fusion.8), channel_id=1, source_target_pairs={{2,0},{4,2},{6,4},{7,6},{5,7},{3,5},{1,3},{0,1},{10,8},{12,10},{14... | collective-permute-start | bytes 1474568 | tf_op jit(solution)/shard_map/ppermute | solution.py:511
  104.4 0.1 add_convert_fusion.9
  104.6 7.7 %collective-permute-done.23 = bf16[120,2048]{1,0:T(8,128)(2,1)S(1)} collective-permute-done((bf16[120,2048]{1,0:T(8,128)(2,1)S(1)}, bf16[120,2048]{1,0:T(8,128)(2,1)S(1)}, u32[]{:S(2)}, u32[]{:S(2)}) %collective-permute-start.23) | collective-permute-done | bytes 491552 | tf_op jit(solution)/shard_map/ppermute | solution.py:511
  112.3 0.1 add_convert_fusion.6
  112.4 2.5 %collective-permute-start.27 = (bf16[120,2048]{1,0:T(8,128)(2,1)S(1)}, bf16[120,2048]{1,0:T(8,128)(2,1)S(1)}, u32[]{:S(2)}, u32[]{:S(2)}) collective-permute-start(bf16[120,2048]{1,0:T(8,128)(2,1)S(1)} %add_convert_fusion.6), channel_id=1, source_target_pairs={{2,0},{4,2},{6,4},{7,6},{5,7},{3,5},{1,3},{0,1},{10,8},{12,10},{14... | collective-permute-start | bytes 1474568 | tf_op jit(solution)/shard_map/ppermute | solution.py:511
  115.0 0.1 add_convert_fusion.7
  115.2 7.7 %collective-permute-done.21 = bf16[120,2048]{1,0:T(8,128)(2,1)S(1)} collective-permute-done((bf16[120,2048]{1,0:T(8,128)(2,1)S(1)}, bf16[120,2048]{1,0:T(8,128)(2,1)S(1)}, u32[]{:S(2)}, u32[]{:S(2)}) %collective-permute-start.21) | collective-permute-done | bytes 491552 | tf_op jit(solution)/shard_map/ppermute | solution.py:511
  122.8 0.1 add_convert_fusion.4
  123.0 2.5 %collective-permute-start.25 = (bf16[120,2048]{1,0:T(8,128)(2,1)S(1)}, bf16[120,2048]{1,0:T(8,128)(2,1)S(1)}, u32[]{:S(2)}, u32[]{:S(2)}) collective-permute-start(bf16[120,2048]{1,0:T(8,128)(2,1)S(1)} %add_convert_fusion.4), channel_id=1, source_target_pairs={{2,0},{4,2},{6,4},{7,6},{5,7},{3,5},{1,3},{0,1},{10,8},{12,10},{14... | collective-permute-start | bytes 1474568 | tf_op jit(solution)/shard_map/ppermute | solution.py:511
  125.5 0.1 add_convert_fusion.5
  125.8 7.6 %collective-permute-done.27 = bf16[120,2048]{1,0:T(8,128)(2,1)S(1)} collective-permute-done((bf16[120,2048]{1,0:T(8,128)(2,1)S(1)}, bf16[120,2048]{1,0:T(8,128)(2,1)S(1)}, u32[]{:S(2)}, u32[]{:S(2)}) %collective-permute-start.27) | collective-permute-done | bytes 491552 | tf_op jit(solution)/shard_map/ppermute | solution.py:511
  133.4 1.5 collective-permute-start.16
  134.9 1.0 collective-permute-start.17
  135.9 0.1 add_convert_fusion.3
  136.0 6.7 %collective-permute-done.25 = bf16[120,2048]{1,0:T(8,128)(2,1)S(1)} collective-permute-done((bf16[120,2048]{1,0:T(8,128)(2,1)S(1)}, bf16[120,2048]{1,0:T(8,128)(2,1)S(1)}, u32[]{:S(2)}, u32[]{:S(2)}) %collective-permute-start.25) | collective-permute-done | bytes 491552 | tf_op jit(solution)/shard_map/ppermute | solution.py:511
  142.7 1.7 %collective-permute-start.28 = (bf16[120,2048]{1,0:T(8,128)(2,1)S(1)}, bf16[120,2048]{1,0:T(8,128)(2,1)S(1)}, u32[]{:S(2)}, u32[]{:S(2)}) collective-permute-start(bf16[120,2048]{1,0:T(8,128)(2,1)S(1)} %add_convert_fusion.3), channel_id=1, source_target_pairs={{0,2},{2,4},{4,6},{6,7},{7,5},{5,3},{3,1},{1,0},{8,10},{10,12},{12... | collective-permute-start | bytes 1474568 | tf_op jit(solution)/shard_map/ppermute | solution.py:511
  144.4 0.1 add_convert_fusion.2
  144.5 0.4 collective-permute-start.29
  144.9 0.2 fusion.5
  145.1 0.3 convolution_convert_fusion
  145.4 0.8 collective-permute-done.17
  146.2 0.7 copy.20
  146.9 0.1 add_convert_fusion.16
  147.0 6.2 %collective-permute-done.28 = bf16[120,2048]{1,0:T(8,128)(2,1)S(1)} collective-permute-done((bf16[120,2048]{1,0:T(8,128)(2,1)S(1)}, bf16[120,2048]{1,0:T(8,128)(2,1)S(1)}, u32[]{:S(2)}, u32[]{:S(2)}) %collective-permute-start.28) | collective-permute-done | bytes 491552 | tf_op jit(solution)/shard_map/ppermute | solution.py:511
  153.2 0.2 add_convert_fusion.1
  153.5 0.2 add_convert_fusion
  153.7 1.1 maximum_maximum_fusion
  (93 shorter events, 1.1 us)
Async XLA Ops:
  7.2 16.3 %copy-start.21 = (s32[64]{0:T(128)S(1)}, s32[64]{0:T(128)}, u32[]{:S(2)}) copy-start(s32[64]{0:T(128)} %param.13) | copy-start | bytes 772
  7.2 16.4 %copy-start.26 = (s32[64]{0:T(128)S(1)}, s32[64]{0:T(128)}, u32[]{:S(2)}) copy-start(s32[64]{0:T(128)} %param.14) | copy-start | bytes 772
  7.2 16.3 %collective-permute-start.1 = (bf16[2,40,2048]{2,1,0:T(8,128)(2,1)}, bf16[2,40,2048]{2,1,0:T(8,128)(2,1)S(1)}, u32[]{:S(2)}, u32[]{:S(2)}) collective-permute-start(bf16[2,40,2048]{2,1,0:T(8,128)(2,1)} %shard_map.95.refs_0_), channel_id=1, source_target_pairs={{0,16},{16,0},{8,24},{24,8},{1,17},{17,1},{9,25},{25,9},{2,18},{18... | collective-permute-start | bytes 983048 | tf_op jit(solution)/shard_map/ppermute | solution.py:23
  9.8 14.2 %collective-permute-start = (bf16[2,40,2048]{2,1,0:T(8,128)(2,1)}, bf16[2,40,2048]{2,1,0:T(8,128)(2,1)S(1)}, u32[]{:S(2)}, u32[]{:S(2)}) collective-permute-start(bf16[2,40,2048]{2,1,0:T(8,128)(2,1)} %shard_map.95.refs_0_), channel_id=1, source_target_pairs={{0,8},{8,0},{16,24},{24,16},{1,9},{9,1},{17,25},{25,17},{2,10},{10... | collective-permute-start | bytes 983048 | tf_op jit(solution)/shard_map/ppermute | solution.py:23
  22.2 23.8 %collective-permute-start.8 = (bf16[2,120,2048]{2,1,0:T(8,128)(2,1)}, bf16[2,120,2048]{2,1,0:T(8,128)(2,1)}, u32[]{:S(2)}, u32[]{:S(2)}) collective-permute-start(bf16[2,120,2048]{2,1,0:T(8,128)(2,1)} %shard_map.96.refs_0_), channel_id=1, source_target_pairs={{0,16},{16,0},{8,24},{24,8},{1,17},{17,1},{9,25},{25,9},{2,18},{18... | collective-permute-start | bytes 2949128 | tf_op jit(solution)/shard_map/ppermute | solution.py:23
  22.3 29.5 %collective-permute-start.7 = (bf16[2,120,2048]{2,1,0:T(8,128)(2,1)}, bf16[2,120,2048]{2,1,0:T(8,128)(2,1)}, u32[]{:S(2)}, u32[]{:S(2)}) collective-permute-start(bf16[2,120,2048]{2,1,0:T(8,128)(2,1)} %shard_map.96.refs_0_), channel_id=1, source_target_pairs={{0,8},{8,0},{16,24},{24,16},{1,9},{9,1},{17,25},{25,17},{2,10},{10... | collective-permute-start | bytes 2949128 | tf_op jit(solution)/shard_map/ppermute | solution.py:23
  23.6 2.0 %copy-start.23 = (bf16[2,40,2048]{2,1,0:T(8,128)(2,1)}, bf16[2,40,2048]{2,1,0:T(8,128)(2,1)S(1)}, u32[]{:S(2)}) copy-start(bf16[2,40,2048]{2,1,0:T(8,128)(2,1)S(1)} %collective-permute-done.1.refs_2_) | copy-start | bytes 983044
  23.6 2.0 %collective-permute-start.2 = (bf16[2,40,2048]{2,1,0:T(8,128)(2,1)S(1)}, bf16[2,40,2048]{2,1,0:T(8,128)(2,1)S(1)}, u32[]{:S(2)}, u32[]{:S(2)}) collective-permute-start(bf16[2,40,2048]{2,1,0:T(8,128)(2,1)S(1)} %collective-permute-done.1.refs_2_), channel_id=1, source_target_pairs={{0,8},{8,0},{16,24},{24,16},{1,9},{9,1},{17,25},{25,17},{2,10},{10... | collective-permute-start | bytes 983048 | tf_op jit(solution)/shard_map/ppermute | solution.py:23
  24.0 16.8 %copy-start = (bf16[320,256]{1,0:T(8,128)(2,1)S(1)}, bf16[320,256]{1,0:T(8,128)(2,1)}, u32[]{:S(2)}) copy-start(bf16[320,256]{1,0:T(8,128)(2,1)} %fresh.3) | copy-start | bytes 491524
  24.0 1.5 copy-start.24
  25.6 0.7 copy-start.25
  38.2 12.5 %copy-start.16 = (bf16[2,40,2048]{2,1,0:T(8,128)(2,1)S(1)}, bf16[2,40,2048]{2,1,0:T(8,128)(2,1)}, u32[]{:S(2)}) copy-start(bf16[2,40,2048]{2,1,0:T(8,128)(2,1)} %get-tuple-element.71) | copy-start | bytes 983044
  38.3 13.4 %copy-start.15 = (bf16[2,40,2048]{2,1,0:T(8,128)(2,1)S(1)}, bf16[2,40,2048]{2,1,0:T(8,128)(2,1)}, u32[]{:S(2)}) copy-start(bf16[2,40,2048]{2,1,0:T(8,128)(2,1)} %get-tuple-element.67) | copy-start | bytes 983044
  38.3 10.9 %collective-permute-start.3 = (bf16[2,40,2048]{2,1,0:T(8,128)(2,1)}, bf16[2,40,2048]{2,1,0:T(8,128)(2,1)S(1)}, u32[]{:S(2)}, u32[]{:S(2)}) collective-permute-start(bf16[2,40,2048]{2,1,0:T(8,128)(2,1)} %get-tuple-element.68), channel_id=1, source_target_pairs={{0,2},{2,4},{4,6},{6,7},{7,5},{5,3},{3,1},{1,0},{8,10},{10,12},{12... | collective-permute-start | bytes 983048 | tf_op jit(solution)/shard_map/ppermute | solution.py:481
  40.7 10.0 %collective-permute-start.4 = (bf16[2,40,2048]{2,1,0:T(8,128)(2,1)}, bf16[2,40,2048]{2,1,0:T(8,128)(2,1)S(1)}, u32[]{:S(2)}, u32[]{:S(2)}) collective-permute-start(bf16[2,40,2048]{2,1,0:T(8,128)(2,1)} %get-tuple-element.69), channel_id=1, source_target_pairs={{2,0},{4,2},{6,4},{7,6},{5,7},{3,5},{1,3},{0,1},{10,8},{12,10},{14... | collective-permute-start | bytes 983048 | tf_op jit(solution)/shard_map/ppermute | solution.py:481
  45.9 7.3 %collective-permute-start.9 = (bf16[2,120,2048]{2,1,0:T(8,128)(2,1)}, bf16[2,120,2048]{2,1,0:T(8,128)(2,1)}, u32[]{:S(2)}, u32[]{:S(2)}) collective-permute-start(bf16[2,120,2048]{2,1,0:T(8,128)(2,1)} %collective-permute-done.8.refs_2_), channel_id=1, source_target_pairs={{0,8},{8,0},{16,24},{24,16},{1,9},{9,1},{17,25},{25,17},{2,10},{10... | collective-permute-start | bytes 2949128 | tf_op jit(solution)/shard_map/ppermute | solution.py:23
  46.0 21.0 %collective-permute-start.11 = (bf16[64,1408]{1,0:T(8,128)(2,1)S(1)}, bf16[64,1408]{1,0:T(8,128)(2,1)S(1)}, u32[]{:S(2)}, u32[]{:S(2)}) collective-permute-start(bf16[64,1408]{1,0:T(8,128)(2,1)S(1)} %pad_maximum_fusion.8), channel_id=1, source_target_pairs={{0,8},{8,0},{16,24},{24,16},{1,9},{9,1},{17,25},{25,17},{2,10},{10... | collective-permute-start | bytes 540680 | tf_op jit(solution)/shard_map/ppermute | solution.py:23
  49.2 17.9 %collective-permute-start.10 = (bf16[64,1408]{1,0:T(8,128)(2,1)S(1)}, bf16[64,1408]{1,0:T(8,128)(2,1)S(1)}, u32[]{:S(2)}, u32[]{:S(2)}) collective-permute-start(bf16[64,1408]{1,0:T(8,128)(2,1)S(1)} %pad_maximum_fusion.8), channel_id=1, source_target_pairs={{0,16},{16,0},{8,24},{24,8},{1,17},{17,1},{9,25},{25,9},{2,18},{18... | collective-permute-start | bytes 540680 | tf_op jit(solution)/shard_map/ppermute | solution.py:23
  50.8 16.2 %collective-permute-start.6 = (bf16[2,40,2048]{2,1,0:T(8,128)(2,1)S(1)}, bf16[2,40,2048]{2,1,0:T(8,128)(2,1)S(1)}, u32[]{:S(2)}, u32[]{:S(2)}) collective-permute-start(bf16[2,40,2048]{2,1,0:T(8,128)(2,1)S(1)} %add_convert_fusion.14), channel_id=1, source_target_pairs={{2,0},{4,2},{6,4},{7,6},{5,7},{3,5},{1,3},{0,1},{10,8},{12,10},{14... | collective-permute-start | bytes 983048 | tf_op jit(solution)/shard_map/ppermute | solution.py:481
  51.8 15.3 %copy-start.14 = (bf16[2,40,2048]{2,1,0:T(8,128)(2,1)S(1)}, bf16[2,40,2048]{2,1,0:T(8,128)(2,1)}, u32[]{:S(2)}) copy-start(bf16[2,40,2048]{2,1,0:T(8,128)(2,1)} %get-tuple-element.80) | copy-start | bytes 983044
  51.8 16.3 %copy-start.13 = (bf16[2,40,2048]{2,1,0:T(8,128)(2,1)S(1)}, bf16[2,40,2048]{2,1,0:T(8,128)(2,1)}, u32[]{:S(2)}) copy-start(bf16[2,40,2048]{2,1,0:T(8,128)(2,1)} %get-tuple-element.66) | copy-start | bytes 983044
  51.8 15.2 %collective-permute-start.5 = (bf16[2,40,2048]{2,1,0:T(8,128)(2,1)S(1)}, bf16[2,40,2048]{2,1,0:T(8,128)(2,1)S(1)}, u32[]{:S(2)}, u32[]{:S(2)}) collective-permute-start(bf16[2,40,2048]{2,1,0:T(8,128)(2,1)S(1)} %add_convert_fusion.15), channel_id=1, source_target_pairs={{0,2},{2,4},{4,6},{6,7},{7,5},{5,3},{3,1},{1,0},{8,10},{10,12},{12... | collective-permute-start | bytes 983048 | tf_op jit(solution)/shard_map/ppermute | solution.py:481
  67.0 3.8 %copy-start.22 = (bf16[120,2048]{1,0:T(8,128)(2,1)S(1)}, bf16[120,2048]{1,0:T(8,128)(2,1)}, u32[]{:S(2)}) copy-start(bf16[120,2048]{1,0:T(8,128)(2,1)} %get-tuple-element.84) | copy-start | bytes 1474564
  67.1 24.7 %collective-permute-start.13 = (bf16[2,40,2048]{2,1,0:T(8,128)(2,1)S(1)}, bf16[2,40,2048]{2,1,0:T(8,128)(2,1)S(1)}, u32[]{:S(2)}, u32[]{:S(2)}) collective-permute-start(bf16[2,40,2048]{2,1,0:T(8,128)(2,1)S(1)} %add_convert_fusion.12), channel_id=1, source_target_pairs={{2,0},{4,2},{6,4},{7,6},{5,7},{3,5},{1,3},{0,1},{10,8},{12,10},{14... | collective-permute-start | bytes 983048 | tf_op jit(solution)/shard_map/ppermute | solution.py:481
  68.1 24.2 %collective-permute-start.12 = (bf16[2,40,2048]{2,1,0:T(8,128)(2,1)S(1)}, bf16[2,40,2048]{2,1,0:T(8,128)(2,1)S(1)}, u32[]{:S(2)}, u32[]{:S(2)}) collective-permute-start(bf16[2,40,2048]{2,1,0:T(8,128)(2,1)S(1)} %add_convert_fusion.13), channel_id=1, source_target_pairs={{0,2},{2,4},{4,6},{6,7},{7,5},{5,3},{3,1},{1,0},{8,10},{10,12},{12... | collective-permute-start | bytes 983048 | tf_op jit(solution)/shard_map/ppermute | solution.py:481
  69.4 18.0 %collective-permute-start.14 = (bf16[120,2048]{1,0:T(8,128)(2,1)}, bf16[120,2048]{1,0:T(8,128)(2,1)S(1)}, u32[]{:S(2)}, u32[]{:S(2)}) collective-permute-start(bf16[120,2048]{1,0:T(8,128)(2,1)} %get-tuple-element.83), channel_id=1, source_target_pairs={{0,2},{2,4},{4,6},{6,7},{7,5},{5,3},{3,1},{1,0},{8,10},{10,12},{12... | collective-permute-start | bytes 1474568 | tf_op jit(solution)/shard_map/ppermute | solution.py:511
  70.8 19.0 %copy-start.8 = (bf16[120,2048]{1,0:T(8,128)(2,1)S(1)}, bf16[120,2048]{1,0:T(8,128)(2,1)}, u32[]{:S(2)}) copy-start(bf16[120,2048]{1,0:T(8,128)(2,1)} %get-tuple-element.88) | copy-start | bytes 1474564
  70.8 19.0 %collective-permute-start.15 = (bf16[120,2048]{1,0:T(8,128)(2,1)S(1)}, bf16[120,2048]{1,0:T(8,128)(2,1)S(1)}, u32[]{:S(2)}, u32[]{:S(2)}) collective-permute-start(bf16[120,2048]{1,0:T(8,128)(2,1)S(1)} %copy-done.22), channel_id=1, source_target_pairs={{2,0},{4,2},{6,4},{7,6},{5,7},{3,5},{1,3},{0,1},{10,8},{12,10},{14... | collective-permute-start | bytes 1474568 | tf_op jit(solution)/shard_map/ppermute | solution.py:511
  85.1 6.6 %copy-start.7 = (bf16[120,2048]{1,0:T(8,128)(2,1)S(1)}, bf16[120,2048]{1,0:T(8,128)(2,1)}, u32[]{:S(2)}) copy-start(bf16[120,2048]{1,0:T(8,128)(2,1)} %get-tuple-element.82) | copy-start | bytes 1474564
  85.1 14.4 %collective-permute-start.18 = (bf16[120,2048]{1,0:T(8,128)(2,1)}, bf16[120,2048]{1,0:T(8,128)(2,1)S(1)}, u32[]{:S(2)}, u32[]{:S(2)}) collective-permute-start(bf16[120,2048]{1,0:T(8,128)(2,1)} %get-tuple-element.97), channel_id=1, source_target_pairs={{0,2},{2,4},{4,6},{6,7},{7,5},{5,3},{3,1},{1,0},{8,10},{10,12},{12... | collective-permute-start | bytes 1474568 | tf_op jit(solution)/shard_map/ppermute | solution.py:511
  87.3 14.5 %collective-permute-start.19 = (bf16[120,2048]{1,0:T(8,128)(2,1)}, bf16[120,2048]{1,0:T(8,128)(2,1)S(1)}, u32[]{:S(2)}, u32[]{:S(2)}) collective-permute-start(bf16[120,2048]{1,0:T(8,128)(2,1)} %get-tuple-element.98), channel_id=1, source_target_pairs={{2,0},{4,2},{6,4},{7,6},{5,7},{3,5},{1,3},{0,1},{10,8},{12,10},{14... | collective-permute-start | bytes 1474568 | tf_op jit(solution)/shard_map/ppermute | solution.py:511
  89.9 2.4 %copy-start.20 = (bf16[40,2048]{1,0:T(8,128)(2,1)S(1)}, bf16[40,2048]{1,0:T(8,128)(2,1)}, u32[]{:S(2)}) copy-start(bf16[40,2048]{1,0:T(8,128)(2,1)} %get-tuple-element.93) | copy-start | bytes 491524
  90.0 2.4 %copy-start.19 = (bf16[40,2048]{1,0:T(8,128)(2,1)S(1)}, bf16[40,2048]{1,0:T(8,128)(2,1)}, u32[]{:S(2)}) copy-start(bf16[40,2048]{1,0:T(8,128)(2,1)} %get-tuple-element.91) | copy-start | bytes 491524
  90.0 11.9 %copy-start.10 = (bf16[120,2048]{1,0:T(8,128)(2,1)S(1)}, bf16[120,2048]{1,0:T(8,128)(2,1)}, u32[]{:S(2)}) copy-start(bf16[120,2048]{1,0:T(8,128)(2,1)} %get-tuple-element.100) | copy-start | bytes 1474564
  90.0 22.3 %collective-permute-start.23 = (bf16[120,2048]{1,0:T(8,128)(2,1)S(1)}, bf16[120,2048]{1,0:T(8,128)(2,1)S(1)}, u32[]{:S(2)}, u32[]{:S(2)}) collective-permute-start(bf16[120,2048]{1,0:T(8,128)(2,1)S(1)} %add_convert_fusion.10), channel_id=1, source_target_pairs={{2,0},{4,2},{6,4},{7,6},{5,7},{3,5},{1,3},{0,1},{10,8},{12,10},{14... | collective-permute-start | bytes 1474568 | tf_op jit(solution)/shard_map/ppermute | solution.py:511
  91.8 12.6 %copy-start.9 = (bf16[120,2048]{1,0:T(8,128)(2,1)S(1)}, bf16[120,2048]{1,0:T(8,128)(2,1)}, u32[]{:S(2)}) copy-start(bf16[120,2048]{1,0:T(8,128)(2,1)} %get-tuple-element.96) | copy-start | bytes 1474564
  91.8 20.5 %collective-permute-start.22 = (bf16[120,2048]{1,0:T(8,128)(2,1)S(1)}, bf16[120,2048]{1,0:T(8,128)(2,1)S(1)}, u32[]{:S(2)}, u32[]{:S(2)}) collective-permute-start(bf16[120,2048]{1,0:T(8,128)(2,1)S(1)} %add_convert_fusion.11), channel_id=1, source_target_pairs={{0,2},{2,4},{4,6},{6,7},{7,5},{5,3},{3,1},{1,0},{8,10},{10,12},{12... | collective-permute-start | bytes 1474568 | tf_op jit(solution)/shard_map/ppermute | solution.py:511
  101.9 10.4 %copy-start.4 = (bf16[120,2048]{1,0:T(8,128)(2,1)S(1)}, bf16[120,2048]{1,0:T(8,128)(2,1)}, u32[]{:S(2)}) copy-start(bf16[120,2048]{1,0:T(8,128)(2,1)} %get-tuple-element.104) | copy-start | bytes 1474564
  102.0 20.8 %collective-permute-start.21 = (bf16[120,2048]{1,0:T(8,128)(2,1)S(1)}, bf16[120,2048]{1,0:T(8,128)(2,1)S(1)}, u32[]{:S(2)}, u32[]{:S(2)}) collective-permute-start(bf16[120,2048]{1,0:T(8,128)(2,1)S(1)} %add_convert_fusion.8), channel_id=1, source_target_pairs={{2,0},{4,2},{6,4},{7,6},{5,7},{3,5},{1,3},{0,1},{10,8},{12,10},{14... | collective-permute-start | bytes 1474568 | tf_op jit(solution)/shard_map/ppermute | solution.py:511
  104.4 10.5 %copy-start.3 = (bf16[120,2048]{1,0:T(8,128)(2,1)S(1)}, bf16[120,2048]{1,0:T(8,128)(2,1)}, u32[]{:S(2)}) copy-start(bf16[120,2048]{1,0:T(8,128)(2,1)} %get-tuple-element.102) | copy-start | bytes 1474564
  104.6 18.3 %collective-permute-start.20 = (bf16[120,2048]{1,0:T(8,128)(2,1)S(1)}, bf16[120,2048]{1,0:T(8,128)(2,1)S(1)}, u32[]{:S(2)}, u32[]{:S(2)}) collective-permute-start(bf16[120,2048]{1,0:T(8,128)(2,1)S(1)} %add_convert_fusion.9), channel_id=1, source_target_pairs={{0,2},{2,4},{4,6},{6,7},{7,5},{5,3},{3,1},{1,0},{8,10},{10,12},{12... | collective-permute-start | bytes 1474568 | tf_op jit(solution)/shard_map/ppermute | solution.py:511
  112.3 10.5 %copy-start.6 = (bf16[120,2048]{1,0:T(8,128)(2,1)S(1)}, bf16[120,2048]{1,0:T(8,128)(2,1)}, u32[]{:S(2)}) copy-start(bf16[120,2048]{1,0:T(8,128)(2,1)} %get-tuple-element.107) | copy-start | bytes 1474564
  112.4 20.9 %collective-permute-start.27 = (bf16[120,2048]{1,0:T(8,128)(2,1)S(1)}, bf16[120,2048]{1,0:T(8,128)(2,1)S(1)}, u32[]{:S(2)}, u32[]{:S(2)}) collective-permute-start(bf16[120,2048]{1,0:T(8,128)(2,1)S(1)} %add_convert_fusion.6), channel_id=1, source_target_pairs={{2,0},{4,2},{6,4},{7,6},{5,7},{3,5},{1,3},{0,1},{10,8},{12,10},{14... | collective-permute-start | bytes 1474568 | tf_op jit(solution)/shard_map/ppermute | solution.py:511
  115.0 10.5 %copy-start.5 = (bf16[120,2048]{1,0:T(8,128)(2,1)S(1)}, bf16[120,2048]{1,0:T(8,128)(2,1)}, u32[]{:S(2)}) copy-start(bf16[120,2048]{1,0:T(8,128)(2,1)} %get-tuple-element.95) | copy-start | bytes 1474564
  115.1 19.8 %collective-permute-start.26 = (bf16[120,2048]{1,0:T(8,128)(2,1)S(1)}, bf16[120,2048]{1,0:T(8,128)(2,1)S(1)}, u32[]{:S(2)}, u32[]{:S(2)}) collective-permute-start(bf16[120,2048]{1,0:T(8,128)(2,1)S(1)} %add_convert_fusion.7), channel_id=1, source_target_pairs={{0,2},{2,4},{4,6},{6,7},{7,5},{5,3},{3,1},{1,0},{8,10},{10,12},{12... | collective-permute-start | bytes 1474568 | tf_op jit(solution)/shard_map/ppermute | solution.py:511
  122.8 13.0 %copy-start.1 = (bf16[120,2048]{1,0:T(8,128)(2,1)S(1)}, bf16[120,2048]{1,0:T(8,128)(2,1)}, u32[]{:S(2)}) copy-start(bf16[120,2048]{1,0:T(8,128)(2,1)} %get-tuple-element.109) | copy-start | bytes 1474564
  123.0 19.7 %collective-permute-start.25 = (bf16[120,2048]{1,0:T(8,128)(2,1)S(1)}, bf16[120,2048]{1,0:T(8,128)(2,1)S(1)}, u32[]{:S(2)}, u32[]{:S(2)}) collective-permute-start(bf16[120,2048]{1,0:T(8,128)(2,1)S(1)} %add_convert_fusion.4), channel_id=1, source_target_pairs={{2,0},{4,2},{6,4},{7,6},{5,7},{3,5},{1,3},{0,1},{10,8},{12,10},{14... | collective-permute-start | bytes 1474568 | tf_op jit(solution)/shard_map/ppermute | solution.py:511
  125.5 18.9 %copy-start.2 = (bf16[120,2048]{1,0:T(8,128)(2,1)S(1)}, bf16[120,2048]{1,0:T(8,128)(2,1)}, u32[]{:S(2)}) copy-start(bf16[120,2048]{1,0:T(8,128)(2,1)} %get-tuple-element.94) | copy-start | bytes 1474564
  125.6 18.7 %collective-permute-start.24 = (bf16[120,2048]{1,0:T(8,128)(2,1)S(1)}, bf16[120,2048]{1,0:T(8,128)(2,1)S(1)}, u32[]{:S(2)}, u32[]{:S(2)}) collective-permute-start(bf16[120,2048]{1,0:T(8,128)(2,1)S(1)} %add_convert_fusion.5), channel_id=1, source_target_pairs={{0,2},{2,4},{4,6},{6,7},{7,5},{5,3},{3,1},{1,0},{8,10},{10,12},{12... | collective-permute-start | bytes 1474568 | tf_op jit(solution)/shard_map/ppermute | solution.py:511
  125.7 19.2 %collective-permute-start.30 = (bf16[64,1408]{1,0:T(8,128)(2,1)S(1)}, bf16[64,1408]{1,0:T(8,128)(2,1)S(1)}, u32[]{:S(2)}, u32[]{:S(2)}) collective-permute-start(bf16[64,1408]{1,0:T(8,128)(2,1)S(1)} %collective-permute-done.10), channel_id=1, source_target_pairs={{0,8},{8,0},{16,24},{24,16},{1,9},{9,1},{17,25},{25,17},{2,10},{10... | collective-permute-start | bytes 540680 | tf_op jit(solution)/shard_map/ppermute | solution.py:23
  133.4 12.1 %collective-permute-start.16 = (bf16[40,2048]{1,0:T(8,128)(2,1)S(1)}, bf16[40,2048]{1,0:T(8,128)(2,1)S(1)}, u32[]{:S(2)}, u32[]{:S(2)}) collective-permute-start(bf16[40,2048]{1,0:T(8,128)(2,1)S(1)} %fusion.3), channel_id=1, source_target_pairs={{0,2},{2,4},{4,6},{6,7},{7,5},{5,3},{3,1},{1,0},{8,10},{10,12},{12... | collective-permute-start | bytes 491528 | tf_op jit(solution)/shard_map/ppermute | solution.py:481
  134.9 11.4 %collective-permute-start.17 = (bf16[40,2048]{1,0:T(8,128)(2,1)S(1)}, bf16[40,2048]{1,0:T(8,128)(2,1)S(1)}, u32[]{:S(2)}, u32[]{:S(2)}) collective-permute-start(bf16[40,2048]{1,0:T(8,128)(2,1)S(1)} %fusion.2), channel_id=1, source_target_pairs={{2,0},{4,2},{6,4},{7,6},{5,7},{3,5},{1,3},{0,1},{10,8},{12,10},{14... | collective-permute-start | bytes 491528 | tf_op jit(solution)/shard_map/ppermute | solution.py:481
  142.7 10.5 %collective-permute-start.28 = (bf16[120,2048]{1,0:T(8,128)(2,1)S(1)}, bf16[120,2048]{1,0:T(8,128)(2,1)S(1)}, u32[]{:S(2)}, u32[]{:S(2)}) collective-permute-start(bf16[120,2048]{1,0:T(8,128)(2,1)S(1)} %add_convert_fusion.3), channel_id=1, source_target_pairs={{0,2},{2,4},{4,6},{6,7},{7,5},{5,3},{3,1},{1,0},{8,10},{10,12},{12... | collective-permute-start | bytes 1474568 | tf_op jit(solution)/shard_map/ppermute | solution.py:511
  144.5 9.0 %collective-permute-start.29 = (bf16[120,2048]{1,0:T(8,128)(2,1)S(1)}, bf16[120,2048]{1,0:T(8,128)(2,1)S(1)}, u32[]{:S(2)}, u32[]{:S(2)}) collective-permute-start(bf16[120,2048]{1,0:T(8,128)(2,1)S(1)} %add_convert_fusion.2), channel_id=1, source_target_pairs={{2,0},{4,2},{6,4},{7,6},{5,7},{3,5},{1,3},{0,1},{10,8},{12,10},{14... | collective-permute-start | bytes 1474568 | tf_op jit(solution)/shard_map/ppermute | solution.py:511
  145.1 1.8 %copy-start.17 = (bf16[40,2048]{1,0:T(8,128)(2,1)S(1)}, bf16[40,2048]{1,0:T(8,128)(2,1)}, u32[]{:S(2)}) copy-start(bf16[40,2048]{1,0:T(8,128)(2,1)} %get-tuple-element.65) | copy-start | bytes 491524
  145.1 1.8 %copy-start.18 = (bf16[40,2048]{1,0:T(8,128)(2,1)S(1)}, bf16[40,2048]{1,0:T(8,128)(2,1)}, u32[]{:S(2)}) copy-start(bf16[40,2048]{1,0:T(8,128)(2,1)} %get-tuple-element.113) | copy-start | bytes 491524
  145.4 7.8 %copy-start.11 = (bf16[120,2048]{1,0:T(8,128)(2,1)S(1)}, bf16[120,2048]{1,0:T(8,128)(2,1)}, u32[]{:S(2)}) copy-start(bf16[120,2048]{1,0:T(8,128)(2,1)} %get-tuple-element.75) | copy-start | bytes 1474564
  146.9 6.6 %copy-start.12 = (bf16[120,2048]{1,0:T(8,128)(2,1)S(1)}, bf16[120,2048]{1,0:T(8,128)(2,1)}, u32[]{:S(2)}) copy-start(bf16[120,2048]{1,0:T(8,128)(2,1)} %get-tuple-element.86) | copy-start | bytes 1474564

commit v4 on v3

--- a/solution.py
+++ b/solution.py
@@ -147,7 +147,7 @@
         for s, limit in zip(scores, limits):
             s = jnp.where(spots <= limit, s, masked_score)
             top = jnp.max(s, 1, keepdims=True)
-            w = jnp.exp((s - top) * scale).astype(jnp.bfloat16)
+            w = jnp.exp2((s - top) * (scale * 1.4426950408889634)).astype(jnp.bfloat16)
             weights.append((w, 1.0 / jnp.sum(w.astype(jnp.float32), 1, keepdims=True)))
         totals = []
         for (w, share), one, two in zip(weights, chosen[::2], chosen[1::2]):
@@ -355,7 +355,7 @@
     places = pieces * len(blocks)
     half = places // 2
     columns = weight.shape[1] // 2
-    tile = min(1024, columns)
+    tile = min(2048, columns)
     tiles = columns // tile
     pair = jax.ShapeDtypeStruct((2, rows, columns), jnp.bfloat16)
     single = jax.ShapeDtypeStruct((rows, columns), jnp.bfloat16)

time: 155 us -> 155 us (level)
  waiting for transfers between devices: 56.7 us -> 58.7 us
  starting transfers between devices: 32.3 us -> 30.7 us
    ppermute x14, waiting for transfers between devices: 46 us -> 49.2 us  [advance(): self.arrived.append(lax.ppermute(own, 'mp', route))]
    ppermute x14, starting transfers between devices: 17.9 us -> 16 us  [advance(): self.arrived.append(lax.ppermute(own, 'mp', route))]
    ppermute x8, waiting for transfers between devices: 4.13 us -> 2.26 us  [advance(): lax.ppermute(block, 'mp', route)]
where the time goes in v4:
time: 155 us
  waiting for transfers between devices  58.7 us (38%)
  Pallas kernels  57.6 us (37%)
  starting transfers between devices  30.7 us (20%)
  other arithmetic  4.17 us (3%)
  local copies, waits for them, and re-layouts  1.94 us (1%)
    ppermute x14, waiting for transfers between devices, advance(): self.arrived.append(lax.ppermute(own, 'mp', route))  49.2 us
    pallas_call x2, Pallas kernels, project_side(): pl.pallas_call(functools.partial(project_side_kernel, len(blocks), pieces...  27.4 us
    pallas_call x2, Pallas kernels, attend(): pl.pallas_call(functools.partial(attention_kernel, size ** (-0.5), first,...  18.3 us
    ppermute x14, starting transfers between devices, advance(): self.arrived.append(lax.ppermute(own, 'mp', route))  16 us
    pallas_call x1, Pallas kernels, project(): pl.pallas_call(functools.partial(project_kernel, len(blocks), pieces, hal...  12 us
    ppermute x8, starting transfers between devices, advance(): lax.ppermute(block, 'mp', route)  8.58 us
    ppermute x9, waiting for transfers between devices, partner(): return lax.ppermute(block, axis, route)  7.16 us
    ppermute x9, starting transfers between devices, partner(): return lax.ppermute(block, axis, route)  6.2 us
  transfers between devices with their start and end apart: 31, of which 13 were waited for; matrix products, arithmetic and copies ran while one was open for 3% of the time, Pallas kernels for 33%

profile of v4, /device:TPU:0, one launch (start us, length us, event | category | flops | bytes accessed | tf_op | source)
XLA Modules:
  0.0 154.6 jit_solution(9127236602968476572)
XLA Ops:
  0.6 6.2 %shard_map.95.refs_0_ = bf16[2,40,2048]{2,1,0:T(8,128)(2,1)} custom-call(s32[64]{0:T(128)} %lens.3, bf16[320,2048]{1,0:T(8,128)(2,1)} %q.1, bf16[64,1024,128]{2,1,0:T(8,128)(2,1)} %bitcast.24, bf16[64,1024,128]{2,1,0:T(8,128)(2,1)} %bitcast.26, bf16[320,256]{1,0:T(8,128)(2,1)} %fresh.3), custom_call_target="tpu_custom_call" | custom-call | flops 671088640 | bytes 8388608 | tf_op jit(solution)/shard_map/pallas_call | solution.py:186
  6.9 3.0 %collective-permute-start.1 = (bf16[2,40,2048]{2,1,0:T(8,128)(2,1)}, bf16[2,40,2048]{2,1,0:T(8,128)(2,1)S(1)}, u32[]{:S(2)}, u32[]{:S(2)}) collective-permute-start(bf16[2,40,2048]{2,1,0:T(8,128)(2,1)} %shard_map.95.refs_0_), channel_id=1, source_target_pairs={{0,16},{16,0},{8,24},{24,8},{1,17},{17,1},{9,25},{25,9},{2,18},{18... | collective-permute-start | bytes 983048 | tf_op jit(solution)/shard_map/ppermute | solution.py:23
  9.9 12.0 %shard_map.96.refs_0_ = bf16[2,120,2048]{2,1,0:T(8,128)(2,1)} custom-call(s32[64]{0:T(128)} %lens.3, bf16[320,2048]{1,0:T(8,128)(2,1)} %q.1, bf16[64,1024,128]{2,1,0:T(8,128)(2,1)} %bitcast.25, bf16[64,1024,128]{2,1,0:T(8,128)(2,1)} %bitcast.27, bf16[320,256]{1,0:T(8,128)(2,1)} %fresh.3), custom_call_target="tpu_custom_call" | custom-call | flops 2013265920 | bytes 25165824 | tf_op jit(solution)/shard_map/pallas_call | solution.py:186
  22.1 0.6 and_select_fusion.2.table
  22.8 0.5 collective-permute-start.2
  23.3 0.1 copy.15
  23.5 0.1 broadcast_in_dim.18
  23.7 1.4 collective-permute-done.2.refs_3_
  25.1 0.7 copy-done.25
  25.8 12.0 %shard_map.97 = (bf16[2,40,2048]{2,1,0:T(8,128)(2,1)}, bf16[2,40,2048]{2,1,0:T(8,128)(2,1)}, bf16[2,40,2048]{2,1,0:T(8,128)(2,1)}, bf16[2,40,2048]{2,1,0:T(8,128...) custom-call(s32[8]{0:T(128)} %and_select_fusion.2.table, ...), custom_call_target="tpu_custom_call" | custom-call | flops 5368709120 | bytes 22020096 | tf_op jit(solution)/shard_map/pallas_call | solution.py:366
  37.8 1.7 %collective-permute-start.3 = (bf16[2,40,2048]{2,1,0:T(8,128)(2,1)}, bf16[2,40,2048]{2,1,0:T(8,128)(2,1)S(1)}, u32[]{:S(2)}, u32[]{:S(2)}) collective-permute-start(bf16[2,40,2048]{2,1,0:T(8,128)(2,1)} %get-tuple-element.68), channel_id=1, source_target_pairs={{0,2},{2,4},{4,6},{6,7},{7,5},{5,3},{3,1},{1,0},{8,10},{10,12},{12... | collective-permute-start | bytes 983048 | tf_op jit(solution)/shard_map/ppermute | solution.py:481
  39.5 0.4 collective-permute-start.4
  39.9 0.1 reshape.69
  40.1 5.7 %collective-permute-done.8.refs_2_ = bf16[2,120,2048]{2,1,0:T(8,128)(2,1)} collective-permute-done((bf16[2,120,2048]{2,1,0:T(8,128)(2,1)}, bf16[2,120,2048]{2,1,0:T(8,128)(2,1)}, u32[]{:S(2)}, u32[]{:S(2)}) %collective-permute-start.8) | collective-permute-done | bytes 983072 | tf_op jit(solution)/shard_map/ppermute | solution.py:23
  45.8 0.6 collective-permute-start.11
  46.4 1.5 collective-permute-done.3
  47.8 1.9 %collective-permute-start.10 = (bf16[64,1408]{1,0:T(8,128)(2,1)S(1)}, bf16[64,1408]{1,0:T(8,128)(2,1)S(1)}, u32[]{:S(2)}, u32[]{:S(2)}) collective-permute-start(bf16[64,1408]{1,0:T(8,128)(2,1)S(1)} %pad_maximum_fusion.8), channel_id=1, source_target_pairs={{0,16},{16,0},{8,24},{24,8},{1,17},{17,1},{9,25},{25,9},{2,18},{18... | collective-permute-start | bytes 540680 | tf_op jit(solution)/shard_map/ppermute | solution.py:23
  49.9 1.6 %collective-permute-start.6 = (bf16[2,40,2048]{2,1,0:T(8,128)(2,1)S(1)}, bf16[2,40,2048]{2,1,0:T(8,128)(2,1)S(1)}, u32[]{:S(2)}, u32[]{:S(2)}) collective-permute-start(bf16[2,40,2048]{2,1,0:T(8,128)(2,1)S(1)} %add_convert_fusion.14), channel_id=1, source_target_pairs={{2,0},{4,2},{6,4},{7,6},{5,7},{3,5},{1,3},{0,1},{10,8},{12,10},{14... | collective-permute-start | bytes 983048 | tf_op jit(solution)/shard_map/ppermute | solution.py:481
  51.5 0.8 collective-permute-start.5
  52.3 13.7 %shard_map.98 = (bf16[120,2048]{1,0:T(8,128)(2,1)}, bf16[120,2048]{1,0:T(8,128)(2,1)}, bf16[120,2048]{1,0:T(8,128)(2,1)}, bf16[120,2048]{1,0:T(8,128)(2,1)}, bf1...) custom-call(s32[8]{0:T(128)} %and_select_fusion.2.table, ...), custom_call_target="tpu_custom_call" | custom-call | flops 8053063680 | bytes 16252928 | tf_op jit(solution)/shard_map/pallas_call | solution.py:417
  66.2 1.6 %collective-permute-start.13 = (bf16[2,40,2048]{2,1,0:T(8,128)(2,1)S(1)}, bf16[2,40,2048]{2,1,0:T(8,128)(2,1)S(1)}, u32[]{:S(2)}, u32[]{:S(2)}) collective-permute-start(bf16[2,40,2048]{2,1,0:T(8,128)(2,1)S(1)} %add_convert_fusion.12), channel_id=1, source_target_pairs={{2,0},{4,2},{6,4},{7,6},{5,7},{3,5},{1,3},{0,1},{10,8},{12,10},{14... | collective-permute-start | bytes 983048 | tf_op jit(solution)/shard_map/ppermute | solution.py:481
  67.9 0.6 collective-permute-start.12
  68.4 1.6 %collective-permute-start.14 = (bf16[120,2048]{1,0:T(8,128)(2,1)}, bf16[120,2048]{1,0:T(8,128)(2,1)S(1)}, u32[]{:S(2)}, u32[]{:S(2)}) collective-permute-start(bf16[120,2048]{1,0:T(8,128)(2,1)} %get-tuple-element.83), channel_id=1, source_target_pairs={{0,2},{2,4},{4,6},{6,7},{7,5},{5,3},{3,1},{1,0},{8,10},{10,12},{12... | collective-permute-start | bytes 1474568 | tf_op jit(solution)/shard_map/ppermute | solution.py:511
  70.0 0.5 collective-permute-start.15
  70.5 13.7 %shard_map.99 = (bf16[120,2048]{1,0:T(8,128)(2,1)}, bf16[120,2048]{1,0:T(8,128)(2,1)}, bf16[120,2048]{1,0:T(8,128)(2,1)}, bf16[120,2048]{1,0:T(8,128)(2,1)}, bf1...) custom-call(s32[8]{0:T(128)} %and_select_fusion.2.table, ...), custom_call_target="tpu_custom_call" | custom-call | flops 8053063680 | bytes 16252928 | tf_op jit(solution)/shard_map/pallas_call | solution.py:417
  84.2 1.6 %collective-permute-start.18 = (bf16[120,2048]{1,0:T(8,128)(2,1)}, bf16[120,2048]{1,0:T(8,128)(2,1)S(1)}, u32[]{:S(2)}, u32[]{:S(2)}) collective-permute-start(bf16[120,2048]{1,0:T(8,128)(2,1)} %get-tuple-element.97), channel_id=1, source_target_pairs={{0,2},{2,4},{4,6},{6,7},{7,5},{5,3},{3,1},{1,0},{8,10},{10,12},{12... | collective-permute-start | bytes 1474568 | tf_op jit(solution)/shard_map/ppermute | solution.py:511
  85.8 2.2 %collective-permute-done.14 = bf16[120,2048]{1,0:T(8,128)(2,1)S(1)} collective-permute-done((bf16[120,2048]{1,0:T(8,128)(2,1)}, bf16[120,2048]{1,0:T(8,128)(2,1)S(1)}, u32[]{:S(2)}, u32[]{:S(2)}) %collective-permute-start.14) | collective-permute-done | bytes 491552 | tf_op jit(solution)/shard_map/ppermute | solution.py:511
  87.9 1.8 %collective-permute-start.19 = (bf16[120,2048]{1,0:T(8,128)(2,1)}, bf16[120,2048]{1,0:T(8,128)(2,1)S(1)}, u32[]{:S(2)}, u32[]{:S(2)}) collective-permute-start(bf16[120,2048]{1,0:T(8,128)(2,1)} %get-tuple-element.98), channel_id=1, source_target_pairs={{2,0},{4,2},{6,4},{7,6},{5,7},{3,5},{1,3},{0,1},{10,8},{12,10},{14... | collective-permute-start | bytes 1474568 | tf_op jit(solution)/shard_map/ppermute | solution.py:511
  89.7 0.1 add_convert_fusion.10
  89.8 1.7 %collective-permute-start.23 = (bf16[120,2048]{1,0:T(8,128)(2,1)S(1)}, bf16[120,2048]{1,0:T(8,128)(2,1)S(1)}, u32[]{:S(2)}, u32[]{:S(2)}) collective-permute-start(bf16[120,2048]{1,0:T(8,128)(2,1)S(1)} %add_convert_fusion.10), channel_id=1, source_target_pairs={{2,0},{4,2},{6,4},{7,6},{5,7},{3,5},{1,3},{0,1},{10,8},{12,10},{14... | collective-permute-start | bytes 1474568 | tf_op jit(solution)/shard_map/ppermute | solution.py:511
  91.5 0.1 add_convert_fusion.11
  91.6 0.5 collective-permute-start.22
  92.2 6.4 %collective-permute-done.18 = bf16[120,2048]{1,0:T(8,128)(2,1)S(1)} collective-permute-done((bf16[120,2048]{1,0:T(8,128)(2,1)}, bf16[120,2048]{1,0:T(8,128)(2,1)S(1)}, u32[]{:S(2)}, u32[]{:S(2)}) %collective-permute-start.18) | collective-permute-done | bytes 491552 | tf_op jit(solution)/shard_map/ppermute | solution.py:511
  98.6 3.7 %collective-permute-done.19 = bf16[120,2048]{1,0:T(8,128)(2,1)S(1)} collective-permute-done((bf16[120,2048]{1,0:T(8,128)(2,1)}, bf16[120,2048]{1,0:T(8,128)(2,1)S(1)}, u32[]{:S(2)}, u32[]{:S(2)}) %collective-permute-start.19) | collective-permute-done | bytes 491552 | tf_op jit(solution)/shard_map/ppermute | solution.py:511
  102.3 0.1 add_convert_fusion.8
  102.4 1.8 %collective-permute-start.21 = (bf16[120,2048]{1,0:T(8,128)(2,1)S(1)}, bf16[120,2048]{1,0:T(8,128)(2,1)S(1)}, u32[]{:S(2)}, u32[]{:S(2)}) collective-permute-start(bf16[120,2048]{1,0:T(8,128)(2,1)S(1)} %add_convert_fusion.8), channel_id=1, source_target_pairs={{2,0},{4,2},{6,4},{7,6},{5,7},{3,5},{1,3},{0,1},{10,8},{12,10},{14... | collective-permute-start | bytes 1474568 | tf_op jit(solution)/shard_map/ppermute | solution.py:511
  104.2 0.1 add_convert_fusion.9
  104.4 0.3 collective-permute-start.20
  104.7 8.1 %collective-permute-done.23 = bf16[120,2048]{1,0:T(8,128)(2,1)S(1)} collective-permute-done((bf16[120,2048]{1,0:T(8,128)(2,1)S(1)}, bf16[120,2048]{1,0:T(8,128)(2,1)S(1)}, u32[]{:S(2)}, u32[]{:S(2)}) %collective-permute-start.23) | collective-permute-done | bytes 491552 | tf_op jit(solution)/shard_map/ppermute | solution.py:511
  112.8 0.1 add_convert_fusion.6
  113.0 1.8 %collective-permute-start.27 = (bf16[120,2048]{1,0:T(8,128)(2,1)S(1)}, bf16[120,2048]{1,0:T(8,128)(2,1)S(1)}, u32[]{:S(2)}, u32[]{:S(2)}) collective-permute-start(bf16[120,2048]{1,0:T(8,128)(2,1)S(1)} %add_convert_fusion.6), channel_id=1, source_target_pairs={{2,0},{4,2},{6,4},{7,6},{5,7},{3,5},{1,3},{0,1},{10,8},{12,10},{14... | collective-permute-start | bytes 1474568 | tf_op jit(solution)/shard_map/ppermute | solution.py:511
  114.8 0.1 add_convert_fusion.7
  114.9 0.3 collective-permute-start.26
  115.2 8.1 %collective-permute-done.21 = bf16[120,2048]{1,0:T(8,128)(2,1)S(1)} collective-permute-done((bf16[120,2048]{1,0:T(8,128)(2,1)S(1)}, bf16[120,2048]{1,0:T(8,128)(2,1)S(1)}, u32[]{:S(2)}, u32[]{:S(2)}) %collective-permute-start.21) | collective-permute-done | bytes 491552 | tf_op jit(solution)/shard_map/ppermute | solution.py:511
  123.4 0.1 add_convert_fusion.4
  123.5 1.8 %collective-permute-start.25 = (bf16[120,2048]{1,0:T(8,128)(2,1)S(1)}, bf16[120,2048]{1,0:T(8,128)(2,1)S(1)}, u32[]{:S(2)}, u32[]{:S(2)}) collective-permute-start(bf16[120,2048]{1,0:T(8,128)(2,1)S(1)} %add_convert_fusion.4), channel_id=1, source_target_pairs={{2,0},{4,2},{6,4},{7,6},{5,7},{3,5},{1,3},{0,1},{10,8},{12,10},{14... | collective-permute-start | bytes 1474568 | tf_op jit(solution)/shard_map/ppermute | solution.py:511
  125.3 0.1 add_convert_fusion.5
  125.4 0.3 collective-permute-start.24
  125.8 8.1 %collective-permute-done.27 = bf16[120,2048]{1,0:T(8,128)(2,1)S(1)} collective-permute-done((bf16[120,2048]{1,0:T(8,128)(2,1)S(1)}, bf16[120,2048]{1,0:T(8,128)(2,1)S(1)}, u32[]{:S(2)}, u32[]{:S(2)}) %collective-permute-start.27) | collective-permute-done | bytes 491552 | tf_op jit(solution)/shard_map/ppermute | solution.py:511
  133.9 2.0 %collective-permute-start.17 = (bf16[40,2048]{1,0:T(8,128)(2,1)S(1)}, bf16[40,2048]{1,0:T(8,128)(2,1)S(1)}, u32[]{:S(2)}, u32[]{:S(2)}) collective-permute-start(bf16[40,2048]{1,0:T(8,128)(2,1)S(1)} %fusion.2), channel_id=1, source_target_pairs={{2,0},{4,2},{6,4},{7,6},{5,7},{3,5},{1,3},{0,1},{10,8},{12,10},{14... | collective-permute-start | bytes 491528 | tf_op jit(solution)/shard_map/ppermute | solution.py:481
  135.9 0.1 add_convert_fusion.3
  136.0 5.3 %collective-permute-done.25 = bf16[120,2048]{1,0:T(8,128)(2,1)S(1)} collective-permute-done((bf16[120,2048]{1,0:T(8,128)(2,1)S(1)}, bf16[120,2048]{1,0:T(8,128)(2,1)S(1)}, u32[]{:S(2)}, u32[]{:S(2)}) %collective-permute-start.25) | collective-permute-done | bytes 491552 | tf_op jit(solution)/shard_map/ppermute | solution.py:511
  141.4 2.0 %collective-permute-start.28 = (bf16[120,2048]{1,0:T(8,128)(2,1)S(1)}, bf16[120,2048]{1,0:T(8,128)(2,1)S(1)}, u32[]{:S(2)}, u32[]{:S(2)}) collective-permute-start(bf16[120,2048]{1,0:T(8,128)(2,1)S(1)} %add_convert_fusion.3), channel_id=1, source_target_pairs={{0,2},{2,4},{4,6},{6,7},{7,5},{5,3},{3,1},{1,0},{8,10},{10,12},{12... | collective-permute-start | bytes 1474568 | tf_op jit(solution)/shard_map/ppermute | solution.py:511
  143.4 0.1 add_convert_fusion.2
  143.6 0.2 fusion.5
  143.8 0.3 convolution_convert_fusion
  144.1 0.1 collective-permute-done.16
  144.2 0.7 collective-permute-done.17
  144.9 0.7 copy.20
  145.6 0.1 add_convert_fusion.16
  145.7 7.2 %collective-permute-done.28 = bf16[120,2048]{1,0:T(8,128)(2,1)S(1)} collective-permute-done((bf16[120,2048]{1,0:T(8,128)(2,1)S(1)}, bf16[120,2048]{1,0:T(8,128)(2,1)S(1)}, u32[]{:S(2)}, u32[]{:S(2)}) %collective-permute-start.28) | collective-permute-done | bytes 491552 | tf_op jit(solution)/shard_map/ppermute | solution.py:511
  153.0 0.2 add_convert_fusion.1
  153.2 0.2 add_convert_fusion
  153.4 1.1 maximum_maximum_fusion
  (93 shorter events, 1.0 us)
Async XLA Ops:
  6.9 15.8 %copy-start.21 = (s32[64]{0:T(128)S(1)}, s32[64]{0:T(128)}, u32[]{:S(2)}) copy-start(s32[64]{0:T(128)} %param.13) | copy-start | bytes 772
  6.9 16.4 %copy-start.26 = (s32[64]{0:T(128)S(1)}, s32[64]{0:T(128)}, u32[]{:S(2)}) copy-start(s32[64]{0:T(128)} %param.14) | copy-start | bytes 772
  6.9 15.9 %collective-permute-start.1 = (bf16[2,40,2048]{2,1,0:T(8,128)(2,1)}, bf16[2,40,2048]{2,1,0:T(8,128)(2,1)S(1)}, u32[]{:S(2)}, u32[]{:S(2)}) collective-permute-start(bf16[2,40,2048]{2,1,0:T(8,128)(2,1)} %shard_map.95.refs_0_), channel_id=1, source_target_pairs={{0,16},{16,0},{8,24},{24,8},{1,17},{17,1},{9,25},{25,9},{2,18},{18... | collective-permute-start | bytes 983048 | tf_op jit(solution)/shard_map/ppermute | solution.py:23
  9.9 13.8 %collective-permute-start = (bf16[2,40,2048]{2,1,0:T(8,128)(2,1)}, bf16[2,40,2048]{2,1,0:T(8,128)(2,1)S(1)}, u32[]{:S(2)}, u32[]{:S(2)}) collective-permute-start(bf16[2,40,2048]{2,1,0:T(8,128)(2,1)} %shard_map.95.refs_0_), channel_id=1, source_target_pairs={{0,8},{8,0},{16,24},{24,16},{1,9},{9,1},{17,25},{25,17},{2,10},{10... | collective-permute-start | bytes 983048 | tf_op jit(solution)/shard_map/ppermute | solution.py:23
  21.9 23.9 %collective-permute-start.8 = (bf16[2,120,2048]{2,1,0:T(8,128)(2,1)}, bf16[2,120,2048]{2,1,0:T(8,128)(2,1)}, u32[]{:S(2)}, u32[]{:S(2)}) collective-permute-start(bf16[2,120,2048]{2,1,0:T(8,128)(2,1)} %shard_map.96.refs_0_), channel_id=1, source_target_pairs={{0,16},{16,0},{8,24},{24,8},{1,17},{17,1},{9,25},{25,9},{2,18},{18... | collective-permute-start | bytes 2949128 | tf_op jit(solution)/shard_map/ppermute | solution.py:23
  22.0 29.5 %collective-permute-start.7 = (bf16[2,120,2048]{2,1,0:T(8,128)(2,1)}, bf16[2,120,2048]{2,1,0:T(8,128)(2,1)}, u32[]{:S(2)}, u32[]{:S(2)}) collective-permute-start(bf16[2,120,2048]{2,1,0:T(8,128)(2,1)} %shard_map.96.refs_0_), channel_id=1, source_target_pairs={{0,8},{8,0},{16,24},{24,16},{1,9},{9,1},{17,25},{25,17},{2,10},{10... | collective-permute-start | bytes 2949128 | tf_op jit(solution)/shard_map/ppermute | solution.py:23
  22.8 2.4 %copy-start.23 = (bf16[2,40,2048]{2,1,0:T(8,128)(2,1)}, bf16[2,40,2048]{2,1,0:T(8,128)(2,1)S(1)}, u32[]{:S(2)}) copy-start(bf16[2,40,2048]{2,1,0:T(8,128)(2,1)S(1)} %collective-permute-done.1.refs_2_) | copy-start | bytes 983044
  22.8 2.3 %collective-permute-start.2 = (bf16[2,40,2048]{2,1,0:T(8,128)(2,1)S(1)}, bf16[2,40,2048]{2,1,0:T(8,128)(2,1)S(1)}, u32[]{:S(2)}, u32[]{:S(2)}) collective-permute-start(bf16[2,40,2048]{2,1,0:T(8,128)(2,1)S(1)} %collective-permute-done.1.refs_2_), channel_id=1, source_target_pairs={{0,8},{8,0},{16,24},{24,16},{1,9},{9,1},{17,25},{25,17},{2,10},{10... | collective-permute-start | bytes 983048 | tf_op jit(solution)/shard_map/ppermute | solution.py:23
  23.7 16.2 %copy-start = (bf16[320,256]{1,0:T(8,128)(2,1)S(1)}, bf16[320,256]{1,0:T(8,128)(2,1)}, u32[]{:S(2)}) copy-start(bf16[320,256]{1,0:T(8,128)(2,1)} %fresh.3) | copy-start | bytes 491524
  23.7 1.4 copy-start.24
  25.1 0.7 copy-start.25
  37.8 12.0 %copy-start.16 = (bf16[2,40,2048]{2,1,0:T(8,128)(2,1)S(1)}, bf16[2,40,2048]{2,1,0:T(8,128)(2,1)}, u32[]{:S(2)}) copy-start(bf16[2,40,2048]{2,1,0:T(8,128)(2,1)} %get-tuple-element.71) | copy-start | bytes 983044
  37.8 13.6 %copy-start.15 = (bf16[2,40,2048]{2,1,0:T(8,128)(2,1)S(1)}, bf16[2,40,2048]{2,1,0:T(8,128)(2,1)}, u32[]{:S(2)}) copy-start(bf16[2,40,2048]{2,1,0:T(8,128)(2,1)} %get-tuple-element.67) | copy-start | bytes 983044
  37.8 10.0 %collective-permute-start.3 = (bf16[2,40,2048]{2,1,0:T(8,128)(2,1)}, bf16[2,40,2048]{2,1,0:T(8,128)(2,1)S(1)}, u32[]{:S(2)}, u32[]{:S(2)}) collective-permute-start(bf16[2,40,2048]{2,1,0:T(8,128)(2,1)} %get-tuple-element.68), channel_id=1, source_target_pairs={{0,2},{2,4},{4,6},{6,7},{7,5},{5,3},{3,1},{1,0},{8,10},{10,12},{12... | collective-permute-start | bytes 983048 | tf_op jit(solution)/shard_map/ppermute | solution.py:481
  39.5 10.3 %collective-permute-start.4 = (bf16[2,40,2048]{2,1,0:T(8,128)(2,1)}, bf16[2,40,2048]{2,1,0:T(8,128)(2,1)S(1)}, u32[]{:S(2)}, u32[]{:S(2)}) collective-permute-start(bf16[2,40,2048]{2,1,0:T(8,128)(2,1)} %get-tuple-element.69), channel_id=1, source_target_pairs={{2,0},{4,2},{6,4},{7,6},{5,7},{3,5},{1,3},{0,1},{10,8},{12,10},{14... | collective-permute-start | bytes 983048 | tf_op jit(solution)/shard_map/ppermute | solution.py:481
  45.8 6.5 %collective-permute-start.9 = (bf16[2,120,2048]{2,1,0:T(8,128)(2,1)}, bf16[2,120,2048]{2,1,0:T(8,128)(2,1)}, u32[]{:S(2)}, u32[]{:S(2)}) collective-permute-start(bf16[2,120,2048]{2,1,0:T(8,128)(2,1)} %collective-permute-done.8.refs_2_), channel_id=1, source_target_pairs={{0,8},{8,0},{16,24},{24,16},{1,9},{9,1},{17,25},{25,17},{2,10},{10... | collective-permute-start | bytes 2949128 | tf_op jit(solution)/shard_map/ppermute | solution.py:23
  45.8 20.3 %collective-permute-start.11 = (bf16[64,1408]{1,0:T(8,128)(2,1)S(1)}, bf16[64,1408]{1,0:T(8,128)(2,1)S(1)}, u32[]{:S(2)}, u32[]{:S(2)}) collective-permute-start(bf16[64,1408]{1,0:T(8,128)(2,1)S(1)} %pad_maximum_fusion.8), channel_id=1, source_target_pairs={{0,8},{8,0},{16,24},{24,16},{1,9},{9,1},{17,25},{25,17},{2,10},{10... | collective-permute-start | bytes 540680 | tf_op jit(solution)/shard_map/ppermute | solution.py:23
  47.8 18.2 %collective-permute-start.10 = (bf16[64,1408]{1,0:T(8,128)(2,1)S(1)}, bf16[64,1408]{1,0:T(8,128)(2,1)S(1)}, u32[]{:S(2)}, u32[]{:S(2)}) collective-permute-start(bf16[64,1408]{1,0:T(8,128)(2,1)S(1)} %pad_maximum_fusion.8), channel_id=1, source_target_pairs={{0,16},{16,0},{8,24},{24,8},{1,17},{17,1},{9,25},{25,9},{2,18},{18... | collective-permute-start | bytes 540680 | tf_op jit(solution)/shard_map/ppermute | solution.py:23
  49.9 16.2 %collective-permute-start.6 = (bf16[2,40,2048]{2,1,0:T(8,128)(2,1)S(1)}, bf16[2,40,2048]{2,1,0:T(8,128)(2,1)S(1)}, u32[]{:S(2)}, u32[]{:S(2)}) collective-permute-start(bf16[2,40,2048]{2,1,0:T(8,128)(2,1)S(1)} %add_convert_fusion.14), channel_id=1, source_target_pairs={{2,0},{4,2},{6,4},{7,6},{5,7},{3,5},{1,3},{0,1},{10,8},{12,10},{14... | collective-permute-start | bytes 983048 | tf_op jit(solution)/shard_map/ppermute | solution.py:481
  51.5 14.6 %copy-start.14 = (bf16[2,40,2048]{2,1,0:T(8,128)(2,1)S(1)}, bf16[2,40,2048]{2,1,0:T(8,128)(2,1)}, u32[]{:S(2)}) copy-start(bf16[2,40,2048]{2,1,0:T(8,128)(2,1)} %get-tuple-element.80) | copy-start | bytes 983044
  51.5 16.3 %copy-start.13 = (bf16[2,40,2048]{2,1,0:T(8,128)(2,1)S(1)}, bf16[2,40,2048]{2,1,0:T(8,128)(2,1)}, u32[]{:S(2)}) copy-start(bf16[2,40,2048]{2,1,0:T(8,128)(2,1)} %get-tuple-element.66) | copy-start | bytes 983044
  51.5 14.6 %collective-permute-start.5 = (bf16[2,40,2048]{2,1,0:T(8,128)(2,1)S(1)}, bf16[2,40,2048]{2,1,0:T(8,128)(2,1)S(1)}, u32[]{:S(2)}, u32[]{:S(2)}) collective-permute-start(bf16[2,40,2048]{2,1,0:T(8,128)(2,1)S(1)} %add_convert_fusion.15), channel_id=1, source_target_pairs={{0,2},{2,4},{4,6},{6,7},{7,5},{5,3},{3,1},{1,0},{8,10},{10,12},{12... | collective-permute-start | bytes 983048 | tf_op jit(solution)/shard_map/ppermute | solution.py:481
  66.1 3.9 %copy-start.22 = (bf16[120,2048]{1,0:T(8,128)(2,1)S(1)}, bf16[120,2048]{1,0:T(8,128)(2,1)}, u32[]{:S(2)}) copy-start(bf16[120,2048]{1,0:T(8,128)(2,1)} %get-tuple-element.84) | copy-start | bytes 1474564
  66.2 25.4 %collective-permute-start.13 = (bf16[2,40,2048]{2,1,0:T(8,128)(2,1)S(1)}, bf16[2,40,2048]{2,1,0:T(8,128)(2,1)S(1)}, u32[]{:S(2)}, u32[]{:S(2)}) collective-permute-start(bf16[2,40,2048]{2,1,0:T(8,128)(2,1)S(1)} %add_convert_fusion.12), channel_id=1, source_target_pairs={{2,0},{4,2},{6,4},{7,6},{5,7},{3,5},{1,3},{0,1},{10,8},{12,10},{14... | collective-permute-start | bytes 983048 | tf_op jit(solution)/shard_map/ppermute | solution.py:481
  67.9 24.2 %collective-permute-start.12 = (bf16[2,40,2048]{2,1,0:T(8,128)(2,1)S(1)}, bf16[2,40,2048]{2,1,0:T(8,128)(2,1)S(1)}, u32[]{:S(2)}, u32[]{:S(2)}) collective-permute-start(bf16[2,40,2048]{2,1,0:T(8,128)(2,1)S(1)} %add_convert_fusion.13), channel_id=1, source_target_pairs={{0,2},{2,4},{4,6},{6,7},{7,5},{5,3},{3,1},{1,0},{8,10},{10,12},{12... | collective-permute-start | bytes 983048 | tf_op jit(solution)/shard_map/ppermute | solution.py:481
  68.4 19.5 %collective-permute-start.14 = (bf16[120,2048]{1,0:T(8,128)(2,1)}, bf16[120,2048]{1,0:T(8,128)(2,1)S(1)}, u32[]{:S(2)}, u32[]{:S(2)}) collective-permute-start(bf16[120,2048]{1,0:T(8,128)(2,1)} %get-tuple-element.83), channel_id=1, source_target_pairs={{0,2},{2,4},{4,6},{6,7},{7,5},{5,3},{3,1},{1,0},{8,10},{10,12},{12... | collective-permute-start | bytes 1474568 | tf_op jit(solution)/shard_map/ppermute | solution.py:511
  70.0 19.7 %copy-start.8 = (bf16[120,2048]{1,0:T(8,128)(2,1)S(1)}, bf16[120,2048]{1,0:T(8,128)(2,1)}, u32[]{:S(2)}) copy-start(bf16[120,2048]{1,0:T(8,128)(2,1)} %get-tuple-element.88) | copy-start | bytes 1474564
  70.0 19.7 %collective-permute-start.15 = (bf16[120,2048]{1,0:T(8,128)(2,1)S(1)}, bf16[120,2048]{1,0:T(8,128)(2,1)S(1)}, u32[]{:S(2)}, u32[]{:S(2)}) collective-permute-start(bf16[120,2048]{1,0:T(8,128)(2,1)S(1)} %copy-done.22), channel_id=1, source_target_pairs={{2,0},{4,2},{6,4},{7,6},{5,7},{3,5},{1,3},{0,1},{10,8},{12,10},{14... | collective-permute-start | bytes 1474568 | tf_op jit(solution)/shard_map/ppermute | solution.py:511
  84.2 7.3 %copy-start.7 = (bf16[120,2048]{1,0:T(8,128)(2,1)S(1)}, bf16[120,2048]{1,0:T(8,128)(2,1)}, u32[]{:S(2)}) copy-start(bf16[120,2048]{1,0:T(8,128)(2,1)} %get-tuple-element.82) | copy-start | bytes 1474564
  84.2 14.4 %collective-permute-start.18 = (bf16[120,2048]{1,0:T(8,128)(2,1)}, bf16[120,2048]{1,0:T(8,128)(2,1)S(1)}, u32[]{:S(2)}, u32[]{:S(2)}) collective-permute-start(bf16[120,2048]{1,0:T(8,128)(2,1)} %get-tuple-element.97), channel_id=1, source_target_pairs={{0,2},{2,4},{4,6},{6,7},{7,5},{5,3},{3,1},{1,0},{8,10},{10,12},{12... | collective-permute-start | bytes 1474568 | tf_op jit(solution)/shard_map/ppermute | solution.py:511
  87.9 14.4 %collective-permute-start.19 = (bf16[120,2048]{1,0:T(8,128)(2,1)}, bf16[120,2048]{1,0:T(8,128)(2,1)S(1)}, u32[]{:S(2)}, u32[]{:S(2)}) collective-permute-start(bf16[120,2048]{1,0:T(8,128)(2,1)} %get-tuple-element.98), channel_id=1, source_target_pairs={{2,0},{4,2},{6,4},{7,6},{5,7},{3,5},{1,3},{0,1},{10,8},{12,10},{14... | collective-permute-start | bytes 1474568 | tf_op jit(solution)/shard_map/ppermute | solution.py:511
  89.7 2.4 %copy-start.20 = (bf16[40,2048]{1,0:T(8,128)(2,1)S(1)}, bf16[40,2048]{1,0:T(8,128)(2,1)}, u32[]{:S(2)}) copy-start(bf16[40,2048]{1,0:T(8,128)(2,1)} %get-tuple-element.93) | copy-start | bytes 491524
  89.8 2.4 %copy-start.19 = (bf16[40,2048]{1,0:T(8,128)(2,1)S(1)}, bf16[40,2048]{1,0:T(8,128)(2,1)}, u32[]{:S(2)}) copy-start(bf16[40,2048]{1,0:T(8,128)(2,1)} %get-tuple-element.91) | copy-start | bytes 491524
  89.8 12.5 %copy-start.10 = (bf16[120,2048]{1,0:T(8,128)(2,1)S(1)}, bf16[120,2048]{1,0:T(8,128)(2,1)}, u32[]{:S(2)}) copy-start(bf16[120,2048]{1,0:T(8,128)(2,1)} %get-tuple-element.100) | copy-start | bytes 1474564
  89.8 23.0 %collective-permute-start.23 = (bf16[120,2048]{1,0:T(8,128)(2,1)S(1)}, bf16[120,2048]{1,0:T(8,128)(2,1)S(1)}, u32[]{:S(2)}, u32[]{:S(2)}) collective-permute-start(bf16[120,2048]{1,0:T(8,128)(2,1)S(1)} %add_convert_fusion.10), channel_id=1, source_target_pairs={{2,0},{4,2},{6,4},{7,6},{5,7},{3,5},{1,3},{0,1},{10,8},{12,10},{14... | collective-permute-start | bytes 1474568 | tf_op jit(solution)/shard_map/ppermute | solution.py:511
  91.6 12.6 %copy-start.9 = (bf16[120,2048]{1,0:T(8,128)(2,1)S(1)}, bf16[120,2048]{1,0:T(8,128)(2,1)}, u32[]{:S(2)}) copy-start(bf16[120,2048]{1,0:T(8,128)(2,1)} %get-tuple-element.96) | copy-start | bytes 1474564
  91.6 21.2 %collective-permute-start.22 = (bf16[120,2048]{1,0:T(8,128)(2,1)S(1)}, bf16[120,2048]{1,0:T(8,128)(2,1)S(1)}, u32[]{:S(2)}, u32[]{:S(2)}) collective-permute-start(bf16[120,2048]{1,0:T(8,128)(2,1)S(1)} %add_convert_fusion.11), channel_id=1, source_target_pairs={{0,2},{2,4},{4,6},{6,7},{7,5},{5,3},{3,1},{1,0},{8,10},{10,12},{12... | collective-permute-start | bytes 1474568 | tf_op jit(solution)/shard_map/ppermute | solution.py:511
  102.3 10.5 %copy-start.4 = (bf16[120,2048]{1,0:T(8,128)(2,1)S(1)}, bf16[120,2048]{1,0:T(8,128)(2,1)}, u32[]{:S(2)}) copy-start(bf16[120,2048]{1,0:T(8,128)(2,1)} %get-tuple-element.104) | copy-start | bytes 1474564
  102.4 20.9 %collective-permute-start.21 = (bf16[120,2048]{1,0:T(8,128)(2,1)S(1)}, bf16[120,2048]{1,0:T(8,128)(2,1)S(1)}, u32[]{:S(2)}, u32[]{:S(2)}) collective-permute-start(bf16[120,2048]{1,0:T(8,128)(2,1)S(1)} %add_convert_fusion.8), channel_id=1, source_target_pairs={{2,0},{4,2},{6,4},{7,6},{5,7},{3,5},{1,3},{0,1},{10,8},{12,10},{14... | collective-permute-start | bytes 1474568 | tf_op jit(solution)/shard_map/ppermute | solution.py:511
  104.2 10.5 %copy-start.3 = (bf16[120,2048]{1,0:T(8,128)(2,1)S(1)}, bf16[120,2048]{1,0:T(8,128)(2,1)}, u32[]{:S(2)}) copy-start(bf16[120,2048]{1,0:T(8,128)(2,1)} %get-tuple-element.102) | copy-start | bytes 1474564
  104.4 19.0 %collective-permute-start.20 = (bf16[120,2048]{1,0:T(8,128)(2,1)S(1)}, bf16[120,2048]{1,0:T(8,128)(2,1)S(1)}, u32[]{:S(2)}, u32[]{:S(2)}) collective-permute-start(bf16[120,2048]{1,0:T(8,128)(2,1)S(1)} %add_convert_fusion.9), channel_id=1, source_target_pairs={{0,2},{2,4},{4,6},{6,7},{7,5},{5,3},{3,1},{1,0},{8,10},{10,12},{12... | collective-permute-start | bytes 1474568 | tf_op jit(solution)/shard_map/ppermute | solution.py:511
  112.8 10.5 %copy-start.6 = (bf16[120,2048]{1,0:T(8,128)(2,1)S(1)}, bf16[120,2048]{1,0:T(8,128)(2,1)}, u32[]{:S(2)}) copy-start(bf16[120,2048]{1,0:T(8,128)(2,1)} %get-tuple-element.107) | copy-start | bytes 1474564
  113.0 20.9 %collective-permute-start.27 = (bf16[120,2048]{1,0:T(8,128)(2,1)S(1)}, bf16[120,2048]{1,0:T(8,128)(2,1)S(1)}, u32[]{:S(2)}, u32[]{:S(2)}) collective-permute-start(bf16[120,2048]{1,0:T(8,128)(2,1)S(1)} %add_convert_fusion.6), channel_id=1, source_target_pairs={{2,0},{4,2},{6,4},{7,6},{5,7},{3,5},{1,3},{0,1},{10,8},{12,10},{14... | collective-permute-start | bytes 1474568 | tf_op jit(solution)/shard_map/ppermute | solution.py:511
  114.8 10.5 %copy-start.5 = (bf16[120,2048]{1,0:T(8,128)(2,1)S(1)}, bf16[120,2048]{1,0:T(8,128)(2,1)}, u32[]{:S(2)}) copy-start(bf16[120,2048]{1,0:T(8,128)(2,1)} %get-tuple-element.95) | copy-start | bytes 1474564
  114.9 19.0 %collective-permute-start.26 = (bf16[120,2048]{1,0:T(8,128)(2,1)S(1)}, bf16[120,2048]{1,0:T(8,128)(2,1)S(1)}, u32[]{:S(2)}, u32[]{:S(2)}) collective-permute-start(bf16[120,2048]{1,0:T(8,128)(2,1)S(1)} %add_convert_fusion.7), channel_id=1, source_target_pairs={{0,2},{2,4},{4,6},{6,7},{7,5},{5,3},{3,1},{1,0},{8,10},{10,12},{12... | collective-permute-start | bytes 1474568 | tf_op jit(solution)/shard_map/ppermute | solution.py:511
  123.4 12.6 %copy-start.1 = (bf16[120,2048]{1,0:T(8,128)(2,1)S(1)}, bf16[120,2048]{1,0:T(8,128)(2,1)}, u32[]{:S(2)}) copy-start(bf16[120,2048]{1,0:T(8,128)(2,1)} %get-tuple-element.109) | copy-start | bytes 1474564
  123.5 17.9 %collective-permute-start.25 = (bf16[120,2048]{1,0:T(8,128)(2,1)S(1)}, bf16[120,2048]{1,0:T(8,128)(2,1)S(1)}, u32[]{:S(2)}, u32[]{:S(2)}) collective-permute-start(bf16[120,2048]{1,0:T(8,128)(2,1)S(1)} %add_convert_fusion.4), channel_id=1, source_target_pairs={{2,0},{4,2},{6,4},{7,6},{5,7},{3,5},{1,3},{0,1},{10,8},{12,10},{14... | collective-permute-start | bytes 1474568 | tf_op jit(solution)/shard_map/ppermute | solution.py:511
  125.3 18.1 %copy-start.2 = (bf16[120,2048]{1,0:T(8,128)(2,1)S(1)}, bf16[120,2048]{1,0:T(8,128)(2,1)}, u32[]{:S(2)}) copy-start(bf16[120,2048]{1,0:T(8,128)(2,1)} %get-tuple-element.94) | copy-start | bytes 1474564
  125.4 18.0 %collective-permute-start.24 = (bf16[120,2048]{1,0:T(8,128)(2,1)S(1)}, bf16[120,2048]{1,0:T(8,128)(2,1)S(1)}, u32[]{:S(2)}, u32[]{:S(2)}) collective-permute-start(bf16[120,2048]{1,0:T(8,128)(2,1)S(1)} %add_convert_fusion.5), channel_id=1, source_target_pairs={{0,2},{2,4},{4,6},{6,7},{7,5},{5,3},{3,1},{1,0},{8,10},{10,12},{12... | collective-permute-start | bytes 1474568 | tf_op jit(solution)/shard_map/ppermute | solution.py:511
  125.8 17.9 %collective-permute-start.30 = (bf16[64,1408]{1,0:T(8,128)(2,1)S(1)}, bf16[64,1408]{1,0:T(8,128)(2,1)S(1)}, u32[]{:S(2)}, u32[]{:S(2)}) collective-permute-start(bf16[64,1408]{1,0:T(8,128)(2,1)S(1)} %collective-permute-done.10), channel_id=1, source_target_pairs={{0,8},{8,0},{16,24},{24,16},{1,9},{9,1},{17,25},{25,17},{2,10},{10... | collective-permute-start | bytes 540680 | tf_op jit(solution)/shard_map/ppermute | solution.py:23
  133.9 10.3 %collective-permute-start.16 = (bf16[40,2048]{1,0:T(8,128)(2,1)S(1)}, bf16[40,2048]{1,0:T(8,128)(2,1)S(1)}, u32[]{:S(2)}, u32[]{:S(2)}) collective-permute-start(bf16[40,2048]{1,0:T(8,128)(2,1)S(1)} %fusion.3), channel_id=1, source_target_pairs={{0,2},{2,4},{4,6},{6,7},{7,5},{5,3},{3,1},{1,0},{8,10},{10,12},{12... | collective-permute-start | bytes 491528 | tf_op jit(solution)/shard_map/ppermute | solution.py:481
  133.9 11.0 %collective-permute-start.17 = (bf16[40,2048]{1,0:T(8,128)(2,1)S(1)}, bf16[40,2048]{1,0:T(8,128)(2,1)S(1)}, u32[]{:S(2)}, u32[]{:S(2)}) collective-permute-start(bf16[40,2048]{1,0:T(8,128)(2,1)S(1)} %fusion.2), channel_id=1, source_target_pairs={{2,0},{4,2},{6,4},{7,6},{5,7},{3,5},{1,3},{0,1},{10,8},{12,10},{14... | collective-permute-start | bytes 491528 | tf_op jit(solution)/shard_map/ppermute | solution.py:481
  141.4 11.6 %collective-permute-start.28 = (bf16[120,2048]{1,0:T(8,128)(2,1)S(1)}, bf16[120,2048]{1,0:T(8,128)(2,1)S(1)}, u32[]{:S(2)}, u32[]{:S(2)}) collective-permute-start(bf16[120,2048]{1,0:T(8,128)(2,1)S(1)} %add_convert_fusion.3), channel_id=1, source_target_pairs={{0,2},{2,4},{4,6},{6,7},{7,5},{5,3},{3,1},{1,0},{8,10},{10,12},{12... | collective-permute-start | bytes 1474568 | tf_op jit(solution)/shard_map/ppermute | solution.py:511
  143.5 9.7 %collective-permute-start.29 = (bf16[120,2048]{1,0:T(8,128)(2,1)S(1)}, bf16[120,2048]{1,0:T(8,128)(2,1)S(1)}, u32[]{:S(2)}, u32[]{:S(2)}) collective-permute-start(bf16[120,2048]{1,0:T(8,128)(2,1)S(1)} %add_convert_fusion.2), channel_id=1, source_target_pairs={{2,0},{4,2},{6,4},{7,6},{5,7},{3,5},{1,3},{0,1},{10,8},{12,10},{14... | collective-permute-start | bytes 1474568 | tf_op jit(solution)/shard_map/ppermute | solution.py:511
  143.8 1.8 %copy-start.17 = (bf16[40,2048]{1,0:T(8,128)(2,1)S(1)}, bf16[40,2048]{1,0:T(8,128)(2,1)}, u32[]{:S(2)}) copy-start(bf16[40,2048]{1,0:T(8,128)(2,1)} %get-tuple-element.65) | copy-start | bytes 491524
  143.8 1.8 %copy-start.18 = (bf16[40,2048]{1,0:T(8,128)(2,1)S(1)}, bf16[40,2048]{1,0:T(8,128)(2,1)}, u32[]{:S(2)}) copy-start(bf16[40,2048]{1,0:T(8,128)(2,1)} %get-tuple-element.113) | copy-start | bytes 491524
  144.1 8.8 %copy-start.11 = (bf16[120,2048]{1,0:T(8,128)(2,1)S(1)}, bf16[120,2048]{1,0:T(8,128)(2,1)}, u32[]{:S(2)}) copy-start(bf16[120,2048]{1,0:T(8,128)(2,1)} %get-tuple-element.75) | copy-start | bytes 1474564
  145.6 7.6 %copy-start.12 = (bf16[120,2048]{1,0:T(8,128)(2,1)S(1)}, bf16[120,2048]{1,0:T(8,128)(2,1)}, u32[]{:S(2)}) copy-start(bf16[120,2048]{1,0:T(8,128)(2,1)} %get-tuple-element.86) | copy-start | bytes 1474564
